TPU v7x, 128 devices: a whole 4x4x4 slice. The times are simulated.
128 devices in a mesh: outer: 2 (over z_hi), inner: 64 (over z_lo, y, x, core).
Axes of the slice: x: 4, y: 4, z: 4 (z_hi: 2, z_lo: 2; z = z_hi * 2 + z_lo), core: 2. Of those that a mesh axis runs over, the one named last changes fastest.
Arguments:
- grad_out: bfloat16 [32768, 3584], P(('outer', 'inner')), may hold values from -6 to 6
- gates: bfloat16 [32768, 4], P(('outer', 'inner')), may hold values from 0.049804688 to 1
- routes: int32 [32768, 4], P(('outer', 'inner')), may hold values from 0 to 127, all different within a row; in each aligned block of 256 rows (0 to 255, 256 to 511, ...) at most 10 rows name the same one
- w_down: bfloat16 [128, 1024, 3584], P('inner', 'outer'), may hold values from -0.1875 to 0.1875
- saved_hidden: bfloat16 [128, 1280, 1024], P('inner', None, 'outer'), may hold values from -0.59765625 to 0.59765625
Outputs:
- d_gates: float32 [32768, 4], P(('outer', 'inner'))
- d_down: bfloat16 [128, 1024, 3584], P('inner', 'outer')
- d_hidden: bfloat16 [128, 1280, 1024], P('inner', None, 'outer')
Inputs may be any that keep to these rules, and one draw needn't show every extreme that they name: `routes`: in the 256 rows of one device no expert is named by more than 10 slots, a bound that some block reaches.
All inputs are finite; a program needn't handle non-finite values.
Results may differ from a plain program's by a relative error of at most 0.0049.
Values may be sent and summed in bfloat16 or wider, within the bound.
No kernel may reach another device: no remote copies, remote signals or barrier semaphores. Data moves between devices by JAX's collectives and lax.ppermute only.
A program may use at most 128 MiB of HBM per device.

v0:
```python
import jax
import jax.numpy as jnp
from jax import lax
from jax.sharding import PartitionSpec as P


def shards(grad_out, gates, routes, w_down, saved_hidden):
    inner_n = lax.axis_size("inner")
    outer_n = lax.axis_size("outer")
    exp_dev = w_down.shape[0]
    experts = exp_dev * inner_n
    count_tokens, top_k = routes.shape
    width = grad_out.shape[1]
    capacity = saved_hidden.shape[1] // (outer_n * inner_n)
    slots_n = experts * capacity
    flat_routes = routes.reshape(-1)
    onehot = (flat_routes[:, None] == jnp.arange(experts, dtype=jnp.int32)[None, :]).astype(
        jnp.int32
    )
    position = jnp.sum((jnp.cumsum(onehot, axis=0) - onehot) * onehot, axis=1)
    local_index = flat_routes % exp_dev
    destination = flat_routes // exp_dev
    slot_index = (local_index * inner_n + destination) * capacity + position
    select = jnp.arange(slots_n, dtype=jnp.int32)[:, None] == slot_index[None, :]
    picker = jnp.sum(select.reshape(slots_n, count_tokens, top_k).astype(jnp.int32), axis=2).astype(
        jnp.bfloat16
    )
    send_rows = jnp.dot(picker, grad_out, preferred_element_type=jnp.float32).astype(jnp.bfloat16)
    gate_flat = gates.reshape(-1).astype(jnp.float32)
    send_gate = jnp.sum(jnp.where(select, gate_flat[None, :], 0.0), axis=1).astype(jnp.bfloat16)
    send_rows = send_rows.reshape(exp_dev, inner_n, capacity, width)
    send_gate = send_gate.reshape(exp_dev, inner_n, capacity)
    got_rows, got_gate = (
        lax.all_to_all(send_rows, "inner", split_axis=1, concat_axis=1, tiled=True),
        lax.all_to_all(send_gate, "inner", split_axis=1, concat_axis=1, tiled=True),
    )
    all_rows, all_gate = (
        lax.all_gather(got_rows, "outer", axis=1, tiled=True),
        lax.all_gather(got_gate, "outer", axis=1, tiled=True),
    )
    routed = all_rows.reshape(exp_dev, -1, width)
    gate_rows = all_gate.reshape(exp_dev, -1).astype(jnp.float32)
    backward = jnp.einsum("erd,efd->erf", routed, w_down, preferred_element_type=jnp.float32)
    d_hidden = (gate_rows[:, :, None] * backward).astype(jnp.bfloat16)
    scaled = (gate_rows[:, :, None] * routed.astype(jnp.float32)).astype(jnp.bfloat16)
    d_down = jnp.einsum(
        "erf,erd->efd", saved_hidden, scaled, preferred_element_type=jnp.float32
    ).astype(jnp.bfloat16)
    gate_terms = jnp.sum(saved_hidden.astype(jnp.float32) * backward, axis=2)
    gate_terms = gate_terms.reshape(exp_dev, outer_n, inner_n, capacity)
    summed = lax.psum_scatter(gate_terms, "outer", scatter_dimension=1, tiled=True)
    returned = lax.all_to_all(summed, "inner", split_axis=2, concat_axis=2, tiled=True)
    returned_flat = returned.reshape(-1)
    d_gates = jnp.sum(jnp.where(select, returned_flat[:, None], 0.0), axis=0).reshape(
        count_tokens, top_k
    )
    return (d_gates, d_down, d_hidden)


def solution(mesh):
    in_specs = (
        P(("outer", "inner"), None),
        P(("outer", "inner"), None),
        P(("outer", "inner"), None),
        P("inner", "outer", None),
        P("inner", None, "outer"),
    )
    out_specs = (P(("outer", "inner"), None), P("inner", "outer", None), P("inner", None, "outer"))
    return jax.shard_map(shards, mesh=mesh, in_specs=in_specs, out_specs=out_specs, check_vma=False)
```

profile of v0, /device:TPU:1, one launch (start us, length us, event | category | flops | bytes accessed | tf_op | source)
XLA Modules:
  0.0 517.5 jit_solution(14574945053318142977)
XLA Ops:
  7.2 0.9 copy.109
  9.5 0.7 fusion.23
  10.2 0.8 convert_reduce_fusion
  11.1 6.1 %convolution_convert_fusion = bf16[1280,3584]{1,0:T(8,128)(2,1)} fusion(bf16[256,3584]{1,0:T(8,128)(2,1)S(1)} %copy-done, s32[1280,256]{1,0:T(8,128)S(1)} %convert_reduce_fusion), kind=kOutput, calls=%fused_computation.5 | convolution fusion | flops 2353725440 | bytes 12320768 | tf_op jit(solution)/shard_map/dot_general | solution.py:28
  17.2 14.2 %reshape.124 = bf16[2,64,10,3584]{3,2,1,0:T(8,128)(2,1)} reshape(bf16[1280,3584]{1,0:T(8,128)(2,1)} %convolution_convert_fusion) | data formatting | bytes 18350080 | tf_op jit(solution)/shard_map/reshape | solution.py:31
  31.4 15.9 %copy.115 = bf16[2,64,10,3584]{3,0,2,1:T(2,128)(2,1)S(1)} copy(bf16[2,64,10,3584]{3,2,1,0:T(8,128)(2,1)} %reshape.124) | data formatting | bytes 18350080 | tf_op jit(solution)/shard_map/reshape | solution.py:31
  47.3 115.0 %all_to_all.15 = bf16[2,64,10,3584]{3,0,2,1:T(2,128)(2,1)} all-to-all(bf16[2,64,10,3584]{3,0,2,1:T(2,128)(2,1)S(1)} %copy.115), channel_id=1, replica_groups=mesh['outer'=2,'inner'=64] {'inner'}, dimensions={1} | all-to-all | bytes 18350080 | tf_op jit(solution)/shard_map/all_to_all | solution.py:34
  162.3 4.4 copy.113
  167.3 218.0 %all-gather.2.cloned.1.call-done = bf16[2,128,10,3584]{3,0,2,1:T(2,128)(2,1)} async-done(((bf16[2,64,10,3584]{3,0,2,1:T(2,128)(2,1)}), bf16[2,128,10,3584]{3,0,2,1:T(2,128)(2,1)}) %all-gather.2.cloned.1.call-update) | async-done | bytes 18350096 | tf_op jit(solution)/shard_map/all_gather | solution.py:38
  385.3 21.2 %multiply_reduce_fusion = (f32[2,1280]{1,0:T(2,128)S(1)}, f32[2,1280,512]{1,2,0:T(8,128)}) fusion(bf16[2,1280,512]{1,2,0:T(8,128)(2,1)} %copy.113, bf16[2,512,3584]{2,1,0:T(8,128)(2,1)} %param.8, bf16[2,1280,3584]{2,0,1:T(2,128)(2,1)} %bitcast.22), kind=kOutput, calls=%fused_computation.11 | convolution fusion | flops 9399171072 | bytes 33564672 | tf_op jit(solution)/shard_map/erd,efd->erf/dot_general | solution.py:43
  406.7 7.0 %all-reduce = f32[2,2,64,10]{2,0,3,1:T(2,128)S(1)} all-reduce(f32[2,2,64,10]{2,0,3,1:T(2,128)S(1)} %copy.117), channel_id=2, replica_groups=mesh['outer'=2,'inner'=64] {'outer'}, use_global_device_ids=true, to_apply=%region_5.6.clone | all-reduce | flops 2560 | bytes 20480
  414.3 0.7 copy.118
  415.1 10.6 %all-to-all-start.1 = ((f32[2,1,64,10]{3,1,0,2:T(1,128)}), f32[2,1,64,10]{3,1,0,2:T(1,128)S(1)}, u32[]{:S(2)}, u32[]{:S(2)}) async-start(f32[2,1,64,10]{3,1,0,2:T(1,128)} %copy.118), calls=%async_computation.1 | async-start | bytes 131072 | tf_op jit(solution)/shard_map/all_to_all | solution.py:52
  425.9 7.9 %all-to-all-done.1 = f32[2,1,64,10]{3,1,0,2:T(1,128)S(1)} async-done(((f32[2,1,64,10]{3,1,0,2:T(1,128)}), f32[2,1,64,10]{3,1,0,2:T(1,128)S(1)}, u32[]{:S(2)}, u32[]{:S(2)}) %all-to-all-start.1) | async-done | bytes 5152 | tf_op jit(solution)/shard_map/all_to_all | solution.py:52
  434.0 1.3 select_reduce_fusion
  436.1 4.4 all-to-all-start.2
  440.7 0.7 copy.126
  441.4 7.1 %all-to-all-done.2 = bf16[2,64,10]{2,0,1:T(2,128)(2,1)S(1)} async-done(((bf16[2,64,10]{2,0,1:T(2,128)(2,1)}), bf16[2,64,10]{2,0,1:T(2,128)(2,1)S(1)}, u32[]{:S(2)}, u32[]{:S(2)}) %all-to-all-start.2) | async-done | bytes 2592 | tf_op jit(solution)/shard_map/all_to_all | solution.py:35
  448.4 5.2 all_gather.7
  454.2 4.3 multiply_convert_fusion.1
  458.6 4.4 copy.128
  463.0 20.3 %multiply_convert_fusion = bf16[2,1280,3584]{2,0,1:T(2,128)(2,1)} fusion(f32[2,1280]{0,1:T(8,128)S(1)} %copy.124, bf16[2,128,10,3584]{3,0,2,1:T(2,128)(2,1)} %all-gather.2.cloned.1.call-done), kind=kLoop, calls=%fused_computation | loop fusion | flops 27525120 | bytes 36710400 | tf_op jit(solution)/shard_map/convert_element_type | solution.py:45
  483.2 17.5 %fusion.7 = bf16[2,512,3584]{1,2,0:T(8,128)(2,1)} fusion(bf16[2,1280,512]{2,1,0:T(8,128)(2,1)} %param.9, bf16[2,1280,3584]{2,0,1:T(2,128)(2,1)} %multiply_convert_fusion), kind=kOutput, calls=%fused_computation.7 | convolution fusion | flops 9398910976 | bytes 28311552 | tf_op jit(solution)/shard_map/erf,erd->efd/dot_general | solution.py:46
  500.7 9.9 %copy.127 = bf16[2,512,3584]{2,1,0:T(8,128)(2,1)} copy(bf16[2,512,3584]{1,2,0:T(8,128)(2,1)} %fusion.7) | data formatting | bytes 14680064
  (38 shorter events, 4.8 us)
Async XLA Ops:
  7.2 3.9 copy-start
  7.2 378.1 %all-gather.2.cloned.1.call-start = ((), (), s32[]{:S(2)}) async-start(), calls=%async_computation.3 | async-start | bytes 27525120 | tf_op jit(solution)/shard_map/all_gather | solution.py:38
  162.3 4.4 copy-start.3
  385.2 40.4 %copy-start.2 = (bf16[256,4]{0,1:T(4,128)(2,1)S(1)}, bf16[256,4]{0,1:T(4,128)(2,1)}, u32[]{:S(2)}) copy-start(bf16[256,4]{0,1:T(4,128)(2,1)} %param.6) | copy-start | bytes 6148
  415.1 18.8 %all-to-all-start.1 = ((f32[2,1,64,10]{3,1,0,2:T(1,128)}), f32[2,1,64,10]{3,1,0,2:T(1,128)S(1)}, u32[]{:S(2)}, u32[]{:S(2)}) async-start(f32[2,1,64,10]{3,1,0,2:T(1,128)} %copy.118), calls=%async_computation.1 | async-start | bytes 131072 | tf_op jit(solution)/shard_map/all_to_all | solution.py:52
  436.1 12.3 %all-to-all-start.2 = ((bf16[2,64,10]{2,0,1:T(2,128)(2,1)}), bf16[2,64,10]{2,0,1:T(2,128)(2,1)S(1)}, u32[]{:S(2)}, u32[]{:S(2)}) async-start(bf16[2,64,10]{2,0,1:T(2,128)(2,1)} %copy.121), calls=%async_computation.2 | async-start | bytes 65536 | tf_op jit(solution)/shard_map/all_to_all | solution.py:35
  483.2 27.4 %copy-start.1 = (bf16[256,3584]{1,0:T(8,128)(2,1)S(1)}, bf16[256,3584]{1,0:T(8,128)(2,1)}, u32[]{:S(2)}) copy-start(bf16[256,3584]{1,0:T(8,128)(2,1)} %param.5) | copy-start | bytes 5505028
Sparse Core Ops, SparseCore 0:
  162.4 222.7 all-gather.1
where the time goes:
time: 519 us; the launch traced here: 517 us
  waiting for transfers between devices  233 us (45%)
  blocking collectives  127 us (24%)
  local copies, waits for them, and re-layouts  55.2 us (11%)
  matrix products  44.8 us (9%)
  other arithmetic  28.1 us (5%)
  starting transfers between devices  15 us (3%)
  between operations  14.2 us (3%)
    all_gather x1, waiting for transfers between devices, shards(): lax.all_gather(got_rows, 'outer', axis=1, tiled=True)  218 us
    all_to_all x1, blocking collectives, shards(): lax.all_to_all(send_rows, 'inner', split_axis=1, concat_axis=1, tiled=True)  115 us
    reshape x2, local copies, waits for them, and re-layouts, shards(): send_rows = send_rows.reshape(exp_dev, inner_n, capacity, width)  30.1 us
    unnamed x15, local copies, waits for them, and re-layouts  21.6 us
    dot_general x1, matrix products, shards(): jnp.einsum('erd,efd->erf', routed, w_down, preferred_element_type=jnp.flo...  21.2 us
    convert_element_type x1, other arithmetic, shards(): (gate_rows[:, :, None] * routed.astype(jnp.float32)).astype(jnp.bfloat16)  20.3 us
    dot_general x1, matrix products, shards(): jnp.einsum('erf,erd->efd', saved_hidden, scaled, preferred_element_type=j...  17.5 us
    all_to_all x1, starting transfers between devices, shards(): lax.all_to_all(summed, 'inner', split_axis=2, concat_axis=2, tiled=True)  10.6 us
  transfers between devices with their start and end apart: 3, of which 3 were waited for; matrix products, arithmetic and copies ran while one was open for 1% of the time, Pallas kernels for 0%

commit v1 on v0

v1 whole, which is shorter than its diff:
```python
import jax
import jax.numpy as jnp
from jax import lax
from jax.sharding import Mesh, PartitionSpec as P

Z = ("zh", "zl")
PLANE = ("y", "x", "core")
ALL = ("zh", "zl", "y", "x", "core")
CAP = 10
BF = jnp.bfloat16
F32 = jnp.float32


def z_shift(value, step):
    return lax.ppermute(value, Z, [(i, (i + step) % 4) for i in range(4)])


def core_swap(value):
    return lax.ppermute(value, "core", [(0, 1), (1, 0)])


def picker(row_ids, rows):
    wanted = jnp.arange(rows, dtype=jnp.int32)[:, None]
    hit = row_ids[0][None, :] == wanted
    for k in range(1, row_ids.shape[0]):
        hit = hit | (row_ids[k][None, :] == wanted)
    return hit.astype(BF)


def dot(a, b, out=F32):
    return jnp.dot(a, b, preferred_element_type=F32).astype(out)


def shards(grad_out, gates, routes, w_down, saved_hidden):
    tokens, width = grad_out.shape
    zh, zl = lax.axis_index("zh"), lax.axis_index("zl")
    core = lax.axis_index("core")
    z = zh * 2 + zl
    inner = ((zl * 4 + lax.axis_index("y")) * 4 + lax.axis_index("x")) * 2 + core
    experts = 128
    hidden = w_down.shape[1]

    from_up = z_shift(grad_out, -1)
    from_down = z_shift(grad_out, 1)
    half = width // 2
    far = jnp.concatenate(
        [z_shift(from_down[:, :half], 1), z_shift(from_up[:, half:], -1)], axis=1
    )
    other = core_swap(grad_out)

    r = routes.T
    names = jnp.arange(experts, dtype=jnp.int32)
    onehot = routes[:, :, None] == names[None, None, :]
    named = jnp.any(onehot, axis=1).astype(BF)
    order = jnp.arange(tokens, dtype=jnp.int32)
    earlier = dot((order[:, None] > order[None, :]).astype(BF), named)
    pos = jnp.sum(jnp.where(onehot, earlier[:, None, :], 0.0), axis=2).astype(jnp.int32).T
    code = r * 16 + pos
    code_other = core_swap(code)

    def fields(c):
        pos, route = c % 16, c // 16
        e, dcore, yx, dzl = route % 2, (route // 2) % 2, (route // 4) % 16, route // 64
        return pos, e, dcore, yx, dzl

    def ids1(c, csrc):
        pos, e, dcore, yx, dzl = fields(c)
        return jnp.where((e == 1) & (dcore == core), yx * 40 + dzl * 20 + csrc * 10 + pos, -1)

    pick1 = picker(jnp.concatenate([ids1(code, core), ids1(code_other, 1 - core)], axis=1), 640)
    send1 = dot(pick1, jnp.concatenate([grad_out, other], axis=0), BF).reshape(16, 40, width)
    got1 = lax.all_to_all(send1, ("y", "x"), 0, 0, tiled=True).reshape(640, width)
    out_row = jnp.arange(320, dtype=jnp.int32)
    at_row = (out_row // 20) * 40 + out_row % 20
    source_row = jnp.arange(640, dtype=jnp.int32)[None, :]
    own = dot((source_row == (at_row + zl * 20)[:, None]).astype(BF), got1, BF)
    away = dot((source_row == (at_row + (1 - zl) * 20)[:, None]).astype(BF), got1, BF)
    rows1 = jnp.concatenate([own, z_shift(away, 1), z_shift(own, 2), z_shift(away, -1)], axis=0)

    codes = [code, z_shift(code, 1), z_shift(code, 2), z_shift(code, -1)]

    def ids0(c, zsrc):
        pos, e, dcore, yx, dzl = fields(c)
        return jnp.where((e == 0) & (dzl == zl), (yx * 2 + dcore) * 40 + zsrc * 10 + pos, -1)

    pick0 = picker(
        jnp.concatenate([ids0(c, (z - k) % 4) for k, c in enumerate(codes)], axis=1), 1280
    )
    line = jnp.concatenate([grad_out, from_down, far, from_up], axis=0)
    send0 = dot(pick0, line, BF).reshape(32, 40, width)
    rows0 = lax.all_to_all(send0, PLANE, 0, 0, tiled=True).reshape(1280, width)

    table = r * CAP + pos
    gate_table = jnp.sum(
        jnp.where(
            table.reshape(1, -1) == jnp.arange(experts * CAP, dtype=jnp.int32)[:, None],
            gates.T.reshape(1, -1).astype(F32),
            0.0,
        ),
        axis=1,
    ).astype(BF)
    all_gates = lax.all_gather(gate_table[None], ALL, axis=0, tiled=True)
    my_gates = lax.dynamic_slice(all_gates, (0, inner * 20), (128, 20)).astype(F32)

    def to0(a):
        return a.reshape(4, 32, CAP, -1).transpose(1, 0, 2, 3).reshape(1280, -1)

    def from0(a):
        return a.reshape(32, 4, CAP, -1).transpose(1, 0, 2, 3).reshape(1280, -1)

    def to1(a):
        a = a.reshape(4, 320, -1)
        return jnp.concatenate(
            [lax.dynamic_index_in_dim(a, (z - k) % 4, 0, False) for k in range(4)], axis=0
        )

    def from1(a):
        a = a.reshape(4, 320, -1)
        return jnp.concatenate(
            [lax.dynamic_index_in_dim(a, (z - i) % 4, 0, False) for i in range(4)], axis=0
        )

    def expert(rows, weight, saved, gate):
        back = lax.dot_general(rows, weight, (((1,), (1,)), ((), ())), preferred_element_type=F32)
        d_hidden = (gate * back).astype(BF)
        scaled = (gate * rows.astype(F32)).astype(BF)
        d_down = lax.dot_general(
            saved, scaled, (((0,), (0,)), ((), ())), preferred_element_type=F32
        ).astype(BF)
        terms = jnp.sum(saved.astype(F32) * back, axis=1, keepdims=True)
        return d_hidden, d_down, terms

    gate0 = to0(my_gates[:, :CAP].reshape(1280, 1))
    gate1 = to1(my_gates[:, CAP:].reshape(1280, 1))
    dh0, dd0, terms0 = expert(rows0, w_down[0], to0(saved_hidden[0]), gate0)
    dh1, dd1, terms1 = expert(rows1, w_down[1], to1(saved_hidden[1]), gate1)
    d_hidden = jnp.stack([from0(dh0), from1(dh1)])
    d_down = jnp.stack([dd0, dd1])

    terms = jnp.concatenate(
        [from0(terms0).reshape(128, CAP), from1(terms1).reshape(128, CAP)], axis=1
    )
    returned = lax.all_to_all(terms, ALL, 0, 0, tiled=True)
    returned = (returned[:64] + returned[64:]).reshape(-1)
    d_gates = jnp.sum(
        jnp.where(
            table.reshape(1, -1) == jnp.arange(experts * CAP, dtype=jnp.int32)[:, None],
            returned[:, None],
            0.0,
        ),
        axis=0,
    ).reshape(4, tokens).T
    return d_gates, d_down, d_hidden


def solution(mesh):
    fine = Mesh(mesh.devices.reshape(2, 2, 4, 4, 2), ALL)
    in_specs = (
        P(ALL, None),
        P(ALL, None),
        P(ALL, None),
        P(("zl", "y", "x", "core"), "zh", None),
        P(("zl", "y", "x", "core"), None, "zh"),
    )
    out_specs = (P(ALL, None), in_specs[3], in_specs[4])
    return jax.shard_map(shards, mesh=fine, in_specs=in_specs, out_specs=out_specs, check_vma=False)
```

time: 519 us -> 347 us (0.67)
  waiting for transfers between devices: 233 us -> 138 us
  blocking collectives: 127 us -> 34.9 us
  matrix products: 44.8 us -> 75.8 us
  local copies, waits for them, and re-layouts: 55.2 us -> 28.9 us
  starting transfers between devices: 15 us -> 39.5 us
  between operations: 14.2 us -> 1.3 us
  other arithmetic: 28.1 us -> 22.9 us
    all_gather x1 -> x0, waiting for transfers between devices: 218 us -> none  [shards(): lax.all_gather(got_rows, 'outer', axis=1, tiled=True)]
    ppermute x0 -> x12, waiting for transfers between devices: none -> 126 us  [the longest x10 125 us: z_shift(): return lax.ppermute(value, Z, [(i, (i + step) % 4) for i in range(4)])]
    all_to_all x1 -> x0, blocking collectives: 115 us -> none  [shards(): lax.all_to_all(send_rows, 'inner', split_axis=1, concat_axis=1, tiled=True)]
    dot_general x3 -> x9, matrix products: 44.8 us -> 75.8 us  [the longest x5 35.1 us: dot(): return jnp.dot(a, b, preferred_element_type=F32).astype(out)]
    all_gather x1, blocking collectives: 5.15 us -> 34.9 us  [shards(): all_gates = lax.all_gather(gate_table[None], ALL, axis=0, tiled=True)]
    reshape x6 -> x5, local copies, waits for them, and re-layouts: 30.6 us -> 4.99 us  [the longest x1 3.73 us: to0(): return a.reshape(4, 32, CAP, -1).transpose(1, 0, 2, 3).reshape(1280, -1)]
    ppermute x0 -> x12, starting transfers between devices: none -> 18 us  [the longest x10 16.1 us: z_shift(): return lax.ppermute(value, Z, [(i, (i + step) % 4) for i in range(4)])]
    unnamed x15 -> x28, local copies, waits for them, and re-layouts: 21.6 us -> 9.99 us
  transfers between devices with their start and end apart: 3 -> 15, of which waited for: 3 -> 8; matrix products, arithmetic and copies ran while one was open for 1% -> 18% of each run, Pallas kernels for 0% -> 0%
where the time goes in v1:
time: 347 us; the launch traced here: 341 us
  waiting for transfers between devices  138 us (40%)
  matrix products  75.8 us (22%)
  starting transfers between devices  39.5 us (11%)
  blocking collectives  34.9 us (10%)
  local copies, waits for them, and re-layouts  28.9 us (8%)
  other arithmetic  22.9 us (7%)
    ppermute x10, waiting for transfers between devices, z_shift(): return lax.ppermute(value, Z, [(i, (i + step) % 4) for i in range(4)])  125 us
    dot_general x5, matrix products, dot(): return jnp.dot(a, b, preferred_element_type=F32).astype(out)  35.1 us
    all_gather x1, blocking collectives, shards(): all_gates = lax.all_gather(gate_table[None], ALL, axis=0, tiled=True)  34.9 us
    dot_general x2, matrix products, expert(): lax.dot_general(rows, weight, (((1,), (1,)), ((), ())), preferred_element...  23.6 us
    dot_general x2, matrix products, expert(): lax.dot_general(saved, scaled, (((0,), (0,)), ((), ())), preferred_elemen...  17.1 us
    ppermute x10, starting transfers between devices, z_shift(): return lax.ppermute(value, Z, [(i, (i + step) % 4) for i in range(4)])  16.1 us
    convert_element_type x1, other arithmetic, expert(): scaled = (gate * rows.astype(F32)).astype(BF)  10.7 us
    unnamed x28, local copies, waits for them, and re-layouts  9.99 us
  transfers between devices with their start and end apart: 15, of which 8 were waited for; matrix products, arithmetic and copies ran while one was open for 18% of the time, Pallas kernels for 0%

profile of v1, /device:TPU:1, one launch (start us, length us, event | category | flops | bytes accessed | tf_op | source)
XLA Modules:
  0.0 341.4 jit_solution(9084522025186407254)
XLA Ops:
  2.1 3.9 %collective-permute-start.5 = (bf16[256,3584]{1,0:T(8,128)(2,1)}, bf16[256,3584]{1,0:T(8,128)(2,1)S(1)}, u32[]{:S(2)}, u32[]{:S(2)}) collective-permute-start(bf16[256,3584]{1,0:T(8,128)(2,1)} %param.5), channel_id=1, source_target_pairs={{0,96},{32,0},{64,32},{96,64},{1,97},{33,1},{65,33},{97,65},{2,98}... | collective-permute-start | bytes 5505032 | tf_op jit(solution)/shard_map/ppermute | solution.py:15
  10.2 6.9 %convolution_convert_fusion.1 = bf16[640,3584]{1,0:T(8,128)(2,1)} fusion(bf16[256,3584]{1,0:T(8,128)(2,1)} %collective-permute-done.8, bf16[256,3584]{1,0:T(8,128)(2,1)} %param.5, s32[512]{0:T(512)S(1)} %bitcast.118, s32[512]{0:T(512)S(1)} %bitcast.119, s32[512]{0:T(512)S(1)} %bitcast.117, s32[512]{0:T(512)S(1)} %bitcast.116), kind=kOutput, calls=%fused_computation.16 | convolution fusion | flops 2360737792 | bytes 8265728 | tf_op jit(solution)/shard_map/dot_general | solution.py:31
  17.1 6.8 %all-to-all-start.1 = ((bf16[16,40,3584]{2,1,0:T(8,128)(2,1)}), bf16[16,40,3584]{2,1,0:T(8,128)(2,1)}, u32[]{:S(2)}, u32[]{:S(2)}) async-start(bf16[16,40,3584]{2,1,0:T(8,128)(2,1)} %bitcast.103), calls=%async_computation.1 | async-start | bytes 9175040 | tf_op jit(solution)/shard_map/all_to_all | solution.py:72
  24.0 4.1 %collective-permute-start.1 = (s32[4,256]{1,0:T(4,128)S(1)}, s32[4,256]{1,0:T(4,128)S(1)}, u32[]{:S(2)}, u32[]{:S(2)}) collective-permute-start(s32[4,256]{1,0:T(4,128)S(1)} %get-tuple-element.18), channel_id=1, source_target_pairs={{0,64},{32,96},{64,0},{96,32},{1,65},{33,97},{65,1},{97,33},{2,66}... | collective-permute-start | bytes 12296 | tf_op jit(solution)/shard_map/ppermute | solution.py:15
  28.1 17.6 %collective-permute-done.5 = bf16[256,3584]{1,0:T(8,128)(2,1)S(1)} collective-permute-done((bf16[256,3584]{1,0:T(8,128)(2,1)}, bf16[256,3584]{1,0:T(8,128)(2,1)S(1)}, u32[]{:S(2)}, u32[]{:S(2)}) %collective-permute-start.5) | collective-permute-done | bytes 1835040 | tf_op jit(solution)/shard_map/ppermute | solution.py:15
  45.8 3.5 %collective-permute-start.6 = (bf16[256,1792]{1,0:T(8,128)(2,1)S(1)}, bf16[256,1792]{1,0:T(8,128)(2,1)S(1)}, u32[]{:S(2)}, u32[]{:S(2)}) collective-permute-start(bf16[256,1792]{1,0:T(8,128)(2,1)S(1)} %slice.79), channel_id=1, source_target_pairs={{0,96},{32,0},{64,32},{96,64},{1,97},{33,1},{65,33},{97,65},{2,98}... | collective-permute-start | bytes 2752520 | tf_op jit(solution)/shard_map/ppermute | solution.py:15
  51.0 17.2 %collective-permute-done.6 = bf16[256,1792]{1,0:T(8,128)(2,1)S(1)} collective-permute-done((bf16[256,1792]{1,0:T(8,128)(2,1)S(1)}, bf16[256,1792]{1,0:T(8,128)(2,1)S(1)}, u32[]{:S(2)}, u32[]{:S(2)}) %collective-permute-start.6) | collective-permute-done | bytes 917536 | tf_op jit(solution)/shard_map/ppermute | solution.py:15
  68.2 4.7 %collective-permute-done.4 = bf16[256,1792]{1,0:T(8,128)(2,1)S(1)} collective-permute-done((bf16[256,1792]{1,0:T(8,128)(2,1)S(1)}, bf16[256,1792]{1,0:T(8,128)(2,1)S(1)}, u32[]{:S(2)}, u32[]{:S(2)}) %collective-permute-start.4) | collective-permute-done | bytes 917536 | tf_op jit(solution)/shard_map/ppermute | solution.py:15
  72.9 16.7 %convolution_convert_fusion = bf16[1280,3584]{1,0:T(8,128)(2,1)} fusion(bf16[256,3584]{1,0:T(8,128)(2,1)S(1)} %collective-permute-done.5, bf16[256,1792]{1,0:T(8,128)(2,1)S(1)} %collective-permute-done.6, bf16[256,1792]{1,0:T(8,128)(2,1)S(1)} %collective-permute-done.4, bf16[256,3584]{1,0:T(8,128)(2,1)} %collective-permute-done.3, ...), kind=kOutput, calls=%fused_computation.2 | convolution fusion | flops 9445703680 | bytes 16531456 | tf_op jit(solution)/shard_map/dot_general | solution.py:31
  92.4 6.7 %all-to-all-start = ((bf16[32,40,3584]{2,1,0:T(8,128)(2,1)}), bf16[32,40,3584]{2,1,0:T(8,128)(2,1)}, u32[]{:S(2)}, u32[]{:S(2)}) async-start(bf16[32,40,3584]{2,1,0:T(8,128)(2,1)} %bitcast.97), calls=%async_computation | async-start | bytes 18350080 | tf_op jit(solution)/shard_map/all_to_all | solution.py:91
  99.2 5.7 %convolution_convert_fusion.3 = bf16[320,3584]{1,0:T(8,128)(2,1)} fusion(bf16[640,3584]{1,0:T(8,128)(2,1)} %bitcast.21, s32[320]{0:T(512)S(1)} %broadcast_add_fusion), kind=kOutput, calls=%fused_computation.21 | convolution fusion | flops 1469358080 | bytes 6882560 | tf_op jit(solution)/shard_map/dot_general | solution.py:31
  107.8 5.7 %convolution_convert_fusion.4 = bf16[320,3584]{1,0:T(8,128)(2,1)} fusion(bf16[640,3584]{1,0:T(8,128)(2,1)} %bitcast.21, s32[320]{0:T(512)S(1)} %broadcast_add_fusion.1), kind=kOutput, calls=%fused_computation.22 | convolution fusion | flops 1469358080 | bytes 6882560 | tf_op jit(solution)/shard_map/dot_general | solution.py:31
  119.9 3.7 %reshape.95 = bf16[1280,512]{1,0:T(8,128)(2,1)} reshape(bf16[32,4,10,512]{3,2,1,0:T(8,128)(2,1)} %copy.37) | data formatting | bytes 2621440 | tf_op jit(solution)/shard_map/reshape | solution.py:106
  123.8 82.3 %collective-permute-done.11 = bf16[320,3584]{1,0:T(8,128)(2,1)} collective-permute-done((bf16[320,3584]{1,0:T(8,128)(2,1)}, bf16[320,3584]{1,0:T(8,128)(2,1)}, u32[]{:S(2)}, u32[]{:S(2)}) %collective-permute-start.11) | collective-permute-done | bytes 2293792 | tf_op jit(solution)/shard_map/ppermute | solution.py:15
  209.3 12.1 %multiply_reduce_fusion = (f32[1280]{0:T(1024)S(1)}, f32[1280,512]{1,0:T(8,128)S(1)}) fusion(bf16[320,512]{1,0:T(8,128)(2,1)S(1)} %get-tuple-element.26, bf16[320,512]{1,0:T(8,128)(2,1)S(1)} %get-tuple-element.27, bf16[320,512]{1,0:T(8,128)(2,1)S(1)} %get-tuple-element.28, bf16[320,512]{1,0:T(8,128)(2,1)S(1)} %get-tuple-element.25, ...), kind=kOutput, calls=%fused_computation.45 | convolution fusion | flops 4740873216 | bytes 16782336 | tf_op jit(solution)/shard_map/dot_general | solution.py:124
  221.8 11.5 %multiply_reduce_fusion.1 = (f32[1280]{0:T(1024)S(1)}, f32[1280,512]{1,0:T(8,128)}) fusion(bf16[1280,512]{1,0:T(8,128)(2,1)} %reshape.95, bf16[1280,3584]{1,0:T(8,128)(2,1)} %bitcast.8, bf16[2,512,3584]{2,1,0:T(8,128)(2,1)} %param.8), kind=kOutput, calls=%fused_computation.46 | convolution fusion | flops 4699585536 | bytes 16782336 | tf_op jit(solution)/shard_map/dot_general | solution.py:124
  234.4 7.9 %all-to-all-start.2 = ((f32[128,1,20]{2,1,0:T(1,128)}), f32[128,1,20]{2,1,0:T(1,128)S(1)}, u32[]{:S(2)}, u32[]{:S(2)}) async-start(f32[128,1,20]{2,1,0:T(1,128)} %copy.40), calls=%async_computation.2 | async-start | bytes 131072 | tf_op jit(solution)/shard_map/all_to_all | solution.py:143
  242.4 9.5 %all-to-all-done.2 = f32[128,1,20]{2,1,0:T(1,128)S(1)} async-done(((f32[128,1,20]{2,1,0:T(1,128)}), f32[128,1,20]{2,1,0:T(1,128)S(1)}, u32[]{:S(2)}, u32[]{:S(2)}) %all-to-all-start.2) | async-done | bytes 10272 | tf_op jit(solution)/shard_map/all_to_all | solution.py:143
  253.5 34.9 %all-gather.1 = bf16[128,1,1280]{2,1,0:T(2,128)(2,1)S(1)} all-gather(bf16[1,1,1280]{2,1,0:T(2,128)(2,1)S(1)} %reshape.106), channel_id=2, replica_groups=mesh['zh'=2,'zl'=2,'y'=4,'x'=4,'core'=2] {'zh','zl','y','x','core'}, dimensions={0}, use_global_device_ids=true | all-gather | bytes 330240 | tf_op jit(solution)/shard_map/all_gather | solution.py:102
  291.2 10.7 %multiply_convert_fusion.1 = bf16[32,40,3584]{2,1,0:T(8,128)(2,1)} fusion(bf16[32,40,3584]{2,1,0:T(8,128)(2,1)} %all-to-all-done, f32[32,40]{1,0:T(8,128)S(1)} %copy.43), kind=kLoop, calls=%fused_computation.1 | loop fusion | flops 13762560 | bytes 18355200 | tf_op jit(solution)/shard_map/convert_element_type | solution.py:126
  301.9 9.0 %fusion.12 = bf16[1,512,3584]{1,2,0:T(8,128)(2,1)S(1)} fusion(bf16[1280,3584]{1,0:T(8,128)(2,1)} %bitcast.98, bf16[1280,512]{1,0:T(8,128)(2,1)S(1)} %copy-done.5), kind=kOutput, calls=%fused_computation.19 | convolution fusion | flops 4699455488 | bytes 14155776 | tf_op jit(solution)/shard_map/dot_general | solution.py:127
  310.9 8.1 %fusion.13 = bf16[1,512,3584]{1,2,0:T(8,128)(2,1)S(1)} fusion(f32[1280]{0:T(1024)S(1)} %reduce.2, bf16[320,3584]{1,0:T(8,128)(2,1)} %collective-permute-done.11, bf16[320,3584]{1,0:T(8,128)(2,1)} %collective-permute-done.10, bf16[320,3584]{1,0:T(8,128)(2,1)} %collective-permute-done.9, bf16[320,3584]{1,0:T(8,128)(2,1)} %convolution_convert_fusion.4, ...), kind=kOutput, calls=%fused_computation.20 | convolution fusion | flops 4750573568 | bytes 14160896 | tf_op jit(solution)/shard_map/dot_general | solution.py:127
  319.1 3.6 %pad_maximum_fusion.1 = bf16[2,512,3584]{1,2,0:T(8,128)(2,1)} fusion(bf16[1,512,3584]{1,2,0:T(8,128)(2,1)S(1)} %fusion.13, bf16[1,512,3584]{1,2,0:T(8,128)(2,1)S(1)} %fusion.12), kind=kLoop, calls=%fused_computation.15 | loop fusion | flops 3670016 | bytes 14680064 | tf_op jit(solution)/shard_map/stack | solution.py:138
  322.6 9.9 %copy.47 = bf16[2,512,3584]{2,1,0:T(8,128)(2,1)} copy(bf16[2,512,3584]{1,2,0:T(8,128)(2,1)} %pad_maximum_fusion.1) | data formatting | bytes 14680064
  (103 shorter events, 37.4 us)
Async XLA Ops:
  0.6 9.6 %collective-permute-start.8 = (bf16[256,3584]{1,0:T(8,128)(2,1)}, bf16[256,3584]{1,0:T(8,128)(2,1)}, u32[]{:S(2)}, u32[]{:S(2)}) collective-permute-start(bf16[256,3584]{1,0:T(8,128)(2,1)} %param.5), channel_id=1, source_target_pairs={{0,1},{1,0},{2,3},{3,2},{4,5},{5,4},{6,7},{7,6},{8,9},{9,8},{10,11... | collective-permute-start | bytes 5505032 | tf_op jit(solution)/shard_map/ppermute | solution.py:19
  2.1 43.6 %collective-permute-start.5 = (bf16[256,3584]{1,0:T(8,128)(2,1)}, bf16[256,3584]{1,0:T(8,128)(2,1)S(1)}, u32[]{:S(2)}, u32[]{:S(2)}) collective-permute-start(bf16[256,3584]{1,0:T(8,128)(2,1)} %param.5), channel_id=1, source_target_pairs={{0,96},{32,0},{64,32},{96,64},{1,97},{33,1},{65,33},{97,65},{2,98}... | collective-permute-start | bytes 5505032 | tf_op jit(solution)/shard_map/ppermute | solution.py:15
  6.0 43.3 %collective-permute-start.3 = (bf16[256,3584]{1,0:T(8,128)(2,1)}, bf16[256,3584]{1,0:T(8,128)(2,1)}, u32[]{:S(2)}, u32[]{:S(2)}) collective-permute-start(bf16[256,3584]{1,0:T(8,128)(2,1)} %param.5), channel_id=1, source_target_pairs={{0,32},{32,64},{64,96},{96,0},{1,33},{33,65},{65,97},{97,1},{2,34}... | collective-permute-start | bytes 5505032 | tf_op jit(solution)/shard_map/ppermute | solution.py:15
  8.9 1.3 collective-permute-start.7
  17.1 75.2 %all-to-all-start.1 = ((bf16[16,40,3584]{2,1,0:T(8,128)(2,1)}), bf16[16,40,3584]{2,1,0:T(8,128)(2,1)}, u32[]{:S(2)}, u32[]{:S(2)}) async-start(bf16[16,40,3584]{2,1,0:T(8,128)(2,1)} %bitcast.103), calls=%async_computation.1 | async-start | bytes 9175040 | tf_op jit(solution)/shard_map/all_to_all | solution.py:72
  23.9 26.9 %collective-permute-start = (s32[4,256]{1,0:T(4,128)S(1)}, s32[4,256]{1,0:T(4,128)S(1)}, u32[]{:S(2)}, u32[]{:S(2)}) collective-permute-start(s32[4,256]{1,0:T(4,128)S(1)} %get-tuple-element.18), channel_id=1, source_target_pairs={{0,32},{32,64},{64,96},{96,0},{1,33},{33,65},{65,97},{97,1},{2,34}... | collective-permute-start | bytes 12296 | tf_op jit(solution)/shard_map/ppermute | solution.py:15
  24.0 26.9 %collective-permute-start.1 = (s32[4,256]{1,0:T(4,128)S(1)}, s32[4,256]{1,0:T(4,128)S(1)}, u32[]{:S(2)}, u32[]{:S(2)}) collective-permute-start(s32[4,256]{1,0:T(4,128)S(1)} %get-tuple-element.18), channel_id=1, source_target_pairs={{0,64},{32,96},{64,0},{96,32},{1,65},{33,97},{65,1},{97,33},{2,66}... | collective-permute-start | bytes 12296 | tf_op jit(solution)/shard_map/ppermute | solution.py:15
  28.1 22.8 %collective-permute-start.2 = (s32[4,256]{1,0:T(4,128)S(1)}, s32[4,256]{1,0:T(4,128)S(1)}, u32[]{:S(2)}, u32[]{:S(2)}) collective-permute-start(s32[4,256]{1,0:T(4,128)S(1)} %get-tuple-element.18), channel_id=1, source_target_pairs={{0,96},{32,0},{64,32},{96,64},{1,97},{33,1},{65,33},{97,65},{2,98}... | collective-permute-start | bytes 12296 | tf_op jit(solution)/shard_map/ppermute | solution.py:15
  45.8 22.4 %collective-permute-start.6 = (bf16[256,1792]{1,0:T(8,128)(2,1)S(1)}, bf16[256,1792]{1,0:T(8,128)(2,1)S(1)}, u32[]{:S(2)}, u32[]{:S(2)}) collective-permute-start(bf16[256,1792]{1,0:T(8,128)(2,1)S(1)} %slice.79), channel_id=1, source_target_pairs={{0,96},{32,0},{64,32},{96,64},{1,97},{33,1},{65,33},{97,65},{2,98}... | collective-permute-start | bytes 2752520 | tf_op jit(solution)/shard_map/ppermute | solution.py:15
  50.5 22.3 %collective-permute-start.4 = (bf16[256,1792]{1,0:T(8,128)(2,1)S(1)}, bf16[256,1792]{1,0:T(8,128)(2,1)S(1)}, u32[]{:S(2)}, u32[]{:S(2)}) collective-permute-start(bf16[256,1792]{1,0:T(8,128)(2,1)S(1)} %slice.78), channel_id=1, source_target_pairs={{0,32},{32,64},{64,96},{96,0},{1,33},{33,65},{65,97},{97,1},{2,34}... | collective-permute-start | bytes 2752520 | tf_op jit(solution)/shard_map/ppermute | solution.py:15
  92.4 129.4 %all-to-all-start = ((bf16[32,40,3584]{2,1,0:T(8,128)(2,1)}), bf16[32,40,3584]{2,1,0:T(8,128)(2,1)}, u32[]{:S(2)}, u32[]{:S(2)}) async-start(bf16[32,40,3584]{2,1,0:T(8,128)(2,1)} %bitcast.97), calls=%async_computation | async-start | bytes 18350080 | tf_op jit(solution)/shard_map/all_to_all | solution.py:91
  104.8 101.2 %collective-permute-start.11 = (bf16[320,3584]{1,0:T(8,128)(2,1)}, bf16[320,3584]{1,0:T(8,128)(2,1)}, u32[]{:S(2)}, u32[]{:S(2)}) collective-permute-start(bf16[320,3584]{1,0:T(8,128)(2,1)} %convolution_convert_fusion.3), channel_id=1, source_target_pairs={{0,96},{32,0},{64,32},{96,64},{1,97},{33,1},{65,33},{97,65},{2,98}... | collective-permute-start | bytes 6881288 | tf_op jit(solution)/shard_map/ppermute | solution.py:15
  107.8 101.5 %collective-permute-start.9 = (bf16[320,3584]{1,0:T(8,128)(2,1)}, bf16[320,3584]{1,0:T(8,128)(2,1)}, u32[]{:S(2)}, u32[]{:S(2)}) collective-permute-start(bf16[320,3584]{1,0:T(8,128)(2,1)} %convolution_convert_fusion.3), channel_id=1, source_target_pairs={{0,32},{32,64},{64,96},{96,0},{1,33},{33,65},{65,97},{97,1},{2,34}... | collective-permute-start | bytes 6881288 | tf_op jit(solution)/shard_map/ppermute | solution.py:15
  113.5 95.8 %collective-permute-start.10 = (bf16[320,3584]{1,0:T(8,128)(2,1)}, bf16[320,3584]{1,0:T(8,128)(2,1)}, u32[]{:S(2)}, u32[]{:S(2)}) collective-permute-start(bf16[320,3584]{1,0:T(8,128)(2,1)} %convolution_convert_fusion.4), channel_id=1, source_target_pairs={{0,64},{32,96},{64,0},{96,32},{1,65},{33,97},{65,1},{97,33},{2,66}... | collective-permute-start | bytes 6881288 | tf_op jit(solution)/shard_map/ppermute | solution.py:15
  119.9 3.7 %copy-start = (bf16[1,1280,512]{2,1,0:T(8,128)(2,1)S(1)}, bf16[1,1280,512]{2,1,0:T(8,128)(2,1)}, u32[]{:S(2)}) copy-start(bf16[1,1280,512]{2,1,0:T(8,128)(2,1)} %get-tuple-element.20) | copy-start | bytes 3932164
  119.9 3.9 %copy-start.10 = (s32[256,4]{0,1:T(4,128)S(1)}, s32[256,4]{0,1:T(4,128)}, u32[]{:S(2)}) copy-start(s32[256,4]{0,1:T(4,128)} %param.7) | copy-start | bytes 12292
  123.7 97.6 %copy-start.6 = (bf16[320,512]{1,0:T(8,128)(2,1)}, bf16[320,512]{1,0:T(8,128)(2,1)S(1)}, u32[]{:S(2)}) copy-start(bf16[320,512]{1,0:T(8,128)(2,1)S(1)} %get-tuple-element.27) | copy-start | bytes 983044
  123.7 97.6 %copy-start.8 = (bf16[320,512]{1,0:T(8,128)(2,1)}, bf16[320,512]{1,0:T(8,128)(2,1)S(1)}, u32[]{:S(2)}) copy-start(bf16[320,512]{1,0:T(8,128)(2,1)S(1)} %get-tuple-element.28) | copy-start | bytes 983044
  221.8 20.5 %copy-start.11 = (bf16[256,4]{0,1:T(4,128)(2,1)S(1)}, bf16[256,4]{0,1:T(4,128)(2,1)}, u32[]{:S(2)}) copy-start(bf16[256,4]{0,1:T(4,128)(2,1)} %param.6) | copy-start | bytes 6148
  234.4 17.5 %all-to-all-start.2 = ((f32[128,1,20]{2,1,0:T(1,128)}), f32[128,1,20]{2,1,0:T(1,128)S(1)}, u32[]{:S(2)}, u32[]{:S(2)}) async-start(f32[128,1,20]{2,1,0:T(1,128)} %copy.40), calls=%async_computation.2 | async-start | bytes 131072 | tf_op jit(solution)/shard_map/all_to_all | solution.py:143
  291.2 10.7 %copy-start.5 = (bf16[1280,512]{1,0:T(8,128)(2,1)S(1)}, bf16[1280,512]{1,0:T(8,128)(2,1)}, u32[]{:S(2)}) copy-start(bf16[1280,512]{1,0:T(8,128)(2,1)} %reshape.95) | copy-start | bytes 3932164
  301.9 9.0 %copy-start.7 = (bf16[320,512]{1,0:T(8,128)(2,1)S(1)}, bf16[320,512]{1,0:T(8,128)(2,1)}, u32[]{:S(2)}) copy-start(bf16[320,512]{1,0:T(8,128)(2,1)} %copy-done.6) | copy-start | bytes 983044
  301.9 9.0 %copy-start.9 = (bf16[320,512]{1,0:T(8,128)(2,1)S(1)}, bf16[320,512]{1,0:T(8,128)(2,1)}, u32[]{:S(2)}) copy-start(bf16[320,512]{1,0:T(8,128)(2,1)} %copy-done.8) | copy-start | bytes 983044
  336.7 2.7 copy-start.4
  (3 other events, 8.1 us)

commit v2 on v0

v2 whole, which is shorter than its diff:
```python
import functools

import jax
import jax.numpy as jnp
from jax import lax
from jax.experimental import pallas as pl
from jax.experimental.pallas import tpu as pltpu
from jax.sharding import Mesh, PartitionSpec as P

Z = ("zh", "zl")
PLANE = ("y", "x", "core")
ALL = ("zh", "zl", "y", "x", "core")
CAP = 10
TOP = 4
EXPERTS = 128
BF = jnp.bfloat16
F32 = jnp.float32
I32 = jnp.int32
PARAMS = dict(vmem_limit_bytes=48 * 1024 * 1024)


def z_shift(value, step):
    return lax.ppermute(value, Z, [(i, (i + step) % 4) for i in range(4)])


def core_swap(value):
    return lax.ppermute(value, "core", [(0, 1), (1, 0)])


def dot(a, b):
    return jnp.dot(a, b, preferred_element_type=F32)


def cost(flops, nbytes):
    return pl.CostEstimate(flops=int(flops), bytes_accessed=int(nbytes), transcendentals=0)


def positions(meta):
    tokens = meta.shape[1]
    names = lax.broadcasted_iota(I32, (EXPERTS, tokens), 0)
    routes = [meta[k : k + 1, :].astype(I32) for k in range(TOP)]
    hits = [names == r for r in routes]
    named = sum(h.astype(F32) for h in hits)
    first = lax.broadcasted_iota(I32, (tokens, tokens), 0)
    second = lax.broadcasted_iota(I32, (tokens, tokens), 1)
    earlier = dot(named.astype(BF), (first < second).astype(F32).astype(BF))
    places = [
        jnp.sum(jnp.where(h, earlier, 0.0), axis=0, keepdims=True).astype(I32) for h in hits
    ]
    return routes, places


def pick_kernel(sources, expert, where, scalars, *refs):
    metas, tokens = refs[:sources], refs[sources : 2 * sources]
    out, picker = refs[2 * sources], refs[2 * sources + 1]
    rows = picker.shape[0]
    count = metas[0].shape[1]

    @pl.when(pl.program_id(0) == 0)
    def _():
        for s in range(sources):
            meta = metas[s][...]
            routes, places = positions(meta)
            total = jnp.zeros((rows, count), F32)
            wanted = lax.broadcasted_iota(I32, (rows, count), 0)
            for k in range(TOP):
                r = routes[k]
                row = where(scalars, s, r >> 6, (r >> 2) & 15, (r >> 1) & 1, places[k])
                row = jnp.where((r & 1) == expert, row, -1)
                total = total + jnp.where(wanted == row, meta[TOP + k : TOP + k + 1, :], 0.0)
            picker[:, s * count : (s + 1) * count] = total.astype(BF)

    step = 320
    for at in range(0, rows, step):
        total = dot(picker[at : at + step, :count], tokens[0][...])
        for s in range(1, sources):
            total = total + dot(
                picker[at : at + step, s * count : (s + 1) * count], tokens[s][...]
            )
        out[at : at + step, :] = total.astype(BF)


def where_plane_first(scalars, s, dzl, dyx, dcore, place):
    core = scalars[2]
    source = core if s == 0 else 1 - core
    return jnp.where(dcore == core, dyx * 40 + dzl * 20 + source * CAP + place, -1)


def where_line_first(scalars, s, dzl, dyx, dcore, place):
    source = (scalars[0] + 4 - s) & 3
    return jnp.where(dzl == scalars[1], (dyx * 2 + dcore) * 40 + source * CAP + place, -1)


def pick(scalars, metas, tokens, rows, expert, where, block, first, blocks):
    sources = len(metas)
    count = metas[0].shape[1]
    whole = pl.BlockSpec((8, count), lambda j, s: (0, 0))
    return pl.pallas_call(
        functools.partial(pick_kernel, sources, expert, where),
        out_shape=jax.ShapeDtypeStruct((rows, blocks * block), BF),
        grid_spec=pltpu.PrefetchScalarGridSpec(
            num_scalar_prefetch=1,
            grid=(blocks,),
            in_specs=[whole] * sources
            + [
                pl.BlockSpec((count, block), functools.partial(lambda o, j, s: (0, j + o), o))
                for _, o in tokens
            ],
            out_specs=pl.BlockSpec((rows, block), lambda j, s: (0, j)),
            scratch_shapes=[pltpu.VMEM((rows, sources * count), BF)],
        ),
        compiler_params=pltpu.CompilerParams(**PARAMS),
        cost_estimate=cost(
            2 * rows * sources * count * blocks * block,
            2 * (rows + sources * count) * blocks * block,
        ),
    )(scalars, *metas, *[t for t, _ in tokens])


def part_kernel(scalars, got, own, away, picker):
    @pl.when(pl.program_id(0) == 0)
    def _():
        zl = scalars[1]
        for side, layer in ((0, zl), (1, 1 - zl)):
            row = lax.broadcasted_iota(I32, (320, 640), 0)
            source = lax.broadcasted_iota(I32, (320, 640), 1)
            group = row // 20
            hit = source == row + (group + layer) * 20
            picker[side * 320 : side * 320 + 320, :] = hit.astype(F32).astype(BF)

    away[...] = dot(picker[320:, :], got[...]).astype(BF)
    own[...] = dot(picker[:320, :], got[...]).astype(BF)


def part(scalars, got, block, first, blocks):
    shape = jax.ShapeDtypeStruct((320, blocks * block), BF)
    spec = pl.BlockSpec((320, block), lambda j, s: (0, j))
    return pl.pallas_call(
        part_kernel,
        out_shape=(shape, shape),
        grid_spec=pltpu.PrefetchScalarGridSpec(
            num_scalar_prefetch=1,
            grid=(blocks,),
            in_specs=[pl.BlockSpec((640, block), lambda j, s: (0, j + first))],
            out_specs=(spec, spec),
            scratch_shapes=[pltpu.VMEM((640, 640), BF)],
        ),
        compiler_params=pltpu.CompilerParams(**PARAMS),
        cost_estimate=cost(2 * 640 * 640 * blocks * block, 4 * 640 * blocks * block),
    )(scalars, got)


def back_kernel(pieces, has_before, *refs):
    rows, weight = refs[:pieces], refs[pieces]
    refs = refs[pieces + 1 :]
    before = refs[0] if has_before else None
    refs = refs[has_before:]
    size = rows[0].shape[0]
    if has_before:
        saved, hidden, terms, total = refs
    else:
        total = refs[0]

    @pl.when(pl.program_id(0) == 0)
    def _():
        total[...] = before[...] if has_before else jnp.zeros_like(total)

    step = 320
    for p in range(pieces):
        for at in range(0, size, step):
            total[p * size + at : p * size + at + step, :] += lax.dot_general(
                rows[p][at : at + step, :],
                weight[...],
                (((1,), (1,)), ((), ())),
                preferred_element_type=F32,
            )

    if has_before:

        @pl.when(pl.program_id(0) == pl.num_programs(0) - 1)
        def _():
            for at in range(0, pieces * size, step):
                back = total[at : at + step, :]
                hidden[at : at + step, :] = back.astype(BF)
                terms[at : at + step, :] = jnp.sum(
                    saved[at : at + step, :].astype(F32) * back, axis=1, keepdims=True
                )


def back(rows, weight, expert, block, first, blocks, before=None, saved=None):
    pieces, size = len(rows), rows[0].shape[0]
    hidden = weight.shape[1]
    shape = (pieces * size, hidden)
    whole = pl.BlockSpec(shape, lambda j: (0, 0))
    has_before = before is not None
    in_specs = [pl.BlockSpec((size, block), lambda j: (0, j))] * pieces + [
        pl.BlockSpec((None, hidden, block), lambda j: (expert, 0, j + first))
    ]
    args = [*rows, weight]
    if has_before:
        in_specs += [whole, whole]
        args += [before, saved]
        out_shape = (
            jax.ShapeDtypeStruct(shape, BF),
            jax.ShapeDtypeStruct((pieces * size, 1), F32),
        )
        out_specs = (whole, pl.BlockSpec((pieces * size, 1), lambda j: (0, 0)))
        scratch = [pltpu.VMEM(shape, F32)]
    else:
        out_shape, out_specs, scratch = jax.ShapeDtypeStruct(shape, F32), whole, []
    return pl.pallas_call(
        functools.partial(back_kernel, pieces, has_before),
        out_shape=out_shape,
        grid=(blocks,),
        in_specs=in_specs,
        out_specs=out_specs,
        scratch_shapes=scratch,
        compiler_params=pltpu.CompilerParams(**PARAMS),
        cost_estimate=cost(
            2 * pieces * size * hidden * blocks * block, 2 * pieces * size * blocks * block
        ),
    )(*args)


def down_kernel(pieces, *refs):
    saved_t, rows, out = refs[0], refs[1 : 1 + pieces], refs[-1]
    total = dot(saved_t[0], rows[0][...])
    for p in range(1, pieces):
        total = total + dot(saved_t[p], rows[p][...])
    out[...] = total.astype(BF)


def down(result, saved_t, rows, expert, block, first, blocks):
    pieces, size = len(rows), rows[0].shape[0]
    hidden = saved_t.shape[1]
    in_specs = [pl.BlockSpec(saved_t.shape, lambda j: (0, 0, 0))] + [
        pl.BlockSpec((size, block), lambda j: (0, j))
    ] * pieces
    args = [saved_t, *rows]
    width = 7 * block
    aliases = {}
    if result is not None:
        in_specs.append(pl.BlockSpec(memory_space=pl.ANY))
        args.append(result)
        aliases = {len(args) - 1: 0}
    return pl.pallas_call(
        functools.partial(down_kernel, pieces),
        out_shape=jax.ShapeDtypeStruct((2, hidden, width), BF),
        grid=(blocks,),
        in_specs=in_specs,
        out_specs=pl.BlockSpec((None, hidden, block), lambda j: (expert, 0, j + first)),
        input_output_aliases=aliases,
        compiler_params=pltpu.CompilerParams(**PARAMS),
        cost_estimate=cost(
            2 * pieces * size * hidden * blocks * block, 2 * pieces * size * blocks * block
        ),
    )(*args)


def shards(grad_out, gates, routes, w_down, saved_hidden):
    tokens, width = grad_out.shape
    zh, zl = lax.axis_index("zh"), lax.axis_index("zl")
    core = lax.axis_index("core")
    z = zh * 2 + zl
    scalars = jnp.stack([z, zl, core]).astype(I32)
    block = width // 7
    parts = ((0, 4), (4, 3))
    cut = 4 * block

    meta = jnp.concatenate([routes.T.astype(F32), gates.T.astype(F32)], axis=0)
    meta_other, other = core_swap(meta), core_swap(grad_out)
    from_down, from_up = z_shift(grad_out, 1), z_shift(grad_out, -1)
    metas = [meta, z_shift(meta, 1), z_shift(meta, 2), z_shift(meta, -1)]

    send1 = pick(
        scalars, [meta, meta_other], [(grad_out, 0), (other, 0)], 640, 1, where_plane_first,
        block, 0, 7,
    )
    got1 = lax.all_to_all(send1.reshape(16, 40, width), ("y", "x"), 0, 0, tiled=True)
    got1 = got1.reshape(640, width)

    far = (z_shift(from_down[:, :cut], 1), z_shift(from_up[:, cut:], -1))
    rows0 = []
    for (first, blocks), distant in zip(parts, far):
        send0 = pick(
            scalars, metas,
            [(grad_out, first), (from_down, first), (distant, 0), (from_up, first)],
            1280, 0, where_line_first, block, first, blocks,
        )
        got0 = lax.all_to_all(send0.reshape(32, 40, blocks * block), PLANE, 0, 0, tiled=True)
        rows0.append([got0.reshape(1280, blocks * block)])

    rows1 = []
    for first, blocks in parts:
        own, away = part(scalars, got1, block, first, blocks)
        rows1.append([own, z_shift(away, 1), z_shift(own, 2), z_shift(away, -1)])

    def swapped(a, one, two):
        return a.reshape(one, two, CAP, -1).transpose(1, 0, 2, 3).reshape(one * two * CAP, -1)

    def turned(a):
        a = a.reshape(4, 320, -1)
        return jnp.concatenate(
            [lax.dynamic_index_in_dim(a, (z - k) % 4, 0, False) for k in range(4)], axis=0
        )

    saved0 = swapped(saved_hidden[0], 4, 32)
    saved1 = turned(saved_hidden[1])
    saved0_t = saved0.T[None]
    saved1_t = saved1.reshape(4, 320, -1).transpose(0, 2, 1)

    d_down = down(None, saved1_t, rows1[0], 1, block, *parts[0])
    before1 = back(rows1[0], w_down, 1, block, *parts[0])
    d_down = down(d_down, saved0_t, rows0[0], 0, block, *parts[0])
    before0 = back(rows0[0], w_down, 0, block, *parts[0])
    d_down = down(d_down, saved1_t, rows1[1], 1, block, *parts[1])
    hidden1, terms1 = back(rows1[1], w_down, 1, block, *parts[1], before1, saved1)
    hidden0, terms0 = back(rows0[1], w_down, 0, block, *parts[1], before0, saved0)
    d_down = down(d_down, saved0_t, rows0[1], 0, block, *parts[1])
    d_hidden = jnp.stack([swapped(hidden0, 32, 4), turned(hidden1)])

    terms = jnp.concatenate(
        [swapped(terms0, 32, 4).reshape(128, CAP), turned(terms1).reshape(128, CAP)], axis=1
    )
    returned = lax.all_to_all(terms, ALL, 0, 0, tiled=True)
    returned = (returned[:64] + returned[64:]).reshape(-1)

    names = jnp.arange(EXPERTS, dtype=I32)
    onehot = routes[:, :, None] == names[None, None, :]
    order = jnp.arange(tokens, dtype=I32)
    earlier = dot(
        (order[:, None] > order[None, :]).astype(BF), jnp.any(onehot, axis=1).astype(BF)
    )
    place = jnp.sum(jnp.where(onehot, earlier[:, None, :], 0.0), axis=2).astype(I32)
    table = (routes * CAP + place).T.reshape(1, -1)
    d_gates = jnp.sum(
        jnp.where(
            table == jnp.arange(EXPERTS * CAP, dtype=I32)[:, None], returned[:, None], 0.0
        ),
        axis=0,
    ).reshape(TOP, tokens).T
    return d_gates / gates.astype(F32), d_down, d_hidden


def solution(mesh):
    fine = Mesh(mesh.devices.reshape(2, 2, 4, 4, 2), ALL)
    in_specs = (
        P(ALL, None),
        P(ALL, None),
        P(ALL, None),
        P(("zl", "y", "x", "core"), "zh", None),
        P(("zl", "y", "x", "core"), None, "zh"),
    )
    out_specs = (P(ALL, None), in_specs[3], in_specs[4])
    return jax.shard_map(shards, mesh=fine, in_specs=in_specs, out_specs=out_specs, check_vma=False)
```

time: 519 us -> 362 us (0.70)
  blocking collectives: 127 us -> 0 us
  Pallas kernels: 0 us -> 97.5 us
  waiting for transfers between devices: 233 us -> 150 us
  starting transfers between devices: 15 us -> 71.6 us
  matrix products: 44.8 us -> 0.17 us
  local copies, waits for them, and re-layouts: 55.2 us -> 31.1 us
  other arithmetic: 28.1 us -> 9.45 us
  between operations: 14.2 us -> 0.99 us
    all_gather x1 -> x0, waiting for transfers between devices: 218 us -> none  [shards(): lax.all_gather(got_rows, 'outer', axis=1, tiled=True)]
    ppermute x0 -> x15, waiting for transfers between devices: none -> 122 us  [the longest x13 121 us: z_shift(): return lax.ppermute(value, Z, [(i, (i + step) % 4) for i in range(4)])]
    all_to_all x1 -> x0, blocking collectives: 115 us -> none  [shards(): lax.all_to_all(send_rows, 'inner', split_axis=1, concat_axis=1, tiled=True)]
    pallas_call x0 -> x13, Pallas kernels: none -> 97.5 us  [the longest x3 35.8 us: pick(): pl.pallas_call(functools.partial(pick_kernel, sources, expert, where), ou...]
    dot_general x3 -> x1, matrix products: 44.8 us -> 0.17 us  [dot(): return jnp.dot(a, b, preferred_element_type=F32)]
    all_to_all x2 -> x4, starting transfers between devices: 15 us -> 55.3 us  [the longest x1 31 us: shards(): returned = lax.all_to_all(terms, ALL, 0, 0, tiled=True)]
    convert_element_type x2 -> x1, other arithmetic: 24.6 us -> 0.69 us  [shards(): meta = jnp.concatenate([routes.T.astype(F32), gates.T.astype(F32)], axis=0)]
    reshape x6 -> x9, local copies, waits for them, and re-layouts: 30.6 us -> 8.55 us  [the longest x4 5.71 us: swapped(): a.reshape(one, two, CAP, -1).transpose(1, 0, 2, 3)]
  transfers between devices with their start and end apart: 3 -> 19, of which waited for: 3 -> 9; matrix products, arithmetic and copies ran while one was open for 1% -> 8% of each run, Pallas kernels for 0% -> 23%
where the time goes in v2:
time: 362 us; the launch traced here: 361 us
  waiting for transfers between devices  150 us (41%)
  Pallas kernels  97.5 us (27%)
  starting transfers between devices  71.6 us (20%)
  local copies, waits for them, and re-layouts  31.1 us (9%)
  other arithmetic  9.45 us (3%)
    ppermute x13, waiting for transfers between devices, z_shift(): return lax.ppermute(value, Z, [(i, (i + step) % 4) for i in range(4)])  121 us
    pallas_call x3, Pallas kernels, pick(): pl.pallas_call(functools.partial(pick_kernel, sources, expert, where), ou...  35.8 us
    all_to_all x1, starting transfers between devices, shards(): returned = lax.all_to_all(terms, ALL, 0, 0, tiled=True)  31 us
    all_to_all x2, waiting for transfers between devices, shards(): lax.all_to_all(send0.reshape(32, 40, blocks * block), PLANE, 0, 0, tiled=...  28.1 us
    pallas_call x4, Pallas kernels, down(): pl.pallas_call(functools.partial(down_kernel, pieces), out_shape=jax.Shap...  25.4 us
    pallas_call x4, Pallas kernels, back(): pl.pallas_call(functools.partial(back_kernel, pieces, has_before), out_sh...  24.9 us
    all_to_all x2, starting transfers between devices, shards(): lax.all_to_all(send0.reshape(32, 40, blocks * block), PLANE, 0, 0, tiled=...  17.4 us
    ppermute x13, starting transfers between devices, z_shift(): return lax.ppermute(value, Z, [(i, (i + step) % 4) for i in range(4)])  14.7 us
  transfers between devices with their start and end apart: 19, of which 9 were waited for; matrix products, arithmetic and copies ran while one was open for 8% of the time, Pallas kernels for 23%

profile of v2, /device:TPU:1, one launch (start us, length us, event | category | flops | bytes accessed | tf_op | source)
XLA Modules:
  0.0 360.8 jit_solution(11941778091220920070)
XLA Ops:
  8.5 7.8 %shard_map.80 = bf16[640,3584]{1,0:T(8,128)(2,1)} custom-call(s32[3]{0:T(128)S(1)} %pad_add_fusion.scalars, f32[8,256]{1,0:T(8,128)S(1)} %pad_maximum_fusion.2.refs_0_, f32[8,256]{1,0:T(8,128)S(1)} %collective-permute-done.7.refs_1_, bf16[256,3584]{1,0:T(8,128)(2,1)S(1)} %copy-done.8, bf16[256,3584]{1,0:T(8,128)(2,1)S(1)} %collective-permute-done.8.refs_3_), custom_call_target="tpu_custom_call" | custom-call | flops 2348810240 | bytes 8257536 | tf_op jit(solution)/shard_map/pallas_call | solution.py:98
  16.3 6.9 %all-to-all-start.2 = ((bf16[16,40,3584]{2,1,0:T(8,128)(2,1)}), bf16[16,40,3584]{2,1,0:T(8,128)(2,1)}, u32[]{:S(2)}, u32[]{:S(2)}) async-start(bf16[16,40,3584]{2,1,0:T(8,128)(2,1)} %bitcast.70), calls=%async_computation.2 | async-start | bytes 9175040 | tf_op jit(solution)/shard_map/all_to_all | solution.py:279
  27.2 40.2 %collective-permute-done.3.refs_5_ = bf16[256,3584]{1,0:T(8,128)(2,1)S(1)} collective-permute-done((bf16[256,3584]{1,0:T(8,128)(2,1)}, bf16[256,3584]{1,0:T(8,128)(2,1)S(1)}, u32[]{:S(2)}, u32[]{:S(2)}) %collective-permute-start.3) | collective-permute-done | bytes 1835040 | tf_op jit(solution)/shard_map/ppermute | solution.py:23
  72.0 21.0 %collective-permute-done.refs_1_ = f32[8,256]{1,0:T(8,128)S(1)} collective-permute-done((f32[8,256]{1,0:T(8,128)S(1)}, f32[8,256]{1,0:T(8,128)S(1)}, u32[]{:S(2)}, u32[]{:S(2)}) %collective-permute-start) | collective-permute-done | bytes 8224 | tf_op jit(solution)/shard_map/ppermute | solution.py:23
  94.2 14.7 %shard_map.77 = bf16[1280,2048]{1,0:T(8,128)(2,1)} custom-call(s32[3]{0:T(128)S(1)} %pad_add_fusion.scalars, f32[8,256]{1,0:T(8,128)S(1)} %pad_maximum_fusion.2.refs_0_, f32[8,256]{1,0:T(8,128)S(1)} %collective-permute-done.refs_1_, f32[8,256]{1,0:T(8,128)S(1)} %collective-permute-done.1.refs_2_, f32[8,256]{1,0:T(8,128)S(1)} %collective-permute-done.2.refs_3_, ...), custom_call_target="tpu_custom_call" | custom-call | flops 5368709120 | bytes 9437184 | tf_op jit(solution)/shard_map/pallas_call | solution.py:98
  108.9 8.4 %all-to-all-start.1 = ((bf16[32,40,2048]{2,1,0:T(8,128)(2,1)}), bf16[32,40,2048]{2,1,0:T(8,128)(2,1)}, u32[]{:S(2)}, u32[]{:S(2)}) async-start(bf16[32,40,2048]{2,1,0:T(8,128)(2,1)} %bitcast.68), calls=%async_computation.1 | async-start | bytes 10485760 | tf_op jit(solution)/shard_map/all_to_all | solution.py:290
  118.7 5.9 %shard_map.82 = (bf16[320,2048]{1,0:T(8,128)(2,1)}, bf16[320,2048]{1,0:T(8,128)(2,1)}) custom-call(s32[3]{0:T(128)S(1)} %pad_add_fusion.scalars, bf16[640,3584]{1,0:T(8,128)(2,1)} %bitcast.13.got), custom_call_target="tpu_custom_call" | custom-call | flops 1677721600 | bytes 5242880 | tf_op jit(solution)/shard_map/pallas_call | solution.py:138
  126.0 11.6 %collective-permute-done.5.refs_6_ = bf16[256,1536]{1,0:T(8,128)(2,1)S(1)} collective-permute-done((bf16[256,1536]{1,0:T(8,128)(2,1)S(1)}, bf16[256,1536]{1,0:T(8,128)(2,1)S(1)}, u32[]{:S(2)}, u32[]{:S(2)}) %collective-permute-start.5) | collective-permute-done | bytes 786464 | tf_op jit(solution)/shard_map/ppermute | solution.py:23
  137.6 13.2 %shard_map.76 = bf16[1280,1536]{1,0:T(8,128)(2,1)} custom-call(s32[3]{0:T(128)S(1)} %pad_add_fusion.scalars, f32[8,256]{1,0:T(8,128)S(1)} %pad_maximum_fusion.2.refs_0_, f32[8,256]{1,0:T(8,128)S(1)} %collective-permute-done.refs_1_, f32[8,256]{1,0:T(8,128)S(1)} %collective-permute-done.1.refs_2_, f32[8,256]{1,0:T(8,128)S(1)} %collective-permute-done.2.refs_3_, ...), custom_call_target="tpu_custom_call" | custom-call | flops 4026531840 | bytes 7077888 | tf_op jit(solution)/shard_map/pallas_call | solution.py:98
  150.8 28.1 %all-to-all-done.1 = bf16[32,40,2048]{2,1,0:T(8,128)(2,1)} async-done(((bf16[32,40,2048]{2,1,0:T(8,128)(2,1)}), bf16[32,40,2048]{2,1,0:T(8,128)(2,1)}, u32[]{:S(2)}, u32[]{:S(2)}) %all-to-all-start.1) | async-done | bytes 5242912 | tf_op jit(solution)/shard_map/all_to_all | solution.py:290
  178.9 9.0 %all-to-all-start = ((bf16[32,40,1536]{2,1,0:T(8,128)(2,1)}), bf16[32,40,1536]{2,1,0:T(8,128)(2,1)}, u32[]{:S(2)}, u32[]{:S(2)}) async-start(bf16[32,40,1536]{2,1,0:T(8,128)(2,1)} %bitcast.71), calls=%async_computation | async-start | bytes 7864320 | tf_op jit(solution)/shard_map/all_to_all | solution.py:290
  189.0 5.5 %shard_map.81 = (bf16[320,1536]{1,0:T(8,128)(2,1)}, bf16[320,1536]{1,0:T(8,128)(2,1)}) custom-call(s32[3]{0:T(128)S(1)} %pad_add_fusion.scalars, bf16[640,3584]{1,0:T(8,128)(2,1)} %bitcast.13.got), custom_call_target="tpu_custom_call" | custom-call | flops 1258291200 | bytes 3932160 | tf_op jit(solution)/shard_map/pallas_call | solution.py:138
  209.8 9.9 %collective-permute-done.13.refs_2_.refs_3_ = bf16[320,2048]{1,0:T(8,128)(2,1)} collective-permute-done((bf16[320,2048]{1,0:T(8,128)(2,1)}, bf16[320,2048]{1,0:T(8,128)(2,1)}, u32[]{:S(2)}, u32[]{:S(2)}) %collective-permute-start.13) | collective-permute-done | bytes 1310752 | tf_op jit(solution)/shard_map/ppermute | solution.py:23
  219.7 25.5 %collective-permute-done.14.refs_3_.refs_4_ = bf16[320,2048]{1,0:T(8,128)(2,1)} collective-permute-done((bf16[320,2048]{1,0:T(8,128)(2,1)}, bf16[320,2048]{1,0:T(8,128)(2,1)}, u32[]{:S(2)}, u32[]{:S(2)}) %collective-permute-start.14) | collective-permute-done | bytes 1310752 | tf_op jit(solution)/shard_map/ppermute | solution.py:23
  246.6 7.2 %shard_map.83.refs_5_ = f32[1280,512]{1,0:T(8,128)} custom-call(bf16[320,2048]{1,0:T(8,128)(2,1)} %get-tuple-element.14.refs_0_.refs_1_, bf16[320,2048]{1,0:T(8,128)(2,1)S(1)} %copy-done.4, bf16[320,2048]{1,0:T(8,128)(2,1)} %collective-permute-done.13.refs_2_.refs_3_, bf16[320,2048]{1,0:T(8,128)(2,1)} %collective-permute-done.14.refs_3_.refs_4_, ...), custom_call_target="tpu_custom_call" | custom-call | flops 2684354560 | bytes 5242880 | tf_op jit(solution)/shard_map/pallas_call | solution.py:211
  253.7 8.1 %collective-permute-done.10.refs_2_.refs_3_ = bf16[320,1536]{1,0:T(8,128)(2,1)} collective-permute-done((bf16[320,1536]{1,0:T(8,128)(2,1)}, bf16[320,1536]{1,0:T(8,128)(2,1)}, u32[]{:S(2)}, u32[]{:S(2)}) %collective-permute-start.10) | collective-permute-done | bytes 983072 | tf_op jit(solution)/shard_map/ppermute | solution.py:23
  266.3 6.7 %shard_map.84 = (bf16[1280,512]{1,0:T(8,128)(2,1)S(1)}, f32[1280,1]{1,0:T(8,128)S(1)}) custom-call(bf16[320,1536]{1,0:T(8,128)(2,1)} %get-tuple-element.12.refs_0_.refs_1_, bf16[320,1536]{1,0:T(8,128)(2,1)} %collective-permute-done.9.refs_1_.refs_2_, bf16[320,1536]{1,0:T(8,128)(2,1)} %collective-permute-done.10.refs_2_.refs_3_, ...), custom_call_target="tpu_custom_call" | custom-call | flops 2013265920 | bytes 3932160 | tf_op jit(solution)/shard_map/pallas_call | solution.py:211
  276.5 7.7 %shard_map.85.refs_2_ = bf16[2,512,3584]{2,1,0:T(8,128)(2,1)} custom-call(bf16[4,512,320]{2,1,0:T(8,128)(2,1)} %bitcast.60, bf16[320,2048]{1,0:T(8,128)(2,1)} %get-tuple-element.14.refs_0_.refs_1_, bf16[320,2048]{1,0:T(8,128)(2,1)S(1)} %copy-done.5, bf16[320,2048]{1,0:T(8,128)(2,1)} %collective-permute-done.13.refs_2_.refs_3_, ...), custom_call_target="tpu_custom_call" | custom-call | flops 2684354560 | bytes 5242880 | tf_op jit(solution)/shard_map/pallas_call | solution.py:246
  285.4 5.9 %shard_map.78.refs_2_ = f32[1280,512]{1,0:T(8,128)S(1)} custom-call(bf16[1280,2048]{1,0:T(8,128)(2,1)} %bitcast.9.refs_0_.refs_1_, bf16[2,512,3584]{2,1,0:T(8,128)(2,1)} %refs_4_.7), custom_call_target="tpu_custom_call" | custom-call | flops 2684354560 | bytes 5242880 | tf_op jit(solution)/shard_map/pallas_call | solution.py:211
  294.5 5.2 %shard_map.79 = (bf16[1280,512]{1,0:T(8,128)(2,1)S(1)}, f32[1280,1]{1,0:T(8,128)S(1)}) custom-call(bf16[1280,1536]{1,0:T(8,128)(2,1)} %bitcast.7.refs_0_.refs_1_, bf16[2,512,3584]{2,1,0:T(8,128)(2,1)} %refs_4_.7, f32[1280,512]{1,0:T(8,128)S(1)} %copy-done.2, bf16[1280,512]{1,0:T(8,128)(2,1)S(1)} %reshape.64.refs_3_), custom_call_target="tpu_custom_call" | custom-call | flops 2013265920 | bytes 3932160 | tf_op jit(solution)/shard_map/pallas_call | solution.py:211
  302.1 31.0 %all-to-all-start.3 = ((f32[128,1,20]{2,1,0:T(1,128)}), f32[128,1,20]{2,1,0:T(1,128)S(1)}, u32[]{:S(2)}, u32[]{:S(2)}) async-start(f32[128,1,20]{2,1,0:T(1,128)} %copy.34), calls=%async_computation.3 | async-start | bytes 131072 | tf_op jit(solution)/shard_map/all_to_all | solution.py:325
  339.6 6.4 %shard_map.86.refs_5_ = bf16[2,512,3584]{2,1,0:T(8,128)(2,1)} custom-call(bf16[1,512,1280]{2,1,0:T(8,128)(2,1)S(1)} %bitcast.62, bf16[1280,2048]{1,0:T(8,128)(2,1)} %bitcast.9.refs_0_.refs_1_, bf16[2,512,3584]{2,1,0:T(8,128)(2,1)} %shard_map.85.refs_2_), custom_call_target="tpu_custom_call", output_to_operand_aliasing={{}: (2, {})} | custom-call | flops 2684354560 | bytes 5242880 | tf_op jit(solution)/shard_map/pallas_call | solution.py:246
  348.0 6.0 %shard_map.87.refs_2_ = bf16[2,512,3584]{2,1,0:T(8,128)(2,1)} custom-call(bf16[4,512,320]{2,1,0:T(8,128)(2,1)S(1)} %bitcast.61, bf16[320,1536]{1,0:T(8,128)(2,1)} %get-tuple-element.12.refs_0_.refs_1_, bf16[320,1536]{1,0:T(8,128)(2,1)} %collective-permute-done.9.refs_1_.refs_2_, ...), custom_call_target="tpu_custom_call", output_to_operand_aliasing={{}: (5, {})} | custom-call | flops 2013265920 | bytes 3932160 | tf_op jit(solution)/shard_map/pallas_call | solution.py:246
  354.0 5.3 %shard_map.88 = bf16[2,512,3584]{2,1,0:T(8,128)(2,1)} custom-call(bf16[1,512,1280]{2,1,0:T(8,128)(2,1)S(1)} %bitcast.63, bf16[1280,1536]{1,0:T(8,128)(2,1)} %bitcast.7.refs_0_.refs_1_, bf16[2,512,3584]{2,1,0:T(8,128)(2,1)} %shard_map.87.refs_2_), custom_call_target="tpu_custom_call", output_to_operand_aliasing={{}: (2, {})} | custom-call | flops 2013265920 | bytes 3932160 | tf_op jit(solution)/shard_map/pallas_call | solution.py:246
  (99 shorter events, 62.6 us)
Async XLA Ops:
  0.6 6.4 %collective-permute-start.8 = (bf16[256,3584]{1,0:T(8,128)(2,1)}, bf16[256,3584]{1,0:T(8,128)(2,1)S(1)}, u32[]{:S(2)}, u32[]{:S(2)}) collective-permute-start(bf16[256,3584]{1,0:T(8,128)(2,1)} %refs_2_.1), channel_id=1, source_target_pairs={{0,1},{1,0},{2,3},{3,2},{4,5},{5,4},{6,7},{7,6},{8,9},{9,8},{10,11... | collective-permute-start | bytes 5505032 | tf_op jit(solution)/shard_map/ppermute | solution.py:27
  5.8 1.3 collective-permute-start.7
  16.3 92.6 %all-to-all-start.2 = ((bf16[16,40,3584]{2,1,0:T(8,128)(2,1)}), bf16[16,40,3584]{2,1,0:T(8,128)(2,1)}, u32[]{:S(2)}, u32[]{:S(2)}) async-start(bf16[16,40,3584]{2,1,0:T(8,128)(2,1)} %bitcast.70), calls=%async_computation.2 | async-start | bytes 9175040 | tf_op jit(solution)/shard_map/all_to_all | solution.py:279
  23.2 71.0 %copy-start.9 = (bf16[256,3584]{1,0:T(8,128)(2,1)S(1)}, bf16[256,3584]{1,0:T(8,128)(2,1)}, u32[]{:S(2)}) copy-start(bf16[256,3584]{1,0:T(8,128)(2,1)} %refs_2_.1) | copy-start | bytes 5505028
  23.2 44.1 %collective-permute-start.3 = (bf16[256,3584]{1,0:T(8,128)(2,1)}, bf16[256,3584]{1,0:T(8,128)(2,1)S(1)}, u32[]{:S(2)}, u32[]{:S(2)}) collective-permute-start(bf16[256,3584]{1,0:T(8,128)(2,1)} %refs_2_.1), channel_id=1, source_target_pairs={{0,32},{32,64},{64,96},{96,0},{1,33},{33,65},{65,97},{97,1},{2,34}... | collective-permute-start | bytes 5505032 | tf_op jit(solution)/shard_map/ppermute | solution.py:23
  25.0 68.0 %collective-permute-start.4 = (bf16[256,3584]{1,0:T(8,128)(2,1)}, bf16[256,3584]{1,0:T(8,128)(2,1)S(1)}, u32[]{:S(2)}, u32[]{:S(2)}) collective-permute-start(bf16[256,3584]{1,0:T(8,128)(2,1)} %refs_2_.1), channel_id=1, source_target_pairs={{0,96},{32,0},{64,32},{96,64},{1,97},{33,1},{65,33},{97,65},{2,98}... | collective-permute-start | bytes 5505032 | tf_op jit(solution)/shard_map/ppermute | solution.py:23
  67.5 25.5 %collective-permute-start.6 = (bf16[256,2048]{1,0:T(8,128)(2,1)S(1)}, bf16[256,2048]{1,0:T(8,128)(2,1)S(1)}, u32[]{:S(2)}, u32[]{:S(2)}) collective-permute-start(bf16[256,2048]{1,0:T(8,128)(2,1)S(1)} %slice.27), channel_id=1, source_target_pairs={{0,32},{32,64},{64,96},{96,0},{1,33},{33,65},{65,97},{97,1},{2,34}... | collective-permute-start | bytes 3145736 | tf_op jit(solution)/shard_map/ppermute | solution.py:23
  67.6 25.4 %collective-permute-start = (f32[8,256]{1,0:T(8,128)S(1)}, f32[8,256]{1,0:T(8,128)S(1)}, u32[]{:S(2)}, u32[]{:S(2)}) collective-permute-start(f32[8,256]{1,0:T(8,128)S(1)} %pad_maximum_fusion.2.refs_0_), channel_id=1, source_target_pairs={{0,32},{32,64},{64,96},{96,0},{1,33},{33,65},{65,97},{97,1},{2,34}... | collective-permute-start | bytes 24584 | tf_op jit(solution)/shard_map/ppermute | solution.py:23
  68.2 24.7 %collective-permute-start.1 = (f32[8,256]{1,0:T(8,128)S(1)}, f32[8,256]{1,0:T(8,128)S(1)}, u32[]{:S(2)}, u32[]{:S(2)}) collective-permute-start(f32[8,256]{1,0:T(8,128)S(1)} %pad_maximum_fusion.2.refs_0_), channel_id=1, source_target_pairs={{0,64},{32,96},{64,0},{96,32},{1,65},{33,97},{65,1},{97,33},{2,66}... | collective-permute-start | bytes 24584 | tf_op jit(solution)/shard_map/ppermute | solution.py:23
  71.4 21.5 %collective-permute-start.2 = (f32[8,256]{1,0:T(8,128)S(1)}, f32[8,256]{1,0:T(8,128)S(1)}, u32[]{:S(2)}, u32[]{:S(2)}) collective-permute-start(f32[8,256]{1,0:T(8,128)S(1)} %pad_maximum_fusion.2.refs_0_), channel_id=1, source_target_pairs={{0,96},{32,0},{64,32},{96,64},{1,97},{33,1},{65,33},{97,65},{2,98}... | collective-permute-start | bytes 24584 | tf_op jit(solution)/shard_map/ppermute | solution.py:23
  108.9 69.9 %all-to-all-start.1 = ((bf16[32,40,2048]{2,1,0:T(8,128)(2,1)}), bf16[32,40,2048]{2,1,0:T(8,128)(2,1)}, u32[]{:S(2)}, u32[]{:S(2)}) async-start(bf16[32,40,2048]{2,1,0:T(8,128)(2,1)} %bitcast.68), calls=%async_computation.1 | async-start | bytes 10485760 | tf_op jit(solution)/shard_map/all_to_all | solution.py:290
  118.6 19.0 %collective-permute-start.5 = (bf16[256,1536]{1,0:T(8,128)(2,1)S(1)}, bf16[256,1536]{1,0:T(8,128)(2,1)S(1)}, u32[]{:S(2)}, u32[]{:S(2)}) collective-permute-start(bf16[256,1536]{1,0:T(8,128)(2,1)S(1)} %slice.26), channel_id=1, source_target_pairs={{0,96},{32,0},{64,32},{96,64},{1,97},{33,1},{65,33},{97,65},{2,98}... | collective-permute-start | bytes 2359304 | tf_op jit(solution)/shard_map/ppermute | solution.py:23
  118.6 18.9 %copy-start.10 = (bf16[256,3584]{1,0:T(8,128)(2,1)S(1)}, bf16[256,3584]{1,0:T(8,128)(2,1)}, u32[]{:S(2)}) copy-start(bf16[256,3584]{1,0:T(8,128)(2,1)} %refs_2_.1) | copy-start | bytes 5505028
  124.6 72.6 %collective-permute-start.12 = (bf16[320,2048]{1,0:T(8,128)(2,1)}, bf16[320,2048]{1,0:T(8,128)(2,1)S(1)}, u32[]{:S(2)}, u32[]{:S(2)}) collective-permute-start(bf16[320,2048]{1,0:T(8,128)(2,1)} %get-tuple-element.15), channel_id=1, source_target_pairs={{0,32},{32,64},{64,96},{96,0},{1,33},{33,65},{65,97},{97,1},{2,34}... | collective-permute-start | bytes 3932168 | tf_op jit(solution)/shard_map/ppermute | solution.py:23
  178.9 113.9 %all-to-all-start = ((bf16[32,40,1536]{2,1,0:T(8,128)(2,1)}), bf16[32,40,1536]{2,1,0:T(8,128)(2,1)}, u32[]{:S(2)}, u32[]{:S(2)}) async-start(bf16[32,40,1536]{2,1,0:T(8,128)(2,1)} %bitcast.71), calls=%async_computation | async-start | bytes 7864320 | tf_op jit(solution)/shard_map/all_to_all | solution.py:290
  187.9 31.9 %collective-permute-start.13 = (bf16[320,2048]{1,0:T(8,128)(2,1)}, bf16[320,2048]{1,0:T(8,128)(2,1)}, u32[]{:S(2)}, u32[]{:S(2)}) collective-permute-start(bf16[320,2048]{1,0:T(8,128)(2,1)} %get-tuple-element.14.refs_0_.refs_1_), channel_id=1, source_target_pairs={{0,64},{32,96},{64,0},{96,32},{1,65},{33,97},{65,1},{97,33},{2,66}... | collective-permute-start | bytes 3932168 | tf_op jit(solution)/shard_map/ppermute | solution.py:23
  188.2 57.0 %collective-permute-start.14 = (bf16[320,2048]{1,0:T(8,128)(2,1)}, bf16[320,2048]{1,0:T(8,128)(2,1)}, u32[]{:S(2)}, u32[]{:S(2)}) collective-permute-start(bf16[320,2048]{1,0:T(8,128)(2,1)} %get-tuple-element.15), channel_id=1, source_target_pairs={{0,96},{32,0},{64,32},{96,64},{1,97},{33,1},{65,33},{97,65},{2,98}... | collective-permute-start | bytes 3932168 | tf_op jit(solution)/shard_map/ppermute | solution.py:23
  189.0 9.2 %copy-start.12 = (bf16[2,1280,512]{2,1,0:T(8,128)(2,1)S(1)}, bf16[2,1280,512]{2,1,0:T(8,128)(2,1)}, u32[]{:S(2)}) copy-start(bf16[2,1280,512]{2,1,0:T(8,128)(2,1)} %param.9) | copy-start | bytes 7864324
  194.5 59.2 %collective-permute-start.9 = (bf16[320,1536]{1,0:T(8,128)(2,1)}, bf16[320,1536]{1,0:T(8,128)(2,1)}, u32[]{:S(2)}, u32[]{:S(2)}) collective-permute-start(bf16[320,1536]{1,0:T(8,128)(2,1)} %get-tuple-element.13), channel_id=1, source_target_pairs={{0,32},{32,64},{64,96},{96,0},{1,33},{33,65},{65,97},{97,1},{2,34}... | collective-permute-start | bytes 2949128 | tf_op jit(solution)/shard_map/ppermute | solution.py:23
  195.2 71.2 %collective-permute-start.11 = (bf16[320,1536]{1,0:T(8,128)(2,1)}, bf16[320,1536]{1,0:T(8,128)(2,1)}, u32[]{:S(2)}, u32[]{:S(2)}) collective-permute-start(bf16[320,1536]{1,0:T(8,128)(2,1)} %get-tuple-element.13), channel_id=1, source_target_pairs={{0,96},{32,0},{64,32},{96,64},{1,97},{33,1},{65,33},{97,65},{2,98}... | collective-permute-start | bytes 2949128 | tf_op jit(solution)/shard_map/ppermute | solution.py:23
  197.2 64.7 %collective-permute-start.10 = (bf16[320,1536]{1,0:T(8,128)(2,1)}, bf16[320,1536]{1,0:T(8,128)(2,1)}, u32[]{:S(2)}, u32[]{:S(2)}) collective-permute-start(bf16[320,1536]{1,0:T(8,128)(2,1)} %get-tuple-element.12.refs_0_.refs_1_), channel_id=1, source_target_pairs={{0,64},{32,96},{64,0},{96,32},{1,65},{33,97},{65,1},{97,33},{2,66}... | collective-permute-start | bytes 2949128 | tf_op jit(solution)/shard_map/ppermute | solution.py:23
  302.1 57.2 %all-to-all-start.3 = ((f32[128,1,20]{2,1,0:T(1,128)}), f32[128,1,20]{2,1,0:T(1,128)S(1)}, u32[]{:S(2)}, u32[]{:S(2)}) async-start(f32[128,1,20]{2,1,0:T(1,128)} %copy.34), calls=%async_computation.3 | async-start | bytes 131072 | tf_op jit(solution)/shard_map/all_to_all | solution.py:325
  339.6 6.4 %copy-start.11 = (bf16[1,1280,512]{2,1,0:T(8,128)(2,1)S(1)}, bf16[1,1280,512]{2,1,0:T(8,128)(2,1)}, u32[]{:S(2)}) copy-start(bf16[1,1280,512]{2,1,0:T(8,128)(2,1)} %maximum_bitcast_fusion) | copy-start | bytes 3932164
  354.0 6.2 %copy-start.14 = (bf16[256,4]{0,1:T(4,128)(2,1)S(1)}, bf16[256,4]{0,1:T(4,128)(2,1)}, u32[]{:S(2)}) copy-start(bf16[256,4]{0,1:T(4,128)(2,1)} %param.6) | copy-start | bytes 6148
  (10 other events, 15.4 us)

commit v3 on v2

v3 whole, which is shorter than its diff:
```python
import functools

import jax
import jax.numpy as jnp
from jax import lax
from jax.experimental import pallas as pl
from jax.experimental.pallas import tpu as pltpu
from jax.sharding import Mesh, PartitionSpec as P

Z = ("zh", "zl")
PLANE = ("y", "x", "core")
ALL = ("zh", "zl", "y", "x", "core")
CAP = 10
TOP = 4
EXPERTS = 128
BF = jnp.bfloat16
F32 = jnp.float32
I32 = jnp.int32


def z_shift(value, step):
    return lax.ppermute(value, Z, [(i, (i + step) % 4) for i in range(4)])


def core_swap(value):
    return lax.ppermute(value, "core", [(0, 1), (1, 0)])


def dot(a, b):
    return jnp.dot(a, b, preferred_element_type=F32)


def call(body, token, args, in_specs, out_shape, out_specs, grid, micros, scratch=(), aliases=None,
         scalars=None, after=()):
    lead = 0 if scalars is None else 1
    extra = [token, *after]
    n_in, n_out = lead + len(args), len(out_shape)

    def run(*refs):
        outs = refs[n_in + len(extra) :]
        outs[n_out][...] = jnp.zeros((8, 128), F32)
        body(*refs[:n_in], *outs[:n_out], *outs[n_out + 1 :])

    result = pl.pallas_call(
        run,
        out_shape=[*out_shape, jax.ShapeDtypeStruct((8, 128), F32)],
        grid_spec=pltpu.PrefetchScalarGridSpec(
            num_scalar_prefetch=lead,
            grid=grid,
            in_specs=[*in_specs, *[pl.BlockSpec(memory_space=pl.ANY)] * len(extra)],
            out_specs=[*out_specs, pl.BlockSpec((8, 128), lambda j, *_: (0, 0))],
            scratch_shapes=list(scratch),
        ),
        input_output_aliases=aliases or {},
        compiler_params=pltpu.CompilerParams(vmem_limit_bytes=60 * 1024 * 1024),
        cost_estimate=pl.CostEstimate(
            flops=int(micros * 1e9), bytes_accessed=0, transcendentals=0
        ),
    )(*([] if scalars is None else [scalars]), *args, *extra)
    return result[:-1], result[-1]


def positions(meta):
    tokens = meta.shape[1]
    names = lax.broadcasted_iota(I32, (EXPERTS, tokens), 0)
    routes = [meta[k : k + 1, :].astype(I32) for k in range(TOP)]
    hits = [names == r for r in routes]
    named = sum(h.astype(F32) for h in hits)
    first = lax.broadcasted_iota(I32, (tokens, tokens), 0)
    second = lax.broadcasted_iota(I32, (tokens, tokens), 1)
    earlier = dot(named.astype(BF), (first < second).astype(F32).astype(BF))
    places = [
        jnp.sum(jnp.where(h, earlier, 0.0), axis=0, keepdims=True).astype(I32) for h in hits
    ]
    return routes, places


def extend_kernel(meta, tokens, out):
    count = tokens.shape[0]
    out[:count, :] = tokens[...]
    out[count:, :] = jnp.zeros((out.shape[0] - count, out.shape[1]), BF)
    out[count:, : meta.shape[1]] = jnp.concatenate(
        [meta[...], jnp.zeros_like(meta[...])], axis=0
    ).astype(BF)


def extend(token, meta, tokens):
    shape = (tokens.shape[0] + 16, tokens.shape[1])
    (out,), token = call(
        extend_kernel, token, [meta, tokens],
        [pl.BlockSpec(x.shape, lambda j: (0, 0)) for x in (meta, tokens)],
        [jax.ShapeDtypeStruct(shape, BF)], [pl.BlockSpec(shape, lambda j: (0, 0))], (1,), 0.1,
    )
    return out, token


def onward_kernel(below, *refs):
    above, down, up = refs[:3], refs[3], refs[4]
    down[...] = below[...]
    width = above[0].shape[1]
    for j in range(3):
        up[:, j * width : (j + 1) * width] = above[j][...]


def onward(token, from_down, from_up, block):
    rows = from_down.shape[0]
    shapes = [(rows, 4 * block), (rows, 3 * block)]
    return call(
        onward_kernel, token, [from_down] + [from_up] * 3,
        [pl.BlockSpec(shapes[0], lambda j: (0, 0))]
        + [
            pl.BlockSpec((rows, block), functools.partial(lambda n, j: (0, n), 4 + n))
            for n in range(3)
        ],
        [jax.ShapeDtypeStruct(sh, BF) for sh in shapes],
        [pl.BlockSpec(sh, lambda j: (0, 0)) for sh in shapes], (1,), 0.1,
    )


def prepare_kernel(scalars, saved, saved0, saved0_t, saved1, saved1_t):
    row = lax.broadcasted_iota(I32, (320, 1), 0)
    source = lax.broadcasted_iota(I32, (320, 1280), 1)
    for q in range(4):
        at = row + q * 320
        plane, line = at // 40, at % 40
        wanted = (line // CAP) * 320 + plane * CAP + line % CAP
        hit = (source == wanted).astype(F32).astype(BF)
        rows = dot(hit, saved[0])
        saved0[q * 320 : q * 320 + 320, :] = rows.astype(BF)
    saved0_t[0] = saved0[...].astype(F32).T.astype(BF)
    for k in range(4):
        at = pl.multiple_of(((scalars[0] + 4 - k) & 3) * 320, 320)
        rows = saved[1, pl.ds(at, 320), :]
        saved1[k * 320 : k * 320 + 320, :] = rows
        saved1_t[k] = rows.astype(F32).T.astype(BF)


def prepare(token, scalars, saved):
    _, rows, hidden = saved.shape
    shapes = [(rows, hidden), (1, hidden, rows), (rows, hidden), (4, hidden, rows // 4)]
    return call(
        prepare_kernel, token, [saved], [pl.BlockSpec(saved.shape, lambda j, s: (0, 0, 0))],
        [jax.ShapeDtypeStruct(sh, BF) for sh in shapes],
        [pl.BlockSpec(sh, functools.partial(lambda n, j, s: (0,) * n, len(sh))) for sh in shapes],
        (1,), 0.1, scalars=scalars,
    )


def picker_kernel(expert, where, sources, scalars, *refs):
    metas, outs = refs[:sources], refs[sources:]
    out, table = outs[0], outs[1] if len(outs) > 1 else None
    rows, count = out.shape[0], metas[0].shape[1]
    for s, ref in enumerate(metas):
        meta = ref[...].astype(F32)
        routes, places = positions(meta)
        total = jnp.zeros((rows, count), F32)
        wanted = lax.broadcasted_iota(I32, (rows, count), 0)
        for k in range(TOP):
            r = routes[k]
            row = where(scalars, s, r >> 6, (r >> 2) & 15, (r >> 1) & 1, places[k])
            row = jnp.where((r & 1) == expert, row, -1)
            total = total + jnp.where(wanted == row, meta[TOP + k : TOP + k + 1, :], 0.0)
            if table is not None and s == 0:
                table[k : k + 1, :] = r * CAP + places[k]
        out[:, s * count : (s + 1) * count] = total.astype(BF)


def picker(token, scalars, metas, specs, count, rows, expert, where, micros, table=False):
    shapes = [((rows, len(metas) * count), BF)] + [((TOP, count), I32)] * table
    return call(
        functools.partial(picker_kernel, expert, where, len(metas)),
        token, metas, specs,
        [jax.ShapeDtypeStruct(*sh) for sh in shapes],
        [pl.BlockSpec(sh[0], lambda j, s: (0, 0)) for sh in shapes],
        (1,), micros, scalars=scalars,
    )


def pick_kernel(sources, count, *refs):
    matrix, tokens, out = refs[0], refs[1 : 1 + sources], refs[-1]
    rows = matrix.shape[0]
    step = 320
    for at in range(0, rows, step):
        total = dot(matrix[at : at + step, :count], tokens[0][...])
        for s in range(1, sources):
            total = total + dot(
                matrix[at : at + step, s * count : (s + 1) * count], tokens[s][...]
            )
        out[at : at + step, :] = total.astype(BF)


def where_plane_first(scalars, s, dzl, dyx, dcore, place):
    core = scalars[2]
    source = core if s == 0 else 1 - core
    return jnp.where(dcore == core, dyx * 40 + dzl * 20 + source * CAP + place, -1)


def where_line_first(scalars, s, dzl, dyx, dcore, place):
    source = (scalars[0] + 4 - s) & 3
    return jnp.where(dzl == scalars[1], (dyx * 2 + dcore) * 40 + source * CAP + place, -1)


def pick(token, matrix, tokens, block, blocks, micros, after=()):
    rows, sources = matrix.shape[0], len(tokens)
    count = matrix.shape[1] // sources
    (out,), token = call(
        functools.partial(pick_kernel, sources, count),
        token, [matrix, *[t for t, _ in tokens]],
        [pl.BlockSpec(matrix.shape, lambda j: (0, 0))]
        + [
            pl.BlockSpec((count, block), functools.partial(lambda o, j: (0, j + o), o))
            for _, o in tokens
        ],
        [jax.ShapeDtypeStruct((rows, blocks * block), BF)],
        [pl.BlockSpec((rows, block), lambda j: (0, j))],
        (blocks,), micros, after=after,
    )
    return out, token


def part_kernel(scalars, got, own, away, picker):
    @pl.when(pl.program_id(0) == 0)
    def _():
        zl = scalars[1]
        for side, layer in ((0, zl), (1, 1 - zl)):
            row = lax.broadcasted_iota(I32, (320, 640), 0)
            source = lax.broadcasted_iota(I32, (320, 640), 1)
            group = row // 20
            hit = source == row + (group + layer) * 20
            picker[side * 320 : side * 320 + 320, :] = hit.astype(F32).astype(BF)

    away[...] = dot(picker[320:, :], got[...]).astype(BF)
    own[...] = dot(picker[:320, :], got[...]).astype(BF)


def part(token, scalars, got, block, first, blocks):
    shape = jax.ShapeDtypeStruct((320, blocks * block), BF)
    spec = pl.BlockSpec((320, block), lambda j, s: (0, j))
    return call(
        part_kernel, token, [got], [pl.BlockSpec((640, block), lambda j, s: (0, j + first))],
        [shape, shape], [spec, spec], (blocks,), 0.1, scratch=[pltpu.VMEM((640, 640), BF)],
        scalars=scalars,
    )


def back_kernel(pieces, has_before, *refs):
    rows, weight = refs[:pieces], refs[pieces]
    refs = refs[pieces + 1 :]
    before = refs[0] if has_before else None
    refs = refs[has_before:]
    size = rows[0].shape[0]
    if has_before:
        saved, hidden, terms, total = refs
    else:
        total = refs[0]

    @pl.when(pl.program_id(0) == 0)
    def _():
        total[...] = before[...] if has_before else jnp.zeros_like(total)

    step = 320
    for p in range(pieces):
        for at in range(0, size, step):
            total[p * size + at : p * size + at + step, :] += lax.dot_general(
                rows[p][at : at + step, :],
                weight[...],
                (((1,), (1,)), ((), ())),
                preferred_element_type=F32,
            )

    if has_before:

        @pl.when(pl.program_id(0) == pl.num_programs(0) - 1)
        def _():
            for at in range(0, pieces * size, step):
                back = total[at : at + step, :]
                hidden[at : at + step, :] = back.astype(BF)
                terms[at : at + step, :] = jnp.sum(
                    saved[at : at + step, :].astype(F32) * back, axis=1, keepdims=True
                )


def back(
    token, rows, weight, expert, block, first, blocks, before=None, saved=None, micros=0.1
):
    pieces, size = len(rows), rows[0].shape[0]
    hidden = weight.shape[1]
    shape = (pieces * size, hidden)
    whole = pl.BlockSpec(shape, lambda j: (0, 0))
    has_before = before is not None
    in_specs = [pl.BlockSpec((size, block), lambda j: (0, j))] * pieces + [
        pl.BlockSpec((None, hidden, block), lambda j: (expert, 0, j + first))
    ]
    args = [*rows, weight]
    if has_before:
        in_specs += [whole, whole]
        args += [before, saved]
        out_shape = [
            jax.ShapeDtypeStruct(shape, BF),
            jax.ShapeDtypeStruct((pieces * size, 1), F32),
        ]
        out_specs = [whole, pl.BlockSpec((pieces * size, 1), lambda j: (0, 0))]
        scratch = [pltpu.VMEM(shape, F32)]
    else:
        out_shape, out_specs, scratch = [jax.ShapeDtypeStruct(shape, F32)], [whole], []
    return call(
        functools.partial(back_kernel, pieces, has_before),
        token, args, in_specs, out_shape, out_specs, (blocks,), micros, scratch=scratch,
    )


def down_kernel(pieces, *refs):
    saved_t, rows, out = refs[0], refs[1 : 1 + pieces], refs[-1]
    total = dot(saved_t[0], rows[0][...])
    for p in range(1, pieces):
        total = total + dot(saved_t[p], rows[p][...])
    out[...] = total.astype(BF)


def down(token, result, saved_t, rows, expert, block, first, blocks):
    pieces, size = len(rows), rows[0].shape[0]
    hidden = saved_t.shape[1]
    in_specs = [pl.BlockSpec(saved_t.shape, lambda j: (0, 0, 0))] + [
        pl.BlockSpec((size, block), lambda j: (0, j))
    ] * pieces
    args = [saved_t, *rows]
    aliases = {}
    if result is not None:
        in_specs.append(pl.BlockSpec(memory_space=pl.ANY))
        args.append(result)
        aliases = {len(args) - 1: 0}
    (out,), token = call(
        functools.partial(down_kernel, pieces),
        token, args, in_specs,
        [jax.ShapeDtypeStruct((2, hidden, 7 * block), BF)],
        [pl.BlockSpec((None, hidden, block), lambda j: (expert, 0, j + first))],
        (blocks,), 0.1, aliases=aliases,
    )
    return out, token


def finish_kernel(scalars, hidden0, hidden1, out):
    for k in range(4):
        at = pl.multiple_of(((scalars[0] + 4 - k) & 3) * 320, 320)
        out[1, pl.ds(at, 320), :] = hidden1[k * 320 : k * 320 + 320, :]
    row = lax.broadcasted_iota(I32, (320, 1), 0)
    wanted = row + (row // CAP) * (3 * CAP)
    source = lax.broadcasted_iota(I32, (320, 1280), 1)
    for k in range(4):
        hit = (source == wanted + k * CAP).astype(F32).astype(BF)
        out[0, k * 320 : k * 320 + 320, :] = dot(hit, hidden0[...]).astype(BF)


def finish(token, scalars, hidden0, hidden1):
    shape = (2, *hidden0.shape)
    whole = pl.BlockSpec(hidden0.shape, lambda j, s: (0, 0))
    (out,), token = call(
        finish_kernel, token, [hidden0, hidden1], [whole, whole],
        [jax.ShapeDtypeStruct(shape, BF)], [pl.BlockSpec(shape, lambda j, s: (0, 0, 0))],
        (1,), 0.1, scalars=scalars,
    )
    return out


def shards(grad_out, gates, routes, w_down, saved_hidden):
    tokens, width = grad_out.shape
    zh, zl = lax.axis_index("zh"), lax.axis_index("zl")
    core = lax.axis_index("core")
    z = zh * 2 + zl
    scalars = jnp.stack([z, zl, core]).astype(I32)
    block = width // 7
    parts = ((0, 4), (4, 3))

    meta = jnp.concatenate([routes.T.astype(F32), gates.T.astype(F32)], axis=0)
    meta_other, other = core_swap(meta), core_swap(grad_out)
    token = jnp.zeros((8, 128), F32)
    extended, token = extend(token, meta, grad_out)
    from_down, from_up = z_shift(extended, 1), z_shift(extended, -1)
    meta_far = z_shift(meta, 2)
    (matrix1, table), token = picker(
        token, scalars, [meta, meta_other],
        [pl.BlockSpec(meta.shape, lambda j, s: (0, 0))] * 2,
        tokens, 640, 1, where_plane_first, 0.1, True,
    )
    send1, token = pick(token, matrix1, [(grad_out, 0), (other, 0)], block, 7, 0.1)
    got1 = lax.all_to_all(send1.reshape(16, 40, width), ("y", "x"), 0, 0, tiled=True)
    got1 = got1.reshape(640, width)

    (saved0, saved0_t, saved1, saved1_t), token = prepare(token, scalars, saved_hidden)
    (onward_down, onward_up), token = onward(token, from_down, from_up, block)
    far = (z_shift(onward_down, 1), z_shift(onward_up, -1))
    below = pl.BlockSpec((16, tokens), lambda j, s: (tokens // 16, 0))
    (matrix0,), token = picker(
        token, scalars, [extended, from_down, meta_far, from_up],
        [below, below, pl.BlockSpec(meta.shape, lambda j, s: (0, 0)), below],
        tokens, 1280, 0, where_line_first, 200,
    )

    def line(c):
        first, blocks = parts[c]
        return [(extended, first), (from_down, first), (far[c], 0), (from_up, first)]

    def exchange0(send):
        got = lax.all_to_all(send.reshape(32, 40, -1), PLANE, 0, 0, tiled=True)
        return [got.reshape(1280, -1)]

    send0, token = pick(token, matrix0, line(0), block, parts[0][1], 200, after=[far[1]])
    rows0 = [exchange0(send0)]
    rows1 = []
    for first, blocks in parts:
        (own, away), token = part(token, scalars, got1, block, first, blocks)
        rows1.append([own, z_shift(away, 1), z_shift(own, 2), z_shift(away, -1)])
    send0, token = pick(token, matrix0, line(1), block, parts[1][1], 0.1)
    rows0.append(exchange0(send0))

    (before0,), token = back(token, rows0[0], w_down, 0, block, *parts[0])
    d_down, token = down(token, None, saved0_t, rows0[0], 0, block, *parts[0])
    (before1,), token = back(token, rows1[0], w_down, 1, block, *parts[0])
    d_down, token = down(token, d_down, saved1_t, rows1[0], 1, block, *parts[0])
    (hidden1, terms1), token = back(
        token, rows1[1], w_down, 1, block, *parts[1], before1, saved1, 200
    )
    (hidden0, terms0), token = back(
        token, rows0[1], w_down, 0, block, *parts[1], before0, saved0
    )
    d_down, token = down(token, d_down, saved1_t, rows1[1], 1, block, *parts[1])
    d_down, token = down(token, d_down, saved0_t, rows0[1], 0, block, *parts[1])
    d_hidden = finish(token, scalars, hidden0, hidden1)

    def swapped(a, one, two):
        return a.reshape(one, two, CAP, -1).transpose(1, 0, 2, 3).reshape(one * two * CAP, -1)

    def turned(a):
        a = a.reshape(4, 320, -1)
        return jnp.concatenate(
            [lax.dynamic_index_in_dim(a, (z - k) % 4, 0, False) for k in range(4)], axis=0
        )

    terms = jnp.concatenate(
        [swapped(terms0, 32, 4).reshape(128, CAP), turned(terms1).reshape(128, CAP)], axis=1
    )
    returned = lax.all_to_all(terms, ALL, 0, 0, tiled=True)
    returned = (returned[:64] + returned[64:]).reshape(-1)

    table = table.reshape(1, -1)
    d_gates = jnp.sum(
        jnp.where(
            table == jnp.arange(EXPERTS * CAP, dtype=I32)[:, None], returned[:, None], 0.0
        ),
        axis=0,
    ).reshape(TOP, tokens).T
    return d_gates / gates.astype(F32), d_down, d_hidden


def solution(mesh):
    fine = Mesh(mesh.devices.reshape(2, 2, 4, 4, 2), ALL)
    in_specs = (
        P(ALL, None),
        P(ALL, None),
        P(ALL, None),
        P(("zl", "y", "x", "core"), "zh", None),
        P(("zl", "y", "x", "core"), None, "zh"),
    )
    out_specs = (P(ALL, None), in_specs[3], in_specs[4])
    return jax.shard_map(shards, mesh=fine, in_specs=in_specs, out_specs=out_specs, check_vma=False)
```

time: 362 us -> 279 us (0.77)
  waiting for transfers between devices: 150 us -> 80.4 us
  Pallas kernels: 97.5 us -> 126 us
  local copies, waits for them, and re-layouts: 31.1 us -> 6.29 us
  starting transfers between devices: 71.6 us -> 56.7 us
    ppermute x13 -> x11, waiting for transfers between devices: 121 us -> 48.9 us  [z_shift(): return lax.ppermute(value, Z, [(i, (i + step) % 4) for i in range(4)])]
    pallas_call x13 -> x19, Pallas kernels: 97.5 us -> 126 us  [call(): pl.pallas_call(run, out_shape=[*out_shape, jax.ShapeDtypeStruct((8, 128),...]
    all_to_all x1, starting transfers between devices: 31 us -> 6.73 us  [shards(): returned = lax.all_to_all(terms, ALL, 0, 0, tiled=True)]
    all_to_all x2, starting transfers between devices: 17.4 us -> 28 us  [exchange0(): got = lax.all_to_all(send.reshape(32, 40, -1), PLANE, 0, 0, tiled=True)]
    all_to_all x1, waiting for transfers between devices: 0.01 us -> 8.31 us  [shards(): lax.all_to_all(send1.reshape(16, 40, width), ('y', 'x'), 0, 0, tiled=True)]
    all_to_all x2, waiting for transfers between devices: 28.1 us -> 21.8 us  [exchange0(): got = lax.all_to_all(send.reshape(32, 40, -1), PLANE, 0, 0, tiled=True)]
    unnamed x31 -> x17, local copies, waits for them, and re-layouts: 9.9 us -> 4.12 us
    reshape x4 -> x1, local copies, waits for them, and re-layouts: 5.71 us -> 0.16 us  [swapped(): a.reshape(one, two, CAP, -1).transpose(1, 0, 2, 3)]
  transfers between devices with their start and end apart: 19 -> 17, of which waited for: 9 -> 8; matrix products, arithmetic and copies ran while one was open for 8% -> 1% of each run, Pallas kernels for 23% -> 42%
where the time goes in v3:
time: 279 us; the launch traced here: 277 us
  Pallas kernels  126 us (45%)
  waiting for transfers between devices  80.4 us (29%)
  starting transfers between devices  56.7 us (20%)
  other arithmetic  6.61 us (2%)
  local copies, waits for them, and re-layouts  6.29 us (2%)
    pallas_call x19, Pallas kernels, call(): pl.pallas_call(run, out_shape=[*out_shape, jax.ShapeDtypeStruct((8, 128),...  126 us
    ppermute x11, waiting for transfers between devices, z_shift(): return lax.ppermute(value, Z, [(i, (i + step) % 4) for i in range(4)])  48.9 us
    all_to_all x2, starting transfers between devices, exchange0(): got = lax.all_to_all(send.reshape(32, 40, -1), PLANE, 0, 0, tiled=True)  28 us
    all_to_all x2, waiting for transfers between devices, exchange0(): got = lax.all_to_all(send.reshape(32, 40, -1), PLANE, 0, 0, tiled=True)  21.8 us
    ppermute x11, starting transfers between devices, z_shift(): return lax.ppermute(value, Z, [(i, (i + step) % 4) for i in range(4)])  14.2 us
    all_to_all x1, waiting for transfers between devices, shards(): lax.all_to_all(send1.reshape(16, 40, width), ('y', 'x'), 0, 0, tiled=True)  8.31 us
    all_to_all x1, starting transfers between devices, shards(): lax.all_to_all(send1.reshape(16, 40, width), ('y', 'x'), 0, 0, tiled=True)  6.8 us
    all_to_all x1, starting transfers between devices, shards(): returned = lax.all_to_all(terms, ALL, 0, 0, tiled=True)  6.73 us
  transfers between devices with their start and end apart: 17, of which 8 were waited for; matrix products, arithmetic and copies ran while one was open for 1% of the time, Pallas kernels for 42%

profile of v3, /device:TPU:1, one launch (start us, length us, event | category | flops | bytes accessed | tf_op | source)
XLA Modules:
  0.0 277.2 jit_solution(11847873906978416100)
XLA Ops:
  19.5 8.1 %shard_map.78 = (bf16[640,3584]{1,0:T(8,128)(2,1)}, f32[8,128]{1,0:T(8,128)}) custom-call(bf16[640,512]{1,0:T(8,128)(2,1)} %get-tuple-element.52.refs_0_, bf16[256,3584]{1,0:T(8,128)(2,1)} %refs_1_.6, bf16[256,3584]{1,0:T(8,128)(2,1)} %collective-permute-done.4.refs_2_, f32[8,128]{1,0:T(8,128)} %get-tuple-element.53.refs_3_), custom_call_target="tpu_custom_call" | custom-call | flops 100000000 | tf_op jit(solution)/shard_map/pallas_call | solution.py:44
  27.6 6.8 %all-to-all-start = ((bf16[16,40,3584]{2,1,0:T(8,128)(2,1)}), bf16[16,40,3584]{2,1,0:T(8,128)(2,1)}, u32[]{:S(2)}, u32[]{:S(2)}) async-start(bf16[16,40,3584]{2,1,0:T(8,128)(2,1)} %bitcast.31), calls=%async_computation | async-start | bytes 9175040 | tf_op jit(solution)/shard_map/all_to_all | solution.py:386
  34.5 7.5 %shard_map.79 = (bf16[1280,512]{1,0:T(8,128)(2,1)}, bf16[1,512,1280]{2,1,0:T(8,128)(2,1)}, bf16[1280,512]{1,0:T(8,128)(2,1)}, bf16[4,512,320]{2,1,0:T(8,128)(2,1)}, f32[8,128]{1,0:T(8,128)}) custom-call(s32[3]{0:T(128)} %pad_add_fusion.refs_0_, bf16[2,1280,512]{2,1,0:T(8,128)(2,1)} %refs_1_.7, f32[8,128]{1,0:T(8,128)} %get-tuple-element.54.refs_2_), custom_call_target="tpu_custom_call" | custom-call | flops 100000000 | tf_op jit(solution)/shard_map/pallas_call | solution.py:44
  41.9 11.3 %collective-permute-done.1.refs_0_.refs_2_ = bf16[272,3584]{1,0:T(8,128)(2,1)} collective-permute-done((bf16[272,3584]{1,0:T(8,128)(2,1)}, bf16[272,3584]{1,0:T(8,128)(2,1)}, u32[]{:S(2)}, u32[]{:S(2)}) %collective-permute-start.1) | collective-permute-done | bytes 1949728 | tf_op jit(solution)/shard_map/ppermute | solution.py:22
  60.3 8.8 %shard_map.81 = (bf16[1280,1024]{1,0:T(8,128)(2,1)}, f32[8,128]{1,0:T(8,128)}) custom-call(s32[3]{0:T(128)} %pad_add_fusion.refs_0_, bf16[272,3584]{1,0:T(8,128)(2,1)} %get-tuple-element.51.refs_1_, bf16[272,3584]{1,0:T(8,128)(2,1)} %collective-permute-done.1.refs_0_.refs_2_, f32[8,256]{1,0:T(8,128)} %copy-done.6, bf16[272,3584]{1,0:T(8,128)(2,1)} %copy-done, ...), custom_call_target="tpu_custom_call" | custom-call | flops 199999995904 | tf_op jit(solution)/shard_map/pallas_call | solution.py:44
  69.1 7.4 %collective-permute-done.5.refs_6_.refs_3_ = bf16[272,1536]{1,0:T(8,128)(2,1)} collective-permute-done((bf16[272,1536]{1,0:T(8,128)(2,1)}, bf16[272,1536]{1,0:T(8,128)(2,1)}, u32[]{:S(2)}, u32[]{:S(2)}) %collective-permute-start.5) | collective-permute-done | bytes 835616 | tf_op jit(solution)/shard_map/ppermute | solution.py:22
  76.4 9.0 %collective-permute-done.6.refs_3_ = bf16[272,2048]{1,0:T(8,128)(2,1)} collective-permute-done((bf16[272,2048]{1,0:T(8,128)(2,1)}, bf16[272,2048]{1,0:T(8,128)(2,1)}, u32[]{:S(2)}, u32[]{:S(2)}) %collective-permute-start.6) | collective-permute-done | bytes 1114144 | tf_op jit(solution)/shard_map/ppermute | solution.py:22
  85.5 9.5 %shard_map.82 = (bf16[1280,2048]{1,0:T(8,128)(2,1)}, f32[8,128]{1,0:T(8,128)}) custom-call(bf16[1280,1024]{1,0:T(8,128)(2,1)} %get-tuple-element.57.refs_0_, bf16[272,3584]{1,0:T(8,128)(2,1)} %get-tuple-element.51.refs_1_, bf16[272,3584]{1,0:T(8,128)(2,1)} %collective-permute-done.1.refs_0_.refs_2_, bf16[272,2048]{1,0:T(8,128)(2,1)} %collective-permute-done.6.refs_3_, ...), custom_call_target="tpu_custom_call" | custom-call | flops 199999995904 | tf_op jit(solution)/shard_map/pallas_call | solution.py:44
  95.0 8.3 %all-to-all-done = bf16[16,40,3584]{2,1,0:T(8,128)(2,1)} async-done(((bf16[16,40,3584]{2,1,0:T(8,128)(2,1)}), bf16[16,40,3584]{2,1,0:T(8,128)(2,1)}, u32[]{:S(2)}, u32[]{:S(2)}) %all-to-all-start) | async-done | bytes 4587552 | tf_op jit(solution)/shard_map/all_to_all | solution.py:386
  103.3 6.4 %all-to-all-start.2 = ((bf16[32,40,2048]{2,1,0:T(8,128)(2,1)}), bf16[32,40,2048]{2,1,0:T(8,128)(2,1)}, u32[]{:S(2)}, u32[]{:S(2)}) async-start(bf16[32,40,2048]{2,1,0:T(8,128)(2,1)} %bitcast.30), calls=%async_computation.2 | async-start | bytes 10485760 | tf_op jit(solution)/shard_map/all_to_all | solution.py:404
  109.8 6.1 %shard_map.83 = (bf16[320,2048]{1,0:T(8,128)(2,1)}, bf16[320,2048]{1,0:T(8,128)(2,1)}, f32[8,128]{1,0:T(8,128)}) custom-call(s32[3]{0:T(128)} %pad_add_fusion.refs_0_, bf16[640,3584]{1,0:T(8,128)(2,1)} %bitcast.6.refs_1_, f32[8,128]{1,0:T(8,128)} %get-tuple-element.62.refs_2_), custom_call_target="tpu_custom_call" | custom-call | flops 100000000 | tf_op jit(solution)/shard_map/pallas_call | solution.py:44
  126.2 21.2 %collective-permute-done.10.refs_1_.refs_2_ = bf16[320,2048]{1,0:T(8,128)(2,1)S(1)} collective-permute-done((bf16[320,2048]{1,0:T(8,128)(2,1)}, bf16[320,2048]{1,0:T(8,128)(2,1)S(1)}, u32[]{:S(2)}, u32[]{:S(2)}) %collective-permute-start.10) | collective-permute-done | bytes 1310752 | tf_op jit(solution)/shard_map/ppermute | solution.py:22
  148.6 8.1 %shard_map.85 = (bf16[1280,1536]{1,0:T(8,128)(2,1)}, f32[8,128]{1,0:T(8,128)}) custom-call(bf16[1280,1024]{1,0:T(8,128)(2,1)} %get-tuple-element.57.refs_0_, bf16[272,3584]{1,0:T(8,128)(2,1)} %get-tuple-element.51.refs_1_, bf16[272,3584]{1,0:T(8,128)(2,1)} %collective-permute-done.1.refs_0_.refs_2_, ...), custom_call_target="tpu_custom_call" | custom-call | flops 100000000 | tf_op jit(solution)/shard_map/pallas_call | solution.py:44
  156.6 14.6 %all-to-all-done.2 = bf16[32,40,2048]{2,1,0:T(8,128)(2,1)} async-done(((bf16[32,40,2048]{2,1,0:T(8,128)(2,1)}), bf16[32,40,2048]{2,1,0:T(8,128)(2,1)}, u32[]{:S(2)}, u32[]{:S(2)}) %all-to-all-start.2) | async-done | bytes 5242912 | tf_op jit(solution)/shard_map/all_to_all | solution.py:404
  171.3 21.6 %all-to-all-start.1 = ((bf16[32,40,1536]{2,1,0:T(8,128)(2,1)}), bf16[32,40,1536]{2,1,0:T(8,128)(2,1)}, u32[]{:S(2)}, u32[]{:S(2)}) async-start(bf16[32,40,1536]{2,1,0:T(8,128)(2,1)} %bitcast.32), calls=%async_computation.1 | async-start | bytes 7864320 | tf_op jit(solution)/shard_map/all_to_all | solution.py:404
  192.8 7.4 %shard_map.86 = (f32[1280,512]{1,0:T(8,128)}, f32[8,128]{1,0:T(8,128)}) custom-call(bf16[1280,2048]{1,0:T(8,128)(2,1)} %bitcast.10.refs_0_.refs_1_, bf16[2,512,3584]{2,1,0:T(8,128)(2,1)} %refs_1_.9, f32[8,128]{1,0:T(8,128)} %get-tuple-element.67.refs_2_), custom_call_target="tpu_custom_call" | custom-call | flops 100000000 | tf_op jit(solution)/shard_map/pallas_call | solution.py:44
  200.2 6.7 %shard_map.87 = (bf16[2,512,3584]{2,1,0:T(8,128)(2,1)}, f32[8,128]{1,0:T(8,128)}) custom-call(bf16[1,512,1280]{2,1,0:T(8,128)(2,1)} %get-tuple-element.74.refs_0_, bf16[1280,2048]{1,0:T(8,128)(2,1)} %bitcast.10.refs_0_.refs_1_, f32[8,128]{1,0:T(8,128)} %get-tuple-element.75.refs_2_), custom_call_target="tpu_custom_call" | custom-call | flops 100000000 | tf_op jit(solution)/shard_map/pallas_call | solution.py:44
  208.0 7.4 %shard_map.88 = (f32[1280,512]{1,0:T(8,128)}, f32[8,128]{1,0:T(8,128)}) custom-call(bf16[320,2048]{1,0:T(8,128)(2,1)} %get-tuple-element.72.refs_0_.refs_1_, bf16[320,2048]{1,0:T(8,128)(2,1)} %copy-done.1, bf16[320,2048]{1,0:T(8,128)(2,1)} %copy-done.2, bf16[320,2048]{1,0:T(8,128)(2,1)} %collective-permute-done.12.refs_3_.refs_4_, ...), custom_call_target="tpu_custom_call" | custom-call | flops 100000000 | tf_op jit(solution)/shard_map/pallas_call | solution.py:44
  215.4 8.0 %shard_map.89 = (bf16[2,512,3584]{2,1,0:T(8,128)(2,1)}, f32[8,128]{1,0:T(8,128)}) custom-call(bf16[4,512,320]{2,1,0:T(8,128)(2,1)} %get-tuple-element.79.refs_0_, bf16[320,2048]{1,0:T(8,128)(2,1)} %get-tuple-element.72.refs_0_.refs_1_, bf16[320,2048]{1,0:T(8,128)(2,1)} %copy-done.1, bf16[320,2048]{1,0:T(8,128)(2,1)} %copy-done.2, ...), custom_call_target="tpu_custom_call", output_to_operand_aliasing={{0}: (5, {})} | custom-call | flops 100000000 | tf_op jit(solution)/shard_map/pallas_call | solution.py:44
  223.4 8.0 %shard_map.90 = (bf16[1280,512]{1,0:T(8,128)(2,1)}, f32[1280,1]{1,0:T(8,128)}, f32[8,128]{1,0:T(8,128)}) custom-call(bf16[320,1536]{1,0:T(8,128)(2,1)} %get-tuple-element.70.refs_0_.refs_1_, bf16[320,1536]{1,0:T(8,128)(2,1)} %collective-permute-done.7.refs_1_.refs_2_, bf16[320,1536]{1,0:T(8,128)(2,1)} %collective-permute-done.8.refs_2_.refs_3_, ...), custom_call_target="tpu_custom_call" | custom-call | flops 199999995904 | tf_op jit(solution)/shard_map/pallas_call | solution.py:44
  233.2 7.2 %all-to-all-done.1 = bf16[32,40,1536]{2,1,0:T(8,128)(2,1)} async-done(((bf16[32,40,1536]{2,1,0:T(8,128)(2,1)}), bf16[32,40,1536]{2,1,0:T(8,128)(2,1)}, u32[]{:S(2)}, u32[]{:S(2)}) %all-to-all-start.1) | async-done | bytes 3932192 | tf_op jit(solution)/shard_map/all_to_all | solution.py:404
  240.4 7.7 %shard_map.91 = (bf16[1280,512]{1,0:T(8,128)(2,1)}, f32[1280,1]{1,0:T(8,128)}, f32[8,128]{1,0:T(8,128)}) custom-call(bf16[1280,1536]{1,0:T(8,128)(2,1)} %bitcast.8.refs_0_.refs_1_, bf16[2,512,3584]{2,1,0:T(8,128)(2,1)} %refs_1_.9, f32[1280,512]{1,0:T(8,128)} %get-tuple-element.68.refs_2_, bf16[1280,512]{1,0:T(8,128)(2,1)} %get-tuple-element.69.refs_3_, ...), custom_call_target="tpu_custom_call" | custom-call | flops 100000000 | tf_op jit(solution)/shard_map/pallas_call | solution.py:44
  250.6 6.7 %all-to-all-start.3 = ((f32[128,1,20]{2,1,0:T(1,128)}), f32[128,1,20]{2,1,0:T(1,128)S(1)}, u32[]{:S(2)}, u32[]{:S(2)}) async-start(f32[128,1,20]{2,1,0:T(1,128)} %copy.19), calls=%async_computation.3 | async-start | bytes 131072 | tf_op jit(solution)/shard_map/all_to_all | solution.py:442
  257.3 6.7 %shard_map.92 = (bf16[2,512,3584]{2,1,0:T(8,128)(2,1)}, f32[8,128]{1,0:T(8,128)}) custom-call(bf16[4,512,320]{2,1,0:T(8,128)(2,1)} %get-tuple-element.79.refs_0_, bf16[320,1536]{1,0:T(8,128)(2,1)} %get-tuple-element.70.refs_0_.refs_1_, bf16[320,1536]{1,0:T(8,128)(2,1)} %collective-permute-done.7.refs_1_.refs_2_, ...), custom_call_target="tpu_custom_call", output_to_operand_aliasing={{0}: (5, {})} | custom-call | flops 100000000 | tf_op jit(solution)/shard_map/pallas_call | solution.py:44
  (69 shorter events, 55.8 us)
Async XLA Ops:
  6.1 47.1 %collective-permute-start.1 = (bf16[272,3584]{1,0:T(8,128)(2,1)}, bf16[272,3584]{1,0:T(8,128)(2,1)}, u32[]{:S(2)}, u32[]{:S(2)}) collective-permute-start(bf16[272,3584]{1,0:T(8,128)(2,1)} %get-tuple-element.51.refs_1_), channel_id=1, source_target_pairs={{0,32},{32,64},{64,96},{96,0},{1,33},{33,65},{65,97},{97,1},{2,34}... | collective-permute-start | bytes 5849096 | tf_op jit(solution)/shard_map/ppermute | solution.py:22
  8.6 44.6 %collective-permute-start.3 = (bf16[272,3584]{1,0:T(8,128)(2,1)}, bf16[272,3584]{1,0:T(8,128)(2,1)S(1)}, u32[]{:S(2)}, u32[]{:S(2)}) collective-permute-start(bf16[272,3584]{1,0:T(8,128)(2,1)} %get-tuple-element.51.refs_1_), channel_id=1, source_target_pairs={{0,96},{32,0},{64,32},{96,64},{1,97},{33,1},{65,33},{97,65},{2,98}... | collective-permute-start | bytes 5849096 | tf_op jit(solution)/shard_map/ppermute | solution.py:22
  10.7 8.8 %collective-permute-start.4 = (bf16[256,3584]{1,0:T(8,128)(2,1)}, bf16[256,3584]{1,0:T(8,128)(2,1)}, u32[]{:S(2)}, u32[]{:S(2)}) collective-permute-start(bf16[256,3584]{1,0:T(8,128)(2,1)} %refs_1_.6), channel_id=1, source_target_pairs={{0,1},{1,0},{2,3},{3,2},{4,5},{5,4},{6,7},{7,6},{8,9},{9,8},{10,11... | collective-permute-start | bytes 5505032 | tf_op jit(solution)/shard_map/ppermute | solution.py:26
  11.7 3.5 %collective-permute-start = (f32[8,256]{1,0:T(8,128)}, f32[8,256]{1,0:T(8,128)S(1)}, u32[]{:S(2)}, u32[]{:S(2)}) collective-permute-start(f32[8,256]{1,0:T(8,128)} %pad_maximum_fusion.refs_0_.refs_1_), channel_id=1, source_target_pairs={{0,1},{1,0},{2,3},{3,2},{4,5},{5,4},{6,7},{7,6},{8,9},{9,8},{10,11... | collective-permute-start | bytes 24584 | tf_op jit(solution)/shard_map/ppermute | solution.py:26
  11.7 48.0 %collective-permute-start.2 = (f32[8,256]{1,0:T(8,128)}, f32[8,256]{1,0:T(8,128)S(1)}, u32[]{:S(2)}, u32[]{:S(2)}) collective-permute-start(f32[8,256]{1,0:T(8,128)} %pad_maximum_fusion.refs_0_.refs_1_), channel_id=1, source_target_pairs={{0,64},{32,96},{64,0},{96,32},{1,65},{33,97},{65,1},{97,33},{2,66}... | collective-permute-start | bytes 24584 | tf_op jit(solution)/shard_map/ppermute | solution.py:22
  15.2 0.6 copy-start.7
  27.6 75.7 %all-to-all-start = ((bf16[16,40,3584]{2,1,0:T(8,128)(2,1)}), bf16[16,40,3584]{2,1,0:T(8,128)(2,1)}, u32[]{:S(2)}, u32[]{:S(2)}) async-start(bf16[16,40,3584]{2,1,0:T(8,128)(2,1)} %bitcast.31), calls=%async_computation | async-start | bytes 9175040 | tf_op jit(solution)/shard_map/all_to_all | solution.py:386
  53.2 1.3 copy-start
  57.3 19.2 %collective-permute-start.5 = (bf16[272,1536]{1,0:T(8,128)(2,1)}, bf16[272,1536]{1,0:T(8,128)(2,1)}, u32[]{:S(2)}, u32[]{:S(2)}) collective-permute-start(bf16[272,1536]{1,0:T(8,128)(2,1)} %get-tuple-element.58), channel_id=1, source_target_pairs={{0,96},{32,0},{64,32},{96,64},{1,97},{33,1},{65,33},{97,65},{2,98}... | collective-permute-start | bytes 2506760 | tf_op jit(solution)/shard_map/ppermute | solution.py:22
  59.7 25.8 %collective-permute-start.6 = (bf16[272,2048]{1,0:T(8,128)(2,1)}, bf16[272,2048]{1,0:T(8,128)(2,1)}, u32[]{:S(2)}, u32[]{:S(2)}) collective-permute-start(bf16[272,2048]{1,0:T(8,128)(2,1)} %get-tuple-element.60), channel_id=1, source_target_pairs={{0,32},{32,64},{64,96},{96,0},{1,33},{33,65},{65,97},{97,1},{2,34}... | collective-permute-start | bytes 3342344 | tf_op jit(solution)/shard_map/ppermute | solution.py:22
  103.3 67.9 %all-to-all-start.2 = ((bf16[32,40,2048]{2,1,0:T(8,128)(2,1)}), bf16[32,40,2048]{2,1,0:T(8,128)(2,1)}, u32[]{:S(2)}, u32[]{:S(2)}) async-start(bf16[32,40,2048]{2,1,0:T(8,128)(2,1)} %bitcast.30), calls=%async_computation.2 | async-start | bytes 10485760 | tf_op jit(solution)/shard_map/all_to_all | solution.py:404
  115.8 32.1 %copy-start.5 = (s32[4,256]{1,0:T(4,128)S(1)}, s32[4,256]{1,0:T(4,128)}, u32[]{:S(2)}) copy-start(s32[4,256]{1,0:T(4,128)} %get-tuple-element.50) | copy-start | bytes 12292
  115.8 31.6 %collective-permute-start.10 = (bf16[320,2048]{1,0:T(8,128)(2,1)}, bf16[320,2048]{1,0:T(8,128)(2,1)S(1)}, u32[]{:S(2)}, u32[]{:S(2)}) collective-permute-start(bf16[320,2048]{1,0:T(8,128)(2,1)} %get-tuple-element.73), channel_id=1, source_target_pairs={{0,32},{32,64},{64,96},{96,0},{1,33},{33,65},{65,97},{97,1},{2,34}... | collective-permute-start | bytes 3932168 | tf_op jit(solution)/shard_map/ppermute | solution.py:22
  115.8 91.0 %collective-permute-start.11 = (bf16[320,2048]{1,0:T(8,128)(2,1)}, bf16[320,2048]{1,0:T(8,128)(2,1)S(1)}, u32[]{:S(2)}, u32[]{:S(2)}) collective-permute-start(bf16[320,2048]{1,0:T(8,128)(2,1)} %get-tuple-element.72.refs_0_.refs_1_), channel_id=1, source_target_pairs={{0,64},{32,96},{64,0},{96,32},{1,65},{33,97},{65,1},{97,33},{2,66}... | collective-permute-start | bytes 3932168 | tf_op jit(solution)/shard_map/ppermute | solution.py:22
  118.8 88.1 %collective-permute-start.12 = (bf16[320,2048]{1,0:T(8,128)(2,1)}, bf16[320,2048]{1,0:T(8,128)(2,1)}, u32[]{:S(2)}, u32[]{:S(2)}) collective-permute-start(bf16[320,2048]{1,0:T(8,128)(2,1)} %get-tuple-element.73), channel_id=1, source_target_pairs={{0,96},{32,0},{64,32},{96,64},{1,97},{33,1},{65,33},{97,65},{2,98}... | collective-permute-start | bytes 3932168 | tf_op jit(solution)/shard_map/ppermute | solution.py:22
  124.8 98.6 %collective-permute-start.7 = (bf16[320,1536]{1,0:T(8,128)(2,1)}, bf16[320,1536]{1,0:T(8,128)(2,1)}, u32[]{:S(2)}, u32[]{:S(2)}) collective-permute-start(bf16[320,1536]{1,0:T(8,128)(2,1)} %get-tuple-element.71), channel_id=1, source_target_pairs={{0,32},{32,64},{64,96},{96,0},{1,33},{33,65},{65,97},{97,1},{2,34}... | collective-permute-start | bytes 2949128 | tf_op jit(solution)/shard_map/ppermute | solution.py:22
  125.5 97.9 %collective-permute-start.8 = (bf16[320,1536]{1,0:T(8,128)(2,1)}, bf16[320,1536]{1,0:T(8,128)(2,1)}, u32[]{:S(2)}, u32[]{:S(2)}) collective-permute-start(bf16[320,1536]{1,0:T(8,128)(2,1)} %get-tuple-element.70.refs_0_.refs_1_), channel_id=1, source_target_pairs={{0,64},{32,96},{64,0},{96,32},{1,65},{33,97},{65,1},{97,33},{2,66}... | collective-permute-start | bytes 2949128 | tf_op jit(solution)/shard_map/ppermute | solution.py:22
  147.4 9.2 %copy-start.1 = (bf16[320,2048]{1,0:T(8,128)(2,1)}, bf16[320,2048]{1,0:T(8,128)(2,1)S(1)}, u32[]{:S(2)}) copy-start(bf16[320,2048]{1,0:T(8,128)(2,1)S(1)} %collective-permute-done.10.refs_1_.refs_2_) | copy-start | bytes 3932164
  147.4 76.0 %collective-permute-start.9 = (bf16[320,1536]{1,0:T(8,128)(2,1)}, bf16[320,1536]{1,0:T(8,128)(2,1)}, u32[]{:S(2)}, u32[]{:S(2)}) collective-permute-start(bf16[320,1536]{1,0:T(8,128)(2,1)} %get-tuple-element.71), channel_id=1, source_target_pairs={{0,96},{32,0},{64,32},{96,64},{1,97},{33,1},{65,33},{97,65},{2,98}... | collective-permute-start | bytes 2949128 | tf_op jit(solution)/shard_map/ppermute | solution.py:22
  171.3 69.1 %all-to-all-start.1 = ((bf16[32,40,1536]{2,1,0:T(8,128)(2,1)}), bf16[32,40,1536]{2,1,0:T(8,128)(2,1)}, u32[]{:S(2)}, u32[]{:S(2)}) async-start(bf16[32,40,1536]{2,1,0:T(8,128)(2,1)} %bitcast.32), calls=%async_computation.1 | async-start | bytes 7864320 | tf_op jit(solution)/shard_map/all_to_all | solution.py:404
  206.9 1.1 copy-start.2
  250.6 25.1 %all-to-all-start.3 = ((f32[128,1,20]{2,1,0:T(1,128)}), f32[128,1,20]{2,1,0:T(1,128)S(1)}, u32[]{:S(2)}, u32[]{:S(2)}) async-start(f32[128,1,20]{2,1,0:T(1,128)} %copy.19), calls=%async_computation.3 | async-start | bytes 131072 | tf_op jit(solution)/shard_map/all_to_all | solution.py:442
  269.8 6.1 %copy-start.3 = (s32[1,2,4,128]{3,1,2,0:T(2,128)S(1)}, s32[1,2,4,128]{3,1,2,0:T(2,128)}, u32[]{:S(2)}) copy-start(s32[1,2,4,128]{3,1,2,0:T(2,128)} %copy.20) | copy-start | bytes 12292
  269.8 6.8 %copy-start.4 = (bf16[256,4]{0,1:T(4,128)(2,1)S(1)}, bf16[256,4]{0,1:T(4,128)(2,1)}, u32[]{:S(2)}) copy-start(bf16[256,4]{0,1:T(4,128)(2,1)} %param.6) | copy-start | bytes 6148
  (1 other events, 0.6 us)

commit v4 on v0

v4 whole, which is shorter than its diff:
```python
import functools

import jax
import jax.numpy as jnp
from jax import lax
from jax.experimental import pallas as pl
from jax.experimental.pallas import tpu as pltpu
from jax.sharding import Mesh, PartitionSpec as P

Z = ("zh", "zl")
PLANE = ("y", "x", "core")
ALL = ("zh", "zl", "y", "x", "core")
CAP = 10
TOP = 4
STEPS = (0, 1, 3, 2)
EXPERTS = 128
BF = jnp.bfloat16
F32 = jnp.float32
I32 = jnp.int32


def z_shift(value, step):
    return lax.ppermute(value, Z, [(i, (i + step) % 4) for i in range(4)])


def core_swap(value):
    return lax.ppermute(value, "core", [(0, 1), (1, 0)])


def dot(a, b):
    return jnp.dot(a, b, preferred_element_type=F32)


def call(body, token, args, in_specs, out_shape, out_specs, grid, micros, scratch=(), aliases=None,
         scalars=None, after=()):
    lead = 0 if scalars is None else 1
    extra = [*([] if token is None else [token]), *after]
    n_in, n_out = lead + len(args), len(out_shape)

    def run(*refs):
        outs = refs[n_in + len(extra) :]
        outs[n_out][...] = jnp.zeros((8, 128), F32)
        body(*refs[:n_in], *outs[:n_out], *outs[n_out + 1 :])

    result = pl.pallas_call(
        run,
        out_shape=[*out_shape, jax.ShapeDtypeStruct((8, 128), F32)],
        grid_spec=pltpu.PrefetchScalarGridSpec(
            num_scalar_prefetch=lead,
            grid=grid,
            in_specs=[*in_specs, *[pl.BlockSpec(memory_space=pl.ANY)] * len(extra)],
            out_specs=[*out_specs, pl.BlockSpec((8, 128), lambda j, *_: (0, 0))],
            scratch_shapes=list(scratch),
        ),
        input_output_aliases=aliases or {},
        compiler_params=pltpu.CompilerParams(vmem_limit_bytes=60 * 1024 * 1024),
        cost_estimate=pl.CostEstimate(
            flops=int(micros * 1e9), bytes_accessed=0, transcendentals=0
        ),
    )(*([] if scalars is None else [scalars]), *args, *extra)
    return result[:-1], result[-1]


def positions(meta):
    tokens = meta.shape[1]
    names = lax.broadcasted_iota(I32, (EXPERTS, tokens), 0)
    routes = [meta[k : k + 1, :].astype(I32) for k in range(TOP)]
    hits = [names == r for r in routes]
    named = sum(h.astype(F32) for h in hits)
    first = lax.broadcasted_iota(I32, (tokens, tokens), 0)
    second = lax.broadcasted_iota(I32, (tokens, tokens), 1)
    earlier = dot(named.astype(BF), (first < second).astype(F32).astype(BF))
    places = [
        jnp.sum(jnp.where(h, earlier, 0.0), axis=0, keepdims=True).astype(I32) for h in hits
    ]
    return routes, places


def onward_kernel(below, above, meta, down, up, meta_out):
    cut = down.shape[1]
    down[...] = below[:, :cut]
    up[...] = above[:, cut:]
    meta_out[...] = meta[...]


def onward(token, from_down, from_up, meta, cut):
    rows, width = from_down.shape
    shapes = [((rows, cut), BF), ((rows, width - cut), BF), (meta.shape, F32)]
    return call(
        onward_kernel, token, [from_down, from_up, meta],
        [
            pl.BlockSpec((rows, cut), lambda j: (0, 0)),
            pl.BlockSpec((rows, width), lambda j: (0, 0)),
            pl.BlockSpec(meta.shape, lambda j: (0, 0)),
        ],
        [jax.ShapeDtypeStruct(*sh) for sh in shapes],
        [pl.BlockSpec(sh[0], lambda j: (0, 0)) for sh in shapes], (1,), 1000,
    )


def prepare_kernel(scalars, saved, saved0, saved0_t, near, near_t, distant, distant_t):
    row = lax.broadcasted_iota(I32, (320, 1), 0)
    source = lax.broadcasted_iota(I32, (320, 1280), 1)
    for q in range(4):
        at = row + q * 320
        plane, line = at // 40, at % 40
        z = jnp.where(line < 32, line // 8, (line - 32) // 2)
        place = jnp.where(line < 32, line % 8, 8 + line % 2)
        hit = (source == z * 320 + plane * CAP + place).astype(F32).astype(BF)
        rows = dot(hit, saved[0])
        saved0[q * 320 : q * 320 + 320, :] = rows.astype(BF)
    saved0_t[...] = saved0[...].astype(F32).T.astype(BF)
    for at, step in enumerate(STEPS):
        begin = pl.multiple_of(((scalars[0] + 4 - step) & 3) * 320, 320)
        rows = saved[1, pl.ds(begin, 320), :]
        if at < 3:
            near[at * 320 : at * 320 + 320, :] = rows
        else:
            distant[...] = rows
    near_t[...] = near[...].astype(F32).T.astype(BF)
    distant_t[...] = distant[...].astype(F32).T.astype(BF)


def prepare(token, scalars, saved):
    _, rows, hidden = saved.shape
    shapes = [(n, hidden)[::turn] for n in (rows, rows * 3 // 4, rows // 4) for turn in (1, -1)]
    return call(
        prepare_kernel, token, [saved], [pl.BlockSpec(saved.shape, lambda j, s: (0, 0, 0))],
        [jax.ShapeDtypeStruct(sh, BF) for sh in shapes],
        [pl.BlockSpec(sh, lambda j, s: (0, 0)) for sh in shapes],
        (1,), 0.1, scalars=scalars,
    )


def picked(meta, rows_of, rows):
    routes, places = positions(meta)
    total = jnp.zeros((rows, meta.shape[1]), F32)
    wanted = lax.broadcasted_iota(I32, total.shape, 0)
    for k in range(TOP):
        row = rows_of(routes[k], places[k])
        total = total + jnp.where(wanted == row, meta[TOP + k : TOP + k + 1, :], 0.0)
    return total.astype(BF), routes, places


def first_picker_kernel(scalars, routes, gates, routes_other, gates_other, out, table, meta):
    core = scalars[2]
    count = meta.shape[1]
    for s, pair in enumerate(((routes, gates), (routes_other, gates_other))):
        both = jnp.concatenate([x[...].astype(F32) for x in pair], axis=0)
        source = core if s == 0 else 1 - core

        def rows_of(r, place):
            row = ((r >> 2) & 15) * 40 + (r >> 6) * 20 + source * CAP + place
            return jnp.where((r & 3) == 2 * core + 1, row, -1)

        matrix, named, places = picked(both, rows_of, out.shape[0])
        out[:, s * count : (s + 1) * count] = matrix
        if s == 0:
            meta[...] = both
            for k in range(TOP):
                r = named[k]
                device = ((r >> 1) & 31) * 4 + (r >> 6) * 2
                table[k : k + 1, :] = (device + (r & 1)) * CAP + places[k]


def first_picker(scalars, *args):
    count = args[0].shape[1]
    shapes = [((640, 2 * count), BF), ((TOP, count), I32), ((2 * TOP, count), F32)]
    return call(
        first_picker_kernel, None, args, [pl.BlockSpec(x.shape, lambda j, s: (0, 0)) for x in args],
        [jax.ShapeDtypeStruct(*sh) for sh in shapes],
        [pl.BlockSpec(sh[0], lambda j, s: (0, 0)) for sh in shapes], (1,), 0.1, scalars=scalars,
    )


def line_picker_kernel(scalars, *refs):
    metas, (first, last) = refs[:4], refs[4:]
    count = metas[0].shape[1]
    for s in range(4):
        source = (scalars[0] + 4 - s) & 3

        def rows_of(r, place, low, high, at):
            mine = ((r >> 6) == scalars[1]) & ((r & 1) == 0) & (place >= low) & (place < high)
            return jnp.where(mine, ((r >> 1) & 31) * 8 + at + place - low, -1)

        meta = metas[s][...]
        routes, places = positions(meta)
        wanted = lax.broadcasted_iota(I32, (256, count), 0)
        for out, low, high, at in ((first, 0, 8, 0), (last, 8, CAP, source * 2)):
            total = jnp.zeros((256, count), F32)
            for k in range(TOP):
                row = rows_of(routes[k], places[k], low, high, at)
                total = total + jnp.where(wanted == row, meta[TOP + k : TOP + k + 1, :], 0.0)
            out[:, s * count : (s + 1) * count] = total.astype(BF)


def line_picker(token, scalars, metas):
    count = metas[0].shape[1]
    shape = (256, 4 * count)
    return call(
        line_picker_kernel, token, metas,
        [pl.BlockSpec(x.shape, lambda j, s: (0, 0)) for x in metas],
        [jax.ShapeDtypeStruct(shape, BF)] * 2, [pl.BlockSpec(shape, lambda j, s: (0, 0))] * 2,
        (1,), 0.1, scalars=scalars,
    )


def pick_kernel(matrix, one, two, out):
    lines = jnp.concatenate([one[...], two[...]], axis=0)
    out[...] = dot(matrix[...], lines).astype(BF)


def pick(token, matrix, tokens, block):
    (count, width), rows = tokens[0].shape, matrix.shape[0]
    (out,), token = call(
        pick_kernel, token, [matrix, *tokens],
        [pl.BlockSpec(matrix.shape, lambda j: (0, 0))]
        + [pl.BlockSpec((count, block), lambda j: (0, j))] * 2,
        [jax.ShapeDtypeStruct((rows, width), BF)],
        [pl.BlockSpec((rows, block), lambda j: (0, j))], (width // block,), 0.1,
    )
    return out, token


def line_pick_kernel(scalars, first, last, here, down, far_left, far_right, up, out):
    count = here.shape[0]
    left = pl.program_id(0) < pl.num_programs(0) // 2
    far = jnp.where(left, far_left[...], far_right[...])
    tokens = [here[...], down[...], far, up[...]]

    def grouped(rows):
        return rows.reshape(32, 8, rows.shape[1]).astype(BF)

    for s in range(4):
        source = (scalars[0] + 4 - s) & 3
        out[:, source] = grouped(dot(first[:, s * count : (s + 1) * count], tokens[s]))
    out[:, 4] = grouped(dot(last[...], jnp.concatenate(tokens, axis=0)))


def line_pick(token, scalars, matrices, here, down, far, up, block):
    count, width = here.shape
    half = width // block // 2
    every = pl.BlockSpec((count, block), lambda j, s: (0, j))
    (out,), token = call(
        line_pick_kernel, token, [*matrices, here, down, *far, up],
        [pl.BlockSpec(m.shape, lambda j, s: (0, 0)) for m in matrices]
        + [
            every, every,
            pl.BlockSpec((count, block), lambda j, s: (0, jnp.minimum(j, half - 1))),
            pl.BlockSpec((count, block), lambda j, s: (0, jnp.maximum(j - half, 0))),
            every,
        ],
        [jax.ShapeDtypeStruct((32, 5, 8, width), BF)],
        [pl.BlockSpec((32, 5, 8, block), lambda j, s: (0, 0, 0, j))],
        (2 * half,), 0.1, scalars=scalars,
    )
    return out, token


def part_kernel(other, scalars, got, *refs):
    out, picker = refs[-3 if other else -2], refs[-1]
    layer = 1 - scalars[1] if other else scalars[1]

    @pl.when(pl.program_id(0) == 0)
    def _():
        row = lax.broadcasted_iota(I32, (160, 1), 0)
        source = lax.broadcasted_iota(I32, (160, 320), 1)
        picker[...] = (source == row + (row // 20 + layer) * 20).astype(F32).astype(BF)

    for half in range(2):
        rows = dot(picker[...], got[half * 320 : half * 320 + 320, :])
        out[half * 160 : half * 160 + 160, :] = rows.astype(BF)


def part(token, scalars, got, carried=None, after=()):
    width = got.shape[1]
    wide = width // 2
    other = carried is not None
    anywhere = [pl.BlockSpec(memory_space=pl.ANY)] * other
    result, token = call(
        functools.partial(part_kernel, other), token, [got] + [carried] * other,
        [pl.BlockSpec((640, wide), lambda j, s: (0, j)), *anywhere],
        [jax.ShapeDtypeStruct((320, width), BF)]
        + [jax.ShapeDtypeStruct(carried.shape, BF) for _ in anywhere],
        [pl.BlockSpec((320, wide), lambda j, s: (0, j)), *anywhere],
        (2,), 0.1, scratch=[pltpu.VMEM((160, 320), BF)], scalars=scalars, after=after,
        aliases={2: 1} if other else {},
    )
    return result, token


def lines_of(rows):
    return jnp.concatenate([r[...] for r in rows], axis=0)


def back_kernel(pieces, *refs):
    rows, (weight, saved, hidden, terms, total) = refs[:pieces], refs[pieces:]

    @pl.when(pl.program_id(0) == 0)
    def _():
        total[...] = jnp.zeros_like(total)

    total[...] += lax.dot_general(
        lines_of(rows), weight[...], (((1,), (1,)), ((), ())), preferred_element_type=F32
    )

    @pl.when(pl.program_id(0) == pl.num_programs(0) - 1)
    def _():
        hidden[...] = total[...].astype(BF)
        products = saved[...].astype(F32) * total[...]
        lanes = sum(products[:, at : at + 128] for at in range(0, products.shape[1], 128))
        terms[...] = jnp.sum(lanes.T, axis=0, keepdims=True)


def back(token, rows, weight, saved, expert):
    shape = saved.shape
    block = weight.shape[2] // 2
    whole = pl.BlockSpec(shape, lambda j: (0, 0))
    return call(
        functools.partial(back_kernel, len(rows)), token, [*rows, weight, saved],
        [pl.BlockSpec((rows[0].shape[0], block), lambda j: (0, j))] * len(rows)
        + [pl.BlockSpec((None, shape[1], block), lambda j: (expert, 0, j)), whole],
        [jax.ShapeDtypeStruct(shape, BF), jax.ShapeDtypeStruct((1, shape[0]), F32)],
        [whole, pl.BlockSpec((1, shape[0]), lambda j: (0, 0))],
        (2,), 0.1, scratch=[pltpu.VMEM(shape, F32)],
    )


def down_kernel(pieces, before, saved_t, *refs):
    rows, out = refs[:pieces], refs[-1]
    total = dot(saved_t[...], lines_of(rows))
    if before:
        total = total + refs[pieces][...]
    out[...] = total.astype(out.dtype)


def down(token, saved_t, rows, width, expert=None, before=None, result=None):
    hidden = saved_t.shape[0]
    block = width // 2
    column = pl.BlockSpec((hidden, block), lambda j: (0, j))
    in_specs = [pl.BlockSpec(saved_t.shape, lambda j: (0, 0)), *[pl.BlockSpec((rows[0].shape[0], block), lambda j: (0, j))] * len(rows)]
    args = [saved_t, *rows]
    if before is not None:
        in_specs.append(column)
        args.append(before)
    aliases = {}
    if result is not None:
        in_specs.append(pl.BlockSpec(memory_space=pl.ANY))
        args.append(result)
        aliases = {len(args) - 1: 0}
    if expert is None:
        out_shape, out_spec = jax.ShapeDtypeStruct((hidden, width), F32), column
    else:
        out_shape = jax.ShapeDtypeStruct((2, hidden, width), BF)
        out_spec = pl.BlockSpec((None, hidden, block), lambda j: (expert, 0, j))
    (out,), token = call(
        functools.partial(down_kernel, len(rows), before is not None), token, args,
        in_specs, [out_shape], [out_spec], (2,), 0.1, aliases=aliases,
    )
    return out, token


def finish_kernel(scalars, hidden0, near, distant, out):
    z = pl.program_id(0)
    step = (scalars[0] + 4 - z) & 3
    begin = pl.multiple_of(jnp.where(step == 3, 2, step & 1) * 320, 320)
    out[1] = jnp.where(step == 2, distant[...], near[pl.ds(begin, 320), :])
    row = lax.broadcasted_iota(I32, (160, 1), 0)
    plane, place = row // CAP, row % CAP
    source = lax.broadcasted_iota(I32, (160, 640), 1)
    line = jnp.where(place < 8, z * 8 + place, 24 + z * 2 + place)
    hit = (source == plane * 40 + line).astype(F32).astype(BF)
    for half in range(2):
        rows = dot(hit, hidden0[half * 640 : half * 640 + 640, :])
        out[0, half * 160 : half * 160 + 160, :] = rows.astype(BF)


def finish(token, scalars, *args):
    rows, hidden = args[0].shape
    (out,), token = call(
        finish_kernel, token, args, [pl.BlockSpec(x.shape, lambda j, s: (0, 0)) for x in args],
        [jax.ShapeDtypeStruct((2, rows, hidden), BF)],
        [pl.BlockSpec((2, rows // 4, hidden), lambda j, s: (0, j, 0))],
        (4,), 0.1, scalars=scalars,
    )
    return out


def shards(grad_out, gates, routes, w_down, saved_hidden):
    tokens, width = grad_out.shape
    zh, zl = lax.axis_index("zh"), lax.axis_index("zl")
    core = lax.axis_index("core")
    z = zh * 2 + zl
    scalars = jnp.stack([z, zl, core]).astype(I32)

    wide = width // 2

    from_down, from_up = z_shift(grad_out, 1), z_shift(grad_out, -1)
    slots = (routes.T, gates.T)
    other = core_swap(grad_out)
    (matrix1, table, meta), token = first_picker(scalars, *slots, *[core_swap(x) for x in slots])
    send1, token = pick(token, matrix1, [grad_out, other], wide)
    got1 = lax.all_to_all(send1.reshape(16, 40, width), ("y", "x"), 0, 0, tiled=True)
    got1 = got1.reshape(640, width)

    (onward_down, onward_up, meta), token = onward(token, from_down, from_up, meta, wide)
    metas = [meta, z_shift(meta, 1), z_shift(meta, 2), z_shift(meta, -1)]
    far = (z_shift(onward_down, 1), z_shift(onward_up, -1))
    saved, token = prepare(token, scalars, saved_hidden)
    saved0, saved0_t, saved_near, saved_near_t, saved_distant, saved_distant_t = saved
    matrices, token = line_picker(token, scalars, metas)

    send0, token = line_pick(
        token, scalars, matrices, grad_out, from_down, far, from_up, width // 4
    )
    (away, send0), token = part(token, scalars, got1, send0)
    rows0 = lax.all_to_all(send0, PLANE, 0, 0, tiled=True).reshape(1280, width)
    near = [z_shift(away, 1), z_shift(away, -1)]
    (own,), token = part(token, scalars, got1, None, near)
    near = [own, *near]
    distant = [z_shift(own, 2)]

    (hidden_near, terms_near), token = back(token, near, w_down, saved_near, 1)
    before, token = down(token, saved_near_t, near, width)
    (hidden0, terms0), token = back(token, [rows0], w_down, saved0, 0)
    (hidden_distant, terms_distant), token = back(token, distant, w_down, saved_distant, 1)
    d_down, token = down(token, saved_distant_t, distant, width, 1, before)
    d_down, token = down(token, saved0_t, [rows0], width, 0, None, d_down)
    d_hidden = finish(token, scalars, hidden0, hidden_near, hidden_distant)

    terms_near = terms_near.reshape(3, 32, CAP)
    terms1 = jnp.stack(
        [terms_near[0], terms_near[1], terms_distant.reshape(32, CAP), terms_near[2]], axis=1
    )
    terms1 = jnp.concatenate(
        [lax.dynamic_index_in_dim(terms1, (z - i) % 4, 1, True) for i in range(4)], axis=1
    )
    terms0 = terms0.reshape(32, 40)
    terms0 = jnp.concatenate(
        [terms0[:, :32].reshape(32, 4, 8), terms0[:, 32:].reshape(32, 4, 2)], axis=2
    )
    terms = jnp.concatenate([terms0, terms1], axis=2).reshape(128, 2 * CAP)
    returned = lax.all_to_all(terms, PLANE + Z, 0, 0, tiled=True)
    returned = returned.reshape(32, 2, 2, 2 * CAP)
    returned = (returned[:, 0] + returned[:, 1]).reshape(-1)

    table = table.reshape(1, -1)
    d_gates = jnp.sum(
        jnp.where(
            table == jnp.arange(EXPERTS * CAP, dtype=I32)[:, None], returned[:, None], 0.0
        ),
        axis=0,
    ).reshape(TOP, tokens).T
    return d_gates / gates.astype(F32), d_down, d_hidden


def solution(mesh):
    fine = Mesh(mesh.devices.reshape(2, 2, 4, 4, 2), ALL)
    in_specs = (
        P(ALL, None),
        P(ALL, None),
        P(ALL, None),
        P(("zl", "y", "x", "core"), "zh", None),
        P(("zl", "y", "x", "core"), None, "zh"),
    )
    out_specs = (P(ALL, None), in_specs[3], in_specs[4])
    return jax.shard_map(shards, mesh=fine, in_specs=in_specs, out_specs=out_specs, check_vma=False)
```

time: 519 us -> 269 us (0.52)
  blocking collectives: 127 us -> 0 us
  waiting for transfers between devices: 233 us -> 120 us
  Pallas kernels: 0 us -> 99.1 us
  local copies, waits for them, and re-layouts: 55.2 us -> 7.43 us
  matrix products: 44.8 us -> 0 us
  other arithmetic: 28.1 us -> 4.08 us
  starting transfers between devices: 15 us -> 36.7 us
  between operations: 14.2 us -> 0.81 us
    all_gather x1 -> x0, waiting for transfers between devices: 218 us -> none  [shards(): lax.all_gather(got_rows, 'outer', axis=1, tiled=True)]
    all_to_all x1 -> x0, blocking collectives: 115 us -> none  [shards(): lax.all_to_all(send_rows, 'inner', split_axis=1, concat_axis=1, tiled=True)]
    pallas_call x0 -> x15, Pallas kernels: none -> 99.1 us  [call(): pl.pallas_call(run, out_shape=[*out_shape, jax.ShapeDtypeStruct((8, 128),...]
    ppermute x0 -> x13, waiting for transfers between devices: none -> 84.5 us  [the longest x10 83.8 us: z_shift(): return lax.ppermute(value, Z, [(i, (i + step) % 4) for i in range(4)])]
    dot_general x3 -> x0, matrix products: 44.8 us -> none  [the longest x1 21.2 us: shards(): jnp.einsum('erd,efd->erf', routed, w_down, preferred_element_type=jnp.flo...]
    reshape x6 -> x2, local copies, waits for them, and re-layouts: 30.6 us -> 0.09 us  [the longest x1 0.08 us: shards(): terms0 = terms0.reshape(32, 40)]
    convert_element_type x2 -> x0, other arithmetic: 24.6 us -> none  [the longest x1 20.3 us: shards(): (gate_rows[:, :, None] * routed.astype(jnp.float32)).astype(jnp.bfloat16)]
    all_to_all x2 -> x3, waiting for transfers between devices: 15 us -> 35.3 us  [the longest x1 30.5 us: shards(): rows0 = lax.all_to_all(send0, PLANE, 0, 0, tiled=True).reshape(1280, width)]
  transfers between devices with their start and end apart: 3 -> 16, of which waited for: 3 -> 9; matrix products, arithmetic and copies ran while one was open for 1% -> 1% of each run, Pallas kernels for 0% -> 33%
where the time goes in v4:
time: 269 us; the launch traced here: 268 us
  waiting for transfers between devices  120 us (45%)
  Pallas kernels  99.1 us (37%)
  starting transfers between devices  36.7 us (14%)
  local copies, waits for them, and re-layouts  7.43 us (3%)
  other arithmetic  4.08 us (2%)
    pallas_call x15, Pallas kernels, call(): pl.pallas_call(run, out_shape=[*out_shape, jax.ShapeDtypeStruct((8, 128),...  99.1 us
    ppermute x10, waiting for transfers between devices, z_shift(): return lax.ppermute(value, Z, [(i, (i + step) % 4) for i in range(4)])  83.8 us
    all_to_all x1, waiting for transfers between devices, shards(): rows0 = lax.all_to_all(send0, PLANE, 0, 0, tiled=True).reshape(1280, width)  30.5 us
    ppermute x10, starting transfers between devices, z_shift(): return lax.ppermute(value, Z, [(i, (i + step) % 4) for i in range(4)])  10.8 us
    all_to_all x1, starting transfers between devices, shards(): returned = lax.all_to_all(terms, PLANE + Z, 0, 0, tiled=True)  10.4 us
    all_to_all x1, starting transfers between devices, shards(): lax.all_to_all(send1.reshape(16, 40, width), ('y', 'x'), 0, 0, tiled=True)  6.8 us
    all_to_all x1, starting transfers between devices, shards(): rows0 = lax.all_to_all(send0, PLANE, 0, 0, tiled=True).reshape(1280, width)  6.75 us
  transfers between devices with their start and end apart: 16, of which 9 were waited for; matrix products, arithmetic and copies ran while one was open for 1% of the time, Pallas kernels for 33%

profile of v4, /device:TPU:1, one launch (start us, length us, event | category | flops | bytes accessed | tf_op | source)
XLA Modules:
  0.0 267.9 jit_solution(14561008037278571711)
XLA Ops:
  8.6 3.8 %shard_map.76 = (bf16[640,512]{1,0:T(8,128)(2,1)}, s32[4,256]{1,0:T(4,128)}, f32[8,256]{1,0:T(8,128)}, f32[8,128]{1,0:T(8,128)}) custom-call(s32[3]{0:T(128)} %pad_add_fusion.refs_0_, s32[4,256]{1,0:T(4,128)} %bitcast.37, bf16[4,256]{1,0:T(4,128)(2,1)} %bitcast.35, s32[4,256]{1,0:T(4,128)} %copy-done.10, bf16[4,256]{1,0:T(4,128)(2,1)} %copy-done.11), custom_call_target="tpu_custom_call" | custom-call | flops 100000000 | tf_op jit(solution)/shard_map/pallas_call | solution.py:45
  13.6 6.0 %shard_map.77 = (bf16[640,3584]{1,0:T(8,128)(2,1)}, f32[8,128]{1,0:T(8,128)}) custom-call(bf16[640,512]{1,0:T(8,128)(2,1)} %get-tuple-element.47.refs_0_, bf16[256,3584]{1,0:T(8,128)(2,1)} %refs_3_.2, bf16[256,3584]{1,0:T(8,128)(2,1)} %copy-done.2, f32[8,128]{1,0:T(8,128)} %get-tuple-element.48.refs_3_), custom_call_target="tpu_custom_call" | custom-call | flops 100000000 | tf_op jit(solution)/shard_map/pallas_call | solution.py:45
  19.7 6.8 %all-to-all-start = ((bf16[16,40,3584]{2,1,0:T(8,128)(2,1)}), bf16[16,40,3584]{2,1,0:T(8,128)(2,1)}, u32[]{:S(2)}, u32[]{:S(2)}) async-start(bf16[16,40,3584]{2,1,0:T(8,128)(2,1)} %bitcast.28), calls=%async_computation | async-start | bytes 9175040 | tf_op jit(solution)/shard_map/all_to_all | solution.py:403
  26.5 20.1 %collective-permute-done.3.refs_0_.refs_4_ = bf16[256,3584]{1,0:T(8,128)(2,1)} collective-permute-done((bf16[256,3584]{1,0:T(8,128)(2,1)}, bf16[256,3584]{1,0:T(8,128)(2,1)}, u32[]{:S(2)}, u32[]{:S(2)}) %collective-permute-start.3) | collective-permute-done | bytes 1835040 | tf_op jit(solution)/shard_map/ppermute | solution.py:23
  46.6 3.0 %shard_map.78 = (bf16[256,1792]{1,0:T(8,128)(2,1)}, bf16[256,1792]{1,0:T(8,128)(2,1)}, f32[8,256]{1,0:T(8,128)}, f32[8,128]{1,0:T(8,128)}) custom-call(bf16[256,3584]{1,0:T(8,128)(2,1)} %collective-permute-done.3.refs_0_.refs_4_, bf16[256,3584]{1,0:T(8,128)(2,1)} %collective-permute-done.4.refs_1_.refs_7_, f32[8,256]{1,0:T(8,128)} %get-tuple-element.50.refs_2_, ...), custom_call_target="tpu_custom_call" | custom-call | flops 999999995904 | tf_op jit(solution)/shard_map/pallas_call | solution.py:45
  54.1 7.7 %shard_map.79 = (bf16[1280,512]{1,0:T(8,128)(2,1)}, bf16[512,1280]{1,0:T(8,128)(2,1)}, bf16[960,512]{1,0:T(8,128)(2,1)}, bf16[512,960]{1,0:T(8,128)(2,1)}, bf16[...) custom-call(s32[3]{0:T(128)} %pad_add_fusion.refs_0_, bf16[2,1280,512]{2,1,0:T(8,128)(2,1)} %refs_1_.5, ...), custom_call_target="tpu_custom_call" | custom-call | flops 100000000 | tf_op jit(solution)/shard_map/pallas_call | solution.py:45
  61.7 9.7 %collective-permute-done.7.refs_4_ = f32[8,256]{1,0:T(8,128)S(1)} collective-permute-done((f32[8,256]{1,0:T(8,128)}, f32[8,256]{1,0:T(8,128)S(1)}, u32[]{:S(2)}, u32[]{:S(2)}) %collective-permute-start.7) | collective-permute-done | bytes 8224 | tf_op jit(solution)/shard_map/ppermute | solution.py:23
  73.7 4.8 %shard_map.80 = (bf16[256,1024]{1,0:T(8,128)(2,1)}, bf16[256,1024]{1,0:T(8,128)(2,1)}, f32[8,128]{1,0:T(8,128)}) custom-call(s32[3]{0:T(128)} %pad_add_fusion.refs_0_, f32[8,256]{1,0:T(8,128)} %get-tuple-element.52.refs_1_, f32[8,256]{1,0:T(8,128)} %copy-done.9, f32[8,256]{1,0:T(8,128)} %copy-done.8, f32[8,256]{1,0:T(8,128)} %copy-done.7, ...), custom_call_target="tpu_custom_call" | custom-call | flops 100000000 | tf_op jit(solution)/shard_map/pallas_call | solution.py:45
  79.8 10.4 %shard_map.81 = (bf16[32,5,8,3584]{3,2,1,0:T(8,128)(2,1)}, f32[8,128]{1,0:T(8,128)}) custom-call(s32[3]{0:T(128)} %pad_add_fusion.refs_0_, bf16[256,1024]{1,0:T(8,128)(2,1)} %get-tuple-element.55.refs_1_, bf16[256,1024]{1,0:T(8,128)(2,1)} %get-tuple-element.56.refs_2_, bf16[256,3584]{1,0:T(8,128)(2,1)} %refs_3_.2, ...), custom_call_target="tpu_custom_call" | custom-call | flops 100000000 | tf_op jit(solution)/shard_map/pallas_call | solution.py:45
  90.2 4.7 %all-to-all-done = bf16[16,40,3584]{2,1,0:T(8,128)(2,1)} async-done(((bf16[16,40,3584]{2,1,0:T(8,128)(2,1)}), bf16[16,40,3584]{2,1,0:T(8,128)(2,1)}, u32[]{:S(2)}, u32[]{:S(2)}) %all-to-all-start) | async-done | bytes 4587552 | tf_op jit(solution)/shard_map/all_to_all | solution.py:403
  94.9 4.9 %shard_map.82 = (bf16[320,3584]{1,0:T(8,128)(2,1)}, bf16[32,5,8,3584]{3,2,1,0:T(8,128)(2,1)}, f32[8,128]{1,0:T(8,128)}) custom-call(s32[3]{0:T(128)} %pad_add_fusion.refs_0_, bf16[640,3584]{1,0:T(8,128)(2,1)} %bitcast.6.refs_1_, bf16[32,5,8,3584]{3,2,1,0:T(8,128)(2,1)} %get-tuple-element.60.refs_2_, ...), custom_call_target="tpu_custom_call", output_to_operand_aliasing={{1}: (2, {})} | custom-call | flops 100000000 | tf_op jit(solution)/shard_map/pallas_call | solution.py:45
  99.8 6.8 %all-to-all-start.1 = ((bf16[32,5,8,3584]{3,2,1,0:T(8,128)(2,1)}), bf16[32,5,8,3584]{3,2,1,0:T(8,128)(2,1)}, u32[]{:S(2)}, u32[]{:S(2)}) async-start(bf16[32,5,8,3584]{3,2,1,0:T(8,128)(2,1)} %get-tuple-element.62), calls=%async_computation.1 | async-start | bytes 18350080 | tf_op jit(solution)/shard_map/all_to_all | solution.py:417
  108.8 49.3 %collective-permute-done.11.refs_4_.refs_2_.refs_3_ = bf16[320,3584]{1,0:T(8,128)(2,1)S(1)} collective-permute-done((bf16[320,3584]{1,0:T(8,128)(2,1)}, bf16[320,3584]{1,0:T(8,128)(2,1)S(1)}, u32[]{:S(2)}, u32[]{:S(2)}) %collective-permute-start.11) | collective-permute-done | bytes 2293792 | tf_op jit(solution)/shard_map/ppermute | solution.py:23
  158.1 3.0 %collective-permute-done.10.refs_3_.refs_1_.refs_2_ = bf16[320,3584]{1,0:T(8,128)(2,1)} collective-permute-done((bf16[320,3584]{1,0:T(8,128)(2,1)}, bf16[320,3584]{1,0:T(8,128)(2,1)}, u32[]{:S(2)}, u32[]{:S(2)}) %collective-permute-start.10) | collective-permute-done | bytes 2293792 | tf_op jit(solution)/shard_map/ppermute | solution.py:23
  161.1 5.0 %shard_map.83 = (bf16[320,3584]{1,0:T(8,128)(2,1)}, f32[8,128]{1,0:T(8,128)}) custom-call(s32[3]{0:T(128)} %pad_add_fusion.refs_0_, bf16[640,3584]{1,0:T(8,128)(2,1)} %bitcast.6.refs_1_, f32[8,128]{1,0:T(8,128)} %get-tuple-element.65.refs_2_, bf16[320,3584]{1,0:T(8,128)(2,1)} %collective-permute-done.10.refs_3_.refs_1_.refs_2_, bf16[320,3584]{1,0:T(8,128)(2,1)} %copy-done), custom_call_target="tpu_custom_call" | custom-call | flops 100000000 | tf_op jit(solution)/shard_map/pallas_call | solution.py:45
  166.5 8.8 %shard_map.84 = (bf16[960,512]{1,0:T(8,128)(2,1)}, f32[1,960]{1,0:T(1,128)}, f32[8,128]{1,0:T(8,128)}) custom-call(bf16[320,3584]{1,0:T(8,128)(2,1)} %get-tuple-element.67.refs_0_.refs_1_, bf16[320,3584]{1,0:T(8,128)(2,1)} %collective-permute-done.10.refs_3_.refs_1_.refs_2_, bf16[320,3584]{1,0:T(8,128)(2,1)} %copy-done, bf16[2,512,3584]{2,1,0:T(8,128)(2,1)} %refs_1_.7, ...), custom_call_target="tpu_custom_call" | custom-call | flops 100000000 | tf_op jit(solution)/shard_map/pallas_call | solution.py:45
  176.7 9.0 %shard_map.85 = (f32[512,3584]{1,0:T(8,128)}, f32[8,128]{1,0:T(8,128)}) custom-call(bf16[512,960]{1,0:T(8,128)(2,1)} %get-tuple-element.64.refs_0_, bf16[320,3584]{1,0:T(8,128)(2,1)} %get-tuple-element.67.refs_0_.refs_1_, bf16[320,3584]{1,0:T(8,128)(2,1)} %collective-permute-done.10.refs_3_.refs_1_.refs_2_, bf16[320,3584]{1,0:T(8,128)(2,1)} %copy-done, ...), custom_call_target="tpu_custom_call" | custom-call | flops 100000000 | tf_op jit(solution)/shard_map/pallas_call | solution.py:45
  185.7 30.5 %all-to-all-done.1 = bf16[32,5,8,3584]{3,2,1,0:T(8,128)(2,1)} async-done(((bf16[32,5,8,3584]{3,2,1,0:T(8,128)(2,1)}), bf16[32,5,8,3584]{3,2,1,0:T(8,128)(2,1)}, u32[]{:S(2)}, u32[]{:S(2)}) %all-to-all-start.1) | async-done | bytes 9175072 | tf_op jit(solution)/shard_map/all_to_all | solution.py:417
  216.3 10.1 %shard_map.86 = (bf16[1280,512]{1,0:T(8,128)(2,1)}, f32[1,1280]{1,0:T(1,128)}, f32[8,128]{1,0:T(8,128)}) custom-call(bf16[1280,3584]{1,0:T(8,128)(2,1)} %bitcast.7.refs_0_.refs_1_, bf16[2,512,3584]{2,1,0:T(8,128)(2,1)} %refs_1_.7, bf16[1280,512]{1,0:T(8,128)(2,1)} %get-tuple-element.63.refs_2_, f32[8,128]{1,0:T(8,128)} %get-tuple-element.71.refs_3_), custom_call_target="tpu_custom_call" | custom-call | flops 100000000 | tf_op jit(solution)/shard_map/pallas_call | solution.py:45
  228.8 4.6 %shard_map.87 = (bf16[320,512]{1,0:T(8,128)(2,1)}, f32[1,320]{1,0:T(1,128)}, f32[8,128]{1,0:T(8,128)}) custom-call(bf16[320,3584]{1,0:T(8,128)(2,1)} %copy-done.1, bf16[2,512,3584]{2,1,0:T(8,128)(2,1)} %refs_1_.7, bf16[320,512]{1,0:T(8,128)(2,1)} %get-tuple-element.74.refs_2_, f32[8,128]{1,0:T(8,128)} %get-tuple-element.75.refs_3_), custom_call_target="tpu_custom_call" | custom-call | flops 100000000 | tf_op jit(solution)/shard_map/pallas_call | solution.py:45
  235.2 10.4 %all-to-all-start.2 = ((f32[128,1,20]{2,1,0:T(1,128)}), f32[128,1,20]{2,1,0:T(1,128)S(1)}, u32[]{:S(2)}, u32[]{:S(2)}) async-start(f32[128,1,20]{2,1,0:T(1,128)} %bitcast.10), calls=%async_computation.2 | async-start | bytes 131072 | tf_op jit(solution)/shard_map/all_to_all | solution.py:443
  245.5 6.3 %shard_map.88 = (bf16[2,512,3584]{2,1,0:T(8,128)(2,1)}, f32[8,128]{1,0:T(8,128)}) custom-call(bf16[512,320]{1,0:T(8,128)(2,1)} %get-tuple-element.78.refs_0_, bf16[320,3584]{1,0:T(8,128)(2,1)} %copy-done.1, f32[512,3584]{1,0:T(8,128)} %get-tuple-element.79.refs_2_, f32[8,128]{1,0:T(8,128)} %get-tuple-element.80.refs_3_), custom_call_target="tpu_custom_call" | custom-call | flops 100000000 | tf_op jit(solution)/shard_map/pallas_call | solution.py:45
  251.9 9.0 %shard_map.89 = (bf16[2,512,3584]{2,1,0:T(8,128)(2,1)}, f32[8,128]{1,0:T(8,128)}) custom-call(bf16[512,1280]{1,0:T(8,128)(2,1)} %get-tuple-element.77.refs_0_, bf16[1280,3584]{1,0:T(8,128)(2,1)} %bitcast.7.refs_0_.refs_1_, bf16[2,512,3584]{2,1,0:T(8,128)(2,1)} %get-tuple-element.81.refs_2_, ...), custom_call_target="tpu_custom_call", output_to_operand_aliasing={{0}: (2, {})} | custom-call | flops 100000000 | tf_op jit(solution)/shard_map/pallas_call | solution.py:45
  260.9 5.6 %shard_map.90 = (bf16[2,1280,512]{2,1,0:T(8,128)(2,1)}, f32[8,128]{1,0:T(8,128)}) custom-call(s32[3]{0:T(128)} %pad_add_fusion.refs_0_, bf16[1280,512]{1,0:T(8,128)(2,1)} %get-tuple-element.84.refs_1_, bf16[960,512]{1,0:T(8,128)(2,1)} %get-tuple-element.85.refs_2_, bf16[320,512]{1,0:T(8,128)(2,1)} %get-tuple-element.86.refs_3_, ...), custom_call_target="tpu_custom_call" | custom-call | flops 100000000 | tf_op jit(solution)/shard_map/pallas_call | solution.py:45
  (74 shorter events, 26.7 us)
Async XLA Ops:
  0.6 11.8 %collective-permute-start.2 = (bf16[256,3584]{1,0:T(8,128)(2,1)}, bf16[256,3584]{1,0:T(8,128)(2,1)S(1)}, u32[]{:S(2)}, u32[]{:S(2)}) collective-permute-start(bf16[256,3584]{1,0:T(8,128)(2,1)} %refs_3_.2), channel_id=1, source_target_pairs={{0,1},{1,0},{2,3},{3,2},{4,5},{5,4},{6,7},{7,6},{8,9},{9,8},{10,11... | collective-permute-start | bytes 5505032 | tf_op jit(solution)/shard_map/ppermute | solution.py:27
  2.1 44.5 %collective-permute-start.3 = (bf16[256,3584]{1,0:T(8,128)(2,1)}, bf16[256,3584]{1,0:T(8,128)(2,1)}, u32[]{:S(2)}, u32[]{:S(2)}) collective-permute-start(bf16[256,3584]{1,0:T(8,128)(2,1)} %refs_3_.2), channel_id=1, source_target_pairs={{0,32},{32,64},{64,96},{96,0},{1,33},{33,65},{65,97},{97,1},{2,34}... | collective-permute-start | bytes 5505032 | tf_op jit(solution)/shard_map/ppermute | solution.py:23
  3.9 42.7 %collective-permute-start.4 = (bf16[256,3584]{1,0:T(8,128)(2,1)}, bf16[256,3584]{1,0:T(8,128)(2,1)}, u32[]{:S(2)}, u32[]{:S(2)}) collective-permute-start(bf16[256,3584]{1,0:T(8,128)(2,1)} %refs_3_.2), channel_id=1, source_target_pairs={{0,96},{32,0},{64,32},{96,64},{1,97},{33,1},{65,33},{97,65},{2,98}... | collective-permute-start | bytes 5505032 | tf_op jit(solution)/shard_map/ppermute | solution.py:23
  6.0 1.5 collective-permute-start.1
  6.4 1.4 collective-permute-start
  12.4 1.2 copy-start.2
  19.7 75.2 %all-to-all-start = ((bf16[16,40,3584]{2,1,0:T(8,128)(2,1)}), bf16[16,40,3584]{2,1,0:T(8,128)(2,1)}, u32[]{:S(2)}, u32[]{:S(2)}) async-start(bf16[16,40,3584]{2,1,0:T(8,128)(2,1)} %bitcast.28), calls=%async_computation | async-start | bytes 9175040 | tf_op jit(solution)/shard_map/all_to_all | solution.py:403
  49.6 28.9 %collective-permute-start.8 = (bf16[256,1792]{1,0:T(8,128)(2,1)}, bf16[256,1792]{1,0:T(8,128)(2,1)S(1)}, u32[]{:S(2)}, u32[]{:S(2)}) collective-permute-start(bf16[256,1792]{1,0:T(8,128)(2,1)} %get-tuple-element.57), channel_id=1, source_target_pairs={{0,32},{32,64},{64,96},{96,0},{1,33},{33,65},{65,97},{97,1},{2,34}... | collective-permute-start | bytes 2752520 | tf_op jit(solution)/shard_map/ppermute | solution.py:23
  50.1 28.4 %collective-permute-start.9 = (bf16[256,1792]{1,0:T(8,128)(2,1)}, bf16[256,1792]{1,0:T(8,128)(2,1)S(1)}, u32[]{:S(2)}, u32[]{:S(2)}) collective-permute-start(bf16[256,1792]{1,0:T(8,128)(2,1)} %get-tuple-element.58), channel_id=1, source_target_pairs={{0,96},{32,0},{64,32},{96,64},{1,97},{33,1},{65,33},{97,65},{2,98}... | collective-permute-start | bytes 2752520 | tf_op jit(solution)/shard_map/ppermute | solution.py:23
  52.3 19.2 %collective-permute-start.7 = (f32[8,256]{1,0:T(8,128)}, f32[8,256]{1,0:T(8,128)S(1)}, u32[]{:S(2)}, u32[]{:S(2)}) collective-permute-start(f32[8,256]{1,0:T(8,128)} %get-tuple-element.52.refs_1_), channel_id=1, source_target_pairs={{0,96},{32,0},{64,32},{96,64},{1,97},{33,1},{65,33},{97,65},{2,98}... | collective-permute-start | bytes 24584 | tf_op jit(solution)/shard_map/ppermute | solution.py:23
  53.4 19.6 %collective-permute-start.6 = (f32[8,256]{1,0:T(8,128)}, f32[8,256]{1,0:T(8,128)S(1)}, u32[]{:S(2)}, u32[]{:S(2)}) collective-permute-start(f32[8,256]{1,0:T(8,128)} %get-tuple-element.52.refs_1_), channel_id=1, source_target_pairs={{0,64},{32,96},{64,0},{96,32},{1,65},{33,97},{65,1},{97,33},{2,66}... | collective-permute-start | bytes 24584 | tf_op jit(solution)/shard_map/ppermute | solution.py:23
  53.4 19.6 %collective-permute-start.5 = (f32[8,256]{1,0:T(8,128)}, f32[8,256]{1,0:T(8,128)S(1)}, u32[]{:S(2)}, u32[]{:S(2)}) collective-permute-start(f32[8,256]{1,0:T(8,128)} %get-tuple-element.52.refs_1_), channel_id=1, source_target_pairs={{0,32},{32,64},{64,96},{96,0},{1,33},{33,65},{65,97},{97,1},{2,34}... | collective-permute-start | bytes 24584 | tf_op jit(solution)/shard_map/ppermute | solution.py:23
  71.5 1.6 copy-start.7
  78.5 0.9 copy-start.3
  78.5 1.3 copy-start.4
  99.8 116.4 %all-to-all-start.1 = ((bf16[32,5,8,3584]{3,2,1,0:T(8,128)(2,1)}), bf16[32,5,8,3584]{3,2,1,0:T(8,128)(2,1)}, u32[]{:S(2)}, u32[]{:S(2)}) async-start(bf16[32,5,8,3584]{3,2,1,0:T(8,128)(2,1)} %get-tuple-element.62), calls=%async_computation.1 | async-start | bytes 18350080 | tf_op jit(solution)/shard_map/all_to_all | solution.py:417
  106.6 51.5 %collective-permute-start.11 = (bf16[320,3584]{1,0:T(8,128)(2,1)}, bf16[320,3584]{1,0:T(8,128)(2,1)S(1)}, u32[]{:S(2)}, u32[]{:S(2)}) collective-permute-start(bf16[320,3584]{1,0:T(8,128)(2,1)} %get-tuple-element.66), channel_id=1, source_target_pairs={{0,96},{32,0},{64,32},{96,64},{1,97},{33,1},{65,33},{97,65},{2,98}... | collective-permute-start | bytes 6881288 | tf_op jit(solution)/shard_map/ppermute | solution.py:23
  108.8 52.3 %collective-permute-start.10 = (bf16[320,3584]{1,0:T(8,128)(2,1)}, bf16[320,3584]{1,0:T(8,128)(2,1)}, u32[]{:S(2)}, u32[]{:S(2)}) collective-permute-start(bf16[320,3584]{1,0:T(8,128)(2,1)} %get-tuple-element.66), channel_id=1, source_target_pairs={{0,32},{32,64},{64,96},{96,0},{1,33},{33,65},{65,97},{97,1},{2,34}... | collective-permute-start | bytes 6881288 | tf_op jit(solution)/shard_map/ppermute | solution.py:23
  158.1 3.0 %copy-start = (bf16[320,3584]{1,0:T(8,128)(2,1)}, bf16[320,3584]{1,0:T(8,128)(2,1)S(1)}, u32[]{:S(2)}) copy-start(bf16[320,3584]{1,0:T(8,128)(2,1)S(1)} %collective-permute-done.11.refs_4_.refs_2_.refs_3_) | copy-start | bytes 6881284
  161.1 5.4 %copy-start.5 = (s32[4,256]{1,0:T(4,128)S(1)}, s32[4,256]{1,0:T(4,128)}, u32[]{:S(2)}) copy-start(s32[4,256]{1,0:T(4,128)} %get-tuple-element.46) | copy-start | bytes 12292
  166.2 61.2 %collective-permute-start.12 = (bf16[320,3584]{1,0:T(8,128)(2,1)}, bf16[320,3584]{1,0:T(8,128)(2,1)S(1)}, u32[]{:S(2)}, u32[]{:S(2)}) collective-permute-start(bf16[320,3584]{1,0:T(8,128)(2,1)} %get-tuple-element.67.refs_0_.refs_1_), channel_id=1, source_target_pairs={{0,64},{32,96},{64,0},{96,32},{1,65},{33,97},{65,1},{97,33},{2,66}... | collective-permute-start | bytes 6881288 | tf_op jit(solution)/shard_map/ppermute | solution.py:23
  227.4 1.4 copy-start.1
  235.2 31.3 %all-to-all-start.2 = ((f32[128,1,20]{2,1,0:T(1,128)}), f32[128,1,20]{2,1,0:T(1,128)S(1)}, u32[]{:S(2)}, u32[]{:S(2)}) async-start(f32[128,1,20]{2,1,0:T(1,128)} %bitcast.10), calls=%async_computation.2 | async-start | bytes 131072 | tf_op jit(solution)/shard_map/all_to_all | solution.py:443
  260.9 6.4 %copy-start.6 = (bf16[256,4]{0,1:T(4,128)(2,1)S(1)}, bf16[256,4]{0,1:T(4,128)(2,1)}, u32[]{:S(2)}) copy-start(bf16[256,4]{0,1:T(4,128)(2,1)} %param.6) | copy-start | bytes 6148
  (4 other events, 2.4 us)

commit v5 on v4

--- a/solution.py
+++ b/solution.py
@@ -142,34 +142,48 @@
     return total.astype(BF), routes, places
 
 
-def first_picker_kernel(scalars, routes, gates, routes_other, gates_other, out, table, meta):
+def first_pick_kernel(
+    scalars, routes, gates, routes_other, gates_other, tokens, tokens_other, out, table, meta, matrix
+):
     core = scalars[2]
     count = meta.shape[1]
-    for s, pair in enumerate(((routes, gates), (routes_other, gates_other))):
-        both = jnp.concatenate([x[...].astype(F32) for x in pair], axis=0)
-        source = core if s == 0 else 1 - core
-
-        def rows_of(r, place):
-            row = ((r >> 2) & 15) * 40 + (r >> 6) * 20 + source * CAP + place
-            return jnp.where((r & 3) == 2 * core + 1, row, -1)
-
-        matrix, named, places = picked(both, rows_of, out.shape[0])
-        out[:, s * count : (s + 1) * count] = matrix
-        if s == 0:
-            meta[...] = both
-            for k in range(TOP):
-                r = named[k]
-                device = ((r >> 1) & 31) * 4 + (r >> 6) * 2
-                table[k : k + 1, :] = (device + (r & 1)) * CAP + places[k]
-
-
-def first_picker(scalars, *args):
-    count = args[0].shape[1]
-    shapes = [((640, 2 * count), BF), ((TOP, count), I32), ((2 * TOP, count), F32)]
-    return call(
-        first_picker_kernel, None, args, [pl.BlockSpec(x.shape, lambda j, s: (0, 0)) for x in args],
+
+    @pl.when(pl.program_id(0) == 0)
+    def _():
+        for s, pair in enumerate(((routes, gates), (routes_other, gates_other))):
+            both = jnp.concatenate([x[...].astype(F32) for x in pair], axis=0)
+            source = core if s == 0 else 1 - core
+
+            def rows_of(r, place):
+                row = ((r >> 2) & 15) * 40 + (r >> 6) * 20 + source * CAP + place
+                return jnp.where((r & 3) == 2 * core + 1, row, -1)
+
+            picks, named, places = picked(both, rows_of, out.shape[0])
+            matrix[:, s * count : (s + 1) * count] = picks
+            if s == 0:
+                meta[...] = both
+                for k in range(TOP):
+                    r = named[k]
+                    device = ((r >> 1) & 31) * 4 + (r >> 6) * 2
+                    table[k : k + 1, :] = (device + (r & 1)) * CAP + places[k]
+
+    lines = jnp.concatenate([tokens[...], tokens_other[...]], axis=0)
+    out[...] = dot(matrix[...], lines).astype(BF)
+
+
+def first_pick(scalars, slots, slots_other, tokens, tokens_other):
+    count, width = tokens.shape
+    wide = width // 2
+    small = [*slots, *slots_other]
+    shapes = [((640, width), BF), ((TOP, count), I32), ((2 * TOP, count), F32)]
+    return call(
+        first_pick_kernel, None, [*small, tokens, tokens_other],
+        [pl.BlockSpec(x.shape, lambda j, s: (0, 0)) for x in small]
+        + [pl.BlockSpec((count, wide), lambda j, s: (0, j))] * 2,
         [jax.ShapeDtypeStruct(*sh) for sh in shapes],
-        [pl.BlockSpec(sh[0], lambda j, s: (0, 0)) for sh in shapes], (1,), 0.1, scalars=scalars,
+        [pl.BlockSpec((640, wide), lambda j, s: (0, j))]
+        + [pl.BlockSpec(sh[0], lambda j, s: (0, 0)) for sh in shapes[1:]],
+        (2,), 0.1, scratch=[pltpu.VMEM((640, 2 * count), BF)], scalars=scalars,
     )
 
 
@@ -203,23 +217,6 @@
         [jax.ShapeDtypeStruct(shape, BF)] * 2, [pl.BlockSpec(shape, lambda j, s: (0, 0))] * 2,
         (1,), 0.1, scalars=scalars,
     )
-
-
-def pick_kernel(matrix, one, two, out):
-    lines = jnp.concatenate([one[...], two[...]], axis=0)
-    out[...] = dot(matrix[...], lines).astype(BF)
-
-
-def pick(token, matrix, tokens, block):
-    (count, width), rows = tokens[0].shape, matrix.shape[0]
-    (out,), token = call(
-        pick_kernel, token, [matrix, *tokens],
-        [pl.BlockSpec(matrix.shape, lambda j: (0, 0))]
-        + [pl.BlockSpec((count, block), lambda j: (0, j))] * 2,
-        [jax.ShapeDtypeStruct((rows, width), BF)],
-        [pl.BlockSpec((rows, block), lambda j: (0, j))], (width // block,), 0.1,
-    )
-    return out, token
 
 
 def line_pick_kernel(scalars, first, last, here, down, far_left, far_right, up, out):
@@ -258,7 +255,7 @@
 
 
 def part_kernel(other, scalars, got, *refs):
-    out, picker = refs[-3 if other else -2], refs[-1]
+    picker = refs[-1]
     layer = 1 - scalars[1] if other else scalars[1]
 
     @pl.when(pl.program_id(0) == 0)
@@ -267,30 +264,65 @@
         source = lax.broadcasted_iota(I32, (160, 320), 1)
         picker[...] = (source == row + (row // 20 + layer) * 20).astype(F32).astype(BF)
 
-    for half in range(2):
-        rows = dot(picker[...], got[half * 320 : half * 320 + 320, :])
-        out[half * 160 : half * 160 + 160, :] = rows.astype(BF)
-
-
-def part(token, scalars, got, carried=None, after=()):
+    def write(out):
+        for half in range(2):
+            rows = dot(picker[...], got[half * 320 : half * 320 + 320, :])
+            out[half * 160 : half * 160 + 160, :] = rows.astype(BF)
+
+    if other:
+        write(refs[-3])
+    else:
+        for side in range(2):
+            pl.when(pl.program_id(0) == side)(functools.partial(write, refs[side]))
+
+
+def part(token, scalars, got, carried=None):
     width = got.shape[1]
     wide = width // 2
-    other = carried is not None
-    anywhere = [pl.BlockSpec(memory_space=pl.ANY)] * other
-    result, token = call(
-        functools.partial(part_kernel, other), token, [got] + [carried] * other,
-        [pl.BlockSpec((640, wide), lambda j, s: (0, j)), *anywhere],
-        [jax.ShapeDtypeStruct((320, width), BF)]
-        + [jax.ShapeDtypeStruct(carried.shape, BF) for _ in anywhere],
-        [pl.BlockSpec((320, wide), lambda j, s: (0, j)), *anywhere],
-        (2,), 0.1, scratch=[pltpu.VMEM((160, 320), BF)], scalars=scalars, after=after,
-        aliases={2: 1} if other else {},
-    )
-    return result, token
+    if carried is None:
+        args, specs, aliases = [got], [], {}
+        shapes = [(320, wide)] * 2
+        out_specs = [pl.BlockSpec((320, wide), lambda j, s: (0, 0))] * 2
+    else:
+        args, specs, aliases = [got, carried], [pl.BlockSpec(memory_space=pl.ANY)], {2: 1}
+        shapes = [(320, width), carried.shape]
+        out_specs = [pl.BlockSpec((320, wide), lambda j, s: (0, j)), *specs]
+    return call(
+        functools.partial(part_kernel, carried is not None), token, args,
+        [pl.BlockSpec((640, wide), lambda j, s: (0, j)), *specs],
+        [jax.ShapeDtypeStruct(sh, BF) for sh in shapes], out_specs,
+        (2,), 0.1, scratch=[pltpu.VMEM((160, 320), BF)], scalars=scalars, aliases=aliases,
+    )
+
+
+def hold(token, carried, after):
+    anywhere = [pl.BlockSpec(memory_space=pl.ANY)] * len(carried)
+    return call(
+        lambda *refs: None, token, carried, anywhere,
+        [jax.ShapeDtypeStruct(x.shape, x.dtype) for x in carried], anywhere, (1,), 0.1,
+        aliases={n: n for n in range(len(carried))}, after=after,
+    )
 
 
 def lines_of(rows):
-    return jnp.concatenate([r[...] for r in rows], axis=0)
+    blocks = [r[...] for r in rows]
+    if len(blocks) > 1:
+        blocks = [jnp.where(pl.program_id(0) == 0, blocks[0], blocks[1]), *blocks[2:]]
+    return jnp.concatenate(blocks, axis=0)
+
+
+def line_specs(rows, wide):
+    return [
+        pl.BlockSpec((r.shape[0], wide), (lambda j: (0, 0)) if r.shape[1] == wide else (lambda j: (0, j)))
+        for r in rows
+    ]
+
+
+def close(total, saved, hidden, terms):
+    hidden[...] = total[...].astype(BF)
+    products = saved[...].astype(F32) * total[...]
+    lanes = sum(products[:, at : at + 128] for at in range(0, products.shape[1], 128))
+    terms[...] = jnp.sum(lanes.T, axis=0, keepdims=True)
 
 
 def back_kernel(pieces, *refs):
@@ -303,87 +335,129 @@
     total[...] += lax.dot_general(
         lines_of(rows), weight[...], (((1,), (1,)), ((), ())), preferred_element_type=F32
     )
-
-    @pl.when(pl.program_id(0) == pl.num_programs(0) - 1)
-    def _():
-        hidden[...] = total[...].astype(BF)
-        products = saved[...].astype(F32) * total[...]
-        lanes = sum(products[:, at : at + 128] for at in range(0, products.shape[1], 128))
-        terms[...] = jnp.sum(lanes.T, axis=0, keepdims=True)
+    pl.when(pl.program_id(0) == 1)(functools.partial(close, total, saved, hidden, terms))
 
 
 def back(token, rows, weight, saved, expert):
     shape = saved.shape
-    block = weight.shape[2] // 2
+    wide = weight.shape[2] // 2
     whole = pl.BlockSpec(shape, lambda j: (0, 0))
     return call(
         functools.partial(back_kernel, len(rows)), token, [*rows, weight, saved],
-        [pl.BlockSpec((rows[0].shape[0], block), lambda j: (0, j))] * len(rows)
-        + [pl.BlockSpec((None, shape[1], block), lambda j: (expert, 0, j)), whole],
+        line_specs(rows, wide)
+        + [pl.BlockSpec((None, shape[1], wide), lambda j: (expert, 0, j)), whole],
         [jax.ShapeDtypeStruct(shape, BF), jax.ShapeDtypeStruct((1, shape[0]), F32)],
         [whole, pl.BlockSpec((1, shape[0]), lambda j: (0, 0))],
         (2,), 0.1, scratch=[pltpu.VMEM(shape, F32)],
     )
 
 
-def down_kernel(pieces, before, saved_t, *refs):
-    rows, out = refs[:pieces], refs[-1]
-    total = dot(saved_t[...], lines_of(rows))
-    if before:
-        total = total + refs[pieces][...]
-    out[...] = total.astype(out.dtype)
-
-
-def down(token, saved_t, rows, width, expert=None, before=None, result=None):
+def down_kernel(pieces, saved_t, *refs):
+    refs[pieces][...] = dot(saved_t[...], lines_of(refs[:pieces]))
+
+
+def down(token, saved_t, rows, width):
     hidden = saved_t.shape[0]
-    block = width // 2
-    column = pl.BlockSpec((hidden, block), lambda j: (0, j))
-    in_specs = [pl.BlockSpec(saved_t.shape, lambda j: (0, 0)), *[pl.BlockSpec((rows[0].shape[0], block), lambda j: (0, j))] * len(rows)]
-    args = [saved_t, *rows]
-    if before is not None:
-        in_specs.append(column)
-        args.append(before)
-    aliases = {}
-    if result is not None:
-        in_specs.append(pl.BlockSpec(memory_space=pl.ANY))
-        args.append(result)
-        aliases = {len(args) - 1: 0}
-    if expert is None:
-        out_shape, out_spec = jax.ShapeDtypeStruct((hidden, width), F32), column
+    wide = width // 2
+    (out,), token = call(
+        functools.partial(down_kernel, len(rows)), token, [saved_t, *rows],
+        [pl.BlockSpec(saved_t.shape, lambda j: (0, 0)), *line_specs(rows, wide)],
+        [jax.ShapeDtypeStruct((hidden, width), F32)],
+        [pl.BlockSpec((hidden, wide), lambda j: (0, j))], (2,), 0.1,
+    )
+    return out, token
+
+
+def distant_kernel(last, rows, weight, saved_t, before, *refs):
+    if last:
+        so_far, saved, _, out, hidden, terms, total = refs
     else:
-        out_shape = jax.ShapeDtypeStruct((2, hidden, width), BF)
-        out_spec = pl.BlockSpec((None, hidden, block), lambda j: (expert, 0, j))
-    (out,), token = call(
-        functools.partial(down_kernel, len(rows), before is not None), token, args,
-        in_specs, [out_shape], [out_spec], (2,), 0.1, aliases=aliases,
-    )
-    return out, token
-
-
-def finish_kernel(scalars, hidden0, near, distant, out):
-    z = pl.program_id(0)
-    step = (scalars[0] + 4 - z) & 3
-    begin = pl.multiple_of(jnp.where(step == 3, 2, step & 1) * 320, 320)
-    out[1] = jnp.where(step == 2, distant[...], near[pl.ds(begin, 320), :])
-    row = lax.broadcasted_iota(I32, (160, 1), 0)
-    plane, place = row // CAP, row % CAP
-    source = lax.broadcasted_iota(I32, (160, 640), 1)
-    line = jnp.where(place < 8, z * 8 + place, 24 + z * 2 + place)
-    hit = (source == plane * 40 + line).astype(F32).astype(BF)
-    for half in range(2):
-        rows = dot(hit, hidden0[half * 640 : half * 640 + 640, :])
-        out[0, half * 160 : half * 160 + 160, :] = rows.astype(BF)
-
-
-def finish(token, scalars, *args):
-    rows, hidden = args[0].shape
-    (out,), token = call(
-        finish_kernel, token, args, [pl.BlockSpec(x.shape, lambda j, s: (0, 0)) for x in args],
-        [jax.ShapeDtypeStruct((2, rows, hidden), BF)],
-        [pl.BlockSpec((2, rows // 4, hidden), lambda j, s: (0, j, 0))],
-        (4,), 0.1, scalars=scalars,
-    )
-    return out
+        out, total = refs
+    out[...] = (dot(saved_t[...], rows[...]) + before[...]).astype(BF)
+
+    @pl.when(pl.program_id(0) == 0)
+    def _():
+        total[...] = so_far[...] if last else jnp.zeros_like(total)
+
+    total[...] += lax.dot_general(
+        rows[...], weight[...], (((1,), (1,)), ((), ())), preferred_element_type=F32
+    )
+    if last:
+        pl.when(pl.program_id(0) == 1)(functools.partial(close, total, saved, hidden, terms))
+
+
+def distant_rows(token, rows, weight, saved, saved_t, before, earlier=None):
+    size, wide = rows.shape
+    hidden = saved.shape[1]
+    block = wide // 2
+    last = earlier is not None
+    side = 2 * last
+    whole = pl.BlockSpec(saved.shape, lambda j: (0, 0))
+    out = jax.ShapeDtypeStruct((2, hidden, 2 * wide), BF)
+    total = jax.ShapeDtypeStruct(saved.shape, F32)
+    args = [rows, weight, saved_t, before]
+    specs = [
+        pl.BlockSpec((size, block), lambda j: (0, j)),
+        pl.BlockSpec((None, hidden, block), lambda j: (1, 0, j + side)),
+        pl.BlockSpec(saved_t.shape, lambda j: (0, 0)),
+        pl.BlockSpec((hidden, block), lambda j: (0, j + side)),
+    ]
+    out_specs = [pl.BlockSpec((None, hidden, block), lambda j: (1, 0, j + side))]
+    if last:
+        args += [earlier[1], saved, earlier[0]]
+        specs += [whole, whole, pl.BlockSpec(memory_space=pl.ANY)]
+        shapes = [out, jax.ShapeDtypeStruct(saved.shape, BF), jax.ShapeDtypeStruct((1, size), F32)]
+        out_specs += [whole, pl.BlockSpec((1, size), lambda j: (0, 0))]
+    else:
+        shapes = [out, total]
+        out_specs.append(whole)
+    return call(
+        functools.partial(distant_kernel, last), token, args, specs, shapes, out_specs,
+        (2,), 0.1, scratch=[pltpu.VMEM(saved.shape, F32)] if last else [],
+        aliases={6: 0} if last else {},
+    )
+
+
+def finish_kernel(scalars, saved_t, rows, hidden0, near, distant, _, down_out, hidden_out):
+    down_out[...] = dot(saved_t[...], rows[...]).astype(BF)
+
+    @pl.when(pl.program_id(0) == 0)
+    def _():
+        row = lax.broadcasted_iota(I32, (160, 1), 0)
+        plane, place = row // CAP, row % CAP
+        source = lax.broadcasted_iota(I32, (160, 640), 1)
+        for z in range(4):
+            line = jnp.where(place < 8, z * 8 + place, 24 + z * 2 + place)
+            hit = (source == plane * 40 + line).astype(F32).astype(BF)
+            for half in range(2):
+                lines = dot(hit, hidden0[half * 640 : half * 640 + 640, :])
+                at = z * 320 + half * 160
+                hidden_out[0, at : at + 160, :] = lines.astype(BF)
+        for at, step in enumerate(STEPS):
+            begin = pl.multiple_of(((scalars[0] + 4 - step) & 3) * 320, 320)
+            hidden_out[1, pl.ds(begin, 320), :] = (
+                near[at * 320 : at * 320 + 320, :] if at < 3 else distant[...]
+            )
+
+
+def finish(token, scalars, saved_t, rows, hidden0, near, distant, result):
+    count, width = rows.shape
+    hidden = saved_t.shape[0]
+    wide = width // 2
+    args = [saved_t, rows, hidden0, near, distant, result]
+    specs = [pl.BlockSpec(x.shape, lambda j, s: (0, 0)) for x in args[:-1]]
+    specs[1] = pl.BlockSpec((count, wide), lambda j, s: (0, j))
+    shape = (2, count, hidden)
+    outs, _ = call(
+        finish_kernel, token, args, [*specs, pl.BlockSpec(memory_space=pl.ANY)],
+        [jax.ShapeDtypeStruct(result.shape, BF), jax.ShapeDtypeStruct(shape, BF)],
+        [
+            pl.BlockSpec((None, hidden, wide), lambda j, s: (0, 0, j)),
+            pl.BlockSpec(shape, lambda j, s: (0, 0, 0)),
+        ],
+        (2,), 0.1, scalars=scalars, aliases={len(args): 0},
+    )
+    return outs
 
 
 def shards(grad_out, gates, routes, w_down, saved_hidden):
@@ -398,8 +472,9 @@
     from_down, from_up = z_shift(grad_out, 1), z_shift(grad_out, -1)
     slots = (routes.T, gates.T)
     other = core_swap(grad_out)
-    (matrix1, table, meta), token = first_picker(scalars, *slots, *[core_swap(x) for x in slots])
-    send1, token = pick(token, matrix1, [grad_out, other], wide)
+    (send1, table, meta), token = first_pick(
+        scalars, slots, [core_swap(x) for x in slots], grad_out, other
+    )
     got1 = lax.all_to_all(send1.reshape(16, 40, width), ("y", "x"), 0, 0, tiled=True)
     got1 = got1.reshape(640, width)
 
@@ -416,17 +491,22 @@
     (away, send0), token = part(token, scalars, got1, send0)
     rows0 = lax.all_to_all(send0, PLANE, 0, 0, tiled=True).reshape(1280, width)
     near = [z_shift(away, 1), z_shift(away, -1)]
-    (own,), token = part(token, scalars, got1, None, near)
-    near = [own, *near]
-    distant = [z_shift(own, 2)]
+    own, token = part(token, scalars, got1)
+    own, token = hold(token, own, near)
+    near = [*own, *near]
+    distant = [z_shift(half, 2) for half in own]
 
     (hidden_near, terms_near), token = back(token, near, w_down, saved_near, 1)
     before, token = down(token, saved_near_t, near, width)
+    more = (w_down, saved_distant, saved_distant_t, before)
+    earlier, token = distant_rows(token, distant[0], *more)
+    (d_down, hidden_distant, terms_distant), token = distant_rows(
+        token, distant[1], *more, earlier
+    )
     (hidden0, terms0), token = back(token, [rows0], w_down, saved0, 0)
-    (hidden_distant, terms_distant), token = back(token, distant, w_down, saved_distant, 1)
-    d_down, token = down(token, saved_distant_t, distant, width, 1, before)
-    d_down, token = down(token, saved0_t, [rows0], width, 0, None, d_down)
-    d_hidden = finish(token, scalars, hidden0, hidden_near, hidden_distant)
+    d_down, d_hidden = finish(
+        token, scalars, saved0_t, rows0, hidden0, hidden_near, hidden_distant, d_down
+    )
 
     terms_near = terms_near.reshape(3, 32, CAP)
     terms1 = jnp.stack(

time: 269 us -> 255 us (0.948)
  waiting for transfers between devices: 120 us -> 104 us
  starting transfers between devices: 36.7 us -> 39.5 us
  Pallas kernels: 99.1 us -> 96.4 us
    all_to_all x1, waiting for transfers between devices: 30.5 us -> 0.01 us  [shards(): rows0 = lax.all_to_all(send0, PLANE, 0, 0, tiled=True).reshape(1280, width)]
    ppermute x10 -> x11, waiting for transfers between devices: 83.8 us -> 101 us  [z_shift(): return lax.ppermute(value, Z, [(i, (i + step) % 4) for i in range(4)])]
    ppermute x10 -> x11, starting transfers between devices: 10.8 us -> 15.2 us  [z_shift(): return lax.ppermute(value, Z, [(i, (i + step) % 4) for i in range(4)])]
    pallas_call x15 -> x14, Pallas kernels: 99.1 us -> 96.4 us  [call(): pl.pallas_call(run, out_shape=[*out_shape, jax.ShapeDtypeStruct((8, 128),...]
    unnamed x25 -> x27, local copies, waits for them, and re-layouts: 5.3 us -> 7.02 us
  transfers between devices with their start and end apart: 16 -> 17, of which waited for: 9 -> 8; matrix products, arithmetic and copies ran while one was open for 1% -> 1% of each run, Pallas kernels for 33% -> 32%
where the time goes in v5:
time: 255 us; the launch traced here: 254 us
  waiting for transfers between devices  104 us (41%)
  Pallas kernels  96.4 us (38%)
  starting transfers between devices  39.5 us (15%)
  local copies, waits for them, and re-layouts  9.16 us (4%)
  other arithmetic  4.06 us (2%)
    ppermute x11, waiting for transfers between devices, z_shift(): return lax.ppermute(value, Z, [(i, (i + step) % 4) for i in range(4)])  101 us
    pallas_call x14, Pallas kernels, call(): pl.pallas_call(run, out_shape=[*out_shape, jax.ShapeDtypeStruct((8, 128),...  96.4 us
    ppermute x11, starting transfers between devices, z_shift(): return lax.ppermute(value, Z, [(i, (i + step) % 4) for i in range(4)])  15.2 us
    all_to_all x1, starting transfers between devices, shards(): returned = lax.all_to_all(terms, PLANE + Z, 0, 0, tiled=True)  9.03 us
    unnamed x27, local copies, waits for them, and re-layouts  7.02 us
    all_to_all x1, starting transfers between devices, shards(): lax.all_to_all(send1.reshape(16, 40, width), ('y', 'x'), 0, 0, tiled=True)  6.8 us
    all_to_all x1, starting transfers between devices, shards(): rows0 = lax.all_to_all(send0, PLANE, 0, 0, tiled=True).reshape(1280, width)  6.47 us
  transfers between devices with their start and end apart: 17, of which 8 were waited for; matrix products, arithmetic and copies ran while one was open for 1% of the time, Pallas kernels for 32%

profile of v5, /device:TPU:1, one launch (start us, length us, event | category | flops | bytes accessed | tf_op | source)
XLA Modules:
  0.0 254.5 jit_solution(18036575839583341428)
XLA Ops:
  9.6 7.8 %shard_map.76 = (bf16[640,3584]{1,0:T(8,128)(2,1)}, s32[4,256]{1,0:T(4,128)}, f32[8,256]{1,0:T(8,128)}, f32[8,128]{1,0:T(8,128)}) custom-call(s32[3]{0:T(128)} %pad_add_fusion.refs_0_, s32[4,256]{1,0:T(4,128)} %bitcast.36, bf16[4,256]{1,0:T(4,128)(2,1)} %bitcast.34, s32[4,256]{1,0:T(4,128)} %copy-done.7, bf16[4,256]{1,0:T(4,128)(2,1)} %copy-done.9, ...), custom_call_target="tpu_custom_call" | custom-call | flops 100000000 | tf_op jit(solution)/shard_map/pallas_call | solution.py:45
  17.4 6.8 %all-to-all-start = ((bf16[16,40,3584]{2,1,0:T(8,128)(2,1)}), bf16[16,40,3584]{2,1,0:T(8,128)(2,1)}, u32[]{:S(2)}, u32[]{:S(2)}) async-start(bf16[16,40,3584]{2,1,0:T(8,128)(2,1)} %bitcast.28), calls=%async_computation | async-start | bytes 9175040 | tf_op jit(solution)/shard_map/all_to_all | solution.py:478
  24.3 22.3 %collective-permute-done.3.refs_0_.refs_4_ = bf16[256,3584]{1,0:T(8,128)(2,1)} collective-permute-done((bf16[256,3584]{1,0:T(8,128)(2,1)}, bf16[256,3584]{1,0:T(8,128)(2,1)}, u32[]{:S(2)}, u32[]{:S(2)}) %collective-permute-start.3) | collective-permute-done | bytes 1835040 | tf_op jit(solution)/shard_map/ppermute | solution.py:23
  46.6 3.0 %shard_map.77 = (bf16[256,1792]{1,0:T(8,128)(2,1)}, bf16[256,1792]{1,0:T(8,128)(2,1)}, f32[8,256]{1,0:T(8,128)}, f32[8,128]{1,0:T(8,128)}) custom-call(bf16[256,3584]{1,0:T(8,128)(2,1)} %collective-permute-done.3.refs_0_.refs_4_, bf16[256,3584]{1,0:T(8,128)(2,1)} %collective-permute-done.4.refs_1_.refs_7_, f32[8,256]{1,0:T(8,128)} %get-tuple-element.51.refs_2_, ...), custom_call_target="tpu_custom_call" | custom-call | flops 999999995904 | tf_op jit(solution)/shard_map/pallas_call | solution.py:45
  52.3 2.3 collective-permute-start.6
  55.3 7.7 %shard_map.78 = (bf16[1280,512]{1,0:T(8,128)(2,1)}, bf16[512,1280]{1,0:T(8,128)(2,1)}, bf16[960,512]{1,0:T(8,128)(2,1)}, bf16[512,960]{1,0:T(8,128)(2,1)}, bf16[...) custom-call(s32[3]{0:T(128)} %pad_add_fusion.refs_0_, bf16[2,1280,512]{2,1,0:T(8,128)(2,1)} %refs_1_.4, ...), custom_call_target="tpu_custom_call" | custom-call | flops 100000000 | tf_op jit(solution)/shard_map/pallas_call | solution.py:45
  63.0 9.6 %collective-permute-done.5.refs_2_ = f32[8,256]{1,0:T(8,128)S(1)} collective-permute-done((f32[8,256]{1,0:T(8,128)}, f32[8,256]{1,0:T(8,128)S(1)}, u32[]{:S(2)}, u32[]{:S(2)}) %collective-permute-start.5) | collective-permute-done | bytes 8224 | tf_op jit(solution)/shard_map/ppermute | solution.py:23
  73.8 4.8 %shard_map.79 = (bf16[256,1024]{1,0:T(8,128)(2,1)}, bf16[256,1024]{1,0:T(8,128)(2,1)}, f32[8,128]{1,0:T(8,128)}) custom-call(s32[3]{0:T(128)} %pad_add_fusion.refs_0_, f32[8,256]{1,0:T(8,128)} %get-tuple-element.53.refs_1_, f32[8,256]{1,0:T(8,128)} %copy-done.10, f32[8,256]{1,0:T(8,128)} %copy-done.11, f32[8,256]{1,0:T(8,128)} %copy-done.12, ...), custom_call_target="tpu_custom_call" | custom-call | flops 100000000 | tf_op jit(solution)/shard_map/pallas_call | solution.py:45
  79.9 10.4 %shard_map.80 = (bf16[32,5,8,3584]{3,2,1,0:T(8,128)(2,1)}, f32[8,128]{1,0:T(8,128)}) custom-call(s32[3]{0:T(128)} %pad_add_fusion.refs_0_, bf16[256,1024]{1,0:T(8,128)(2,1)} %get-tuple-element.56.refs_1_, bf16[256,1024]{1,0:T(8,128)(2,1)} %get-tuple-element.57.refs_2_, bf16[256,3584]{1,0:T(8,128)(2,1)} %refs_3_.1, ...), custom_call_target="tpu_custom_call" | custom-call | flops 100000000 | tf_op jit(solution)/shard_map/pallas_call | solution.py:45
  90.3 2.8 %all-to-all-done = bf16[16,40,3584]{2,1,0:T(8,128)(2,1)} async-done(((bf16[16,40,3584]{2,1,0:T(8,128)(2,1)}), bf16[16,40,3584]{2,1,0:T(8,128)(2,1)}, u32[]{:S(2)}, u32[]{:S(2)}) %all-to-all-start) | async-done | bytes 4587552 | tf_op jit(solution)/shard_map/all_to_all | solution.py:478
  93.1 4.9 %shard_map.81 = (bf16[320,3584]{1,0:T(8,128)(2,1)}, bf16[32,5,8,3584]{3,2,1,0:T(8,128)(2,1)}, f32[8,128]{1,0:T(8,128)}) custom-call(s32[3]{0:T(128)} %pad_add_fusion.refs_0_, bf16[640,3584]{1,0:T(8,128)(2,1)} %bitcast.6.refs_1_, bf16[32,5,8,3584]{3,2,1,0:T(8,128)(2,1)} %get-tuple-element.61.refs_2_, ...), custom_call_target="tpu_custom_call", output_to_operand_aliasing={{1}: (2, {})} | custom-call | flops 100000000 | tf_op jit(solution)/shard_map/pallas_call | solution.py:45
  98.0 6.5 %all-to-all-start.1 = ((bf16[32,5,8,3584]{3,2,1,0:T(8,128)(2,1)}), bf16[32,5,8,3584]{3,2,1,0:T(8,128)(2,1)}, u32[]{:S(2)}, u32[]{:S(2)}) async-start(bf16[32,5,8,3584]{3,2,1,0:T(8,128)(2,1)} %get-tuple-element.63), calls=%async_computation.1 | async-start | bytes 18350080 | tf_op jit(solution)/shard_map/all_to_all | solution.py:492
  107.2 5.2 %shard_map.82 = (bf16[320,1792]{1,0:T(8,128)(2,1)}, bf16[320,1792]{1,0:T(8,128)(2,1)}, f32[8,128]{1,0:T(8,128)}) custom-call(s32[3]{0:T(128)} %pad_add_fusion.refs_0_, bf16[640,3584]{1,0:T(8,128)(2,1)} %bitcast.6.refs_1_, f32[8,128]{1,0:T(8,128)} %get-tuple-element.65.refs_2_), custom_call_target="tpu_custom_call" | custom-call | flops 100000000 | tf_op jit(solution)/shard_map/pallas_call | solution.py:45
  112.4 44.8 %collective-permute-done.10.refs_3_.refs_2_ = bf16[320,3584]{1,0:T(8,128)(2,1)S(1)} collective-permute-done((bf16[320,3584]{1,0:T(8,128)(2,1)}, bf16[320,3584]{1,0:T(8,128)(2,1)S(1)}, u32[]{:S(2)}, u32[]{:S(2)}) %collective-permute-start.10) | collective-permute-done | bytes 2293792 | tf_op jit(solution)/shard_map/ppermute | solution.py:23
  159.5 2.7 %collective-permute-start.12 = (bf16[320,1792]{1,0:T(8,128)(2,1)}, bf16[320,1792]{1,0:T(8,128)(2,1)S(1)}, u32[]{:S(2)}, u32[]{:S(2)}) collective-permute-start(bf16[320,1792]{1,0:T(8,128)(2,1)} %get-tuple-element.70.refs_1_.refs_2_), channel_id=1, source_target_pairs={{0,64},{32,96},{64,0},{96,32},{1,65},{33,97},{65,1},{97,33},{2,66}... | collective-permute-start | bytes 3440648 | tf_op jit(solution)/shard_map/ppermute | solution.py:23
  162.2 8.8 %shard_map.84 = (bf16[960,512]{1,0:T(8,128)(2,1)}, f32[1,960]{1,0:T(1,128)}, f32[8,128]{1,0:T(8,128)}) custom-call(bf16[320,1792]{1,0:T(8,128)(2,1)} %get-tuple-element.73.refs_0_.refs_1_, bf16[320,1792]{1,0:T(8,128)(2,1)} %get-tuple-element.70.refs_1_.refs_2_, bf16[320,3584]{1,0:T(8,128)(2,1)} %copy-done, ...), custom_call_target="tpu_custom_call" | custom-call | flops 100000000 | tf_op jit(solution)/shard_map/pallas_call | solution.py:45
  172.4 8.7 %shard_map.85 = (f32[512,3584]{1,0:T(8,128)}, f32[8,128]{1,0:T(8,128)}) custom-call(bf16[512,960]{1,0:T(8,128)(2,1)} %get-tuple-element.72.refs_0_, bf16[320,1792]{1,0:T(8,128)(2,1)} %get-tuple-element.73.refs_0_.refs_1_, bf16[320,1792]{1,0:T(8,128)(2,1)} %get-tuple-element.70.refs_1_.refs_2_, bf16[320,3584]{1,0:T(8,128)(2,1)} %copy-done, ...), custom_call_target="tpu_custom_call" | custom-call | flops 100000000 | tf_op jit(solution)/shard_map/pallas_call | solution.py:45
  181.0 5.7 %collective-permute-done.13.refs_0_ = bf16[320,1792]{1,0:T(8,128)(2,1)S(1)} collective-permute-done((bf16[320,1792]{1,0:T(8,128)(2,1)}, bf16[320,1792]{1,0:T(8,128)(2,1)S(1)}, u32[]{:S(2)}, u32[]{:S(2)}) %collective-permute-start.13) | collective-permute-done | bytes 1146912 | tf_op jit(solution)/shard_map/ppermute | solution.py:23
  187.8 5.6 %shard_map.86 = (bf16[2,512,3584]{2,1,0:T(8,128)(2,1)}, f32[320,512]{1,0:T(8,128)}, f32[8,128]{1,0:T(8,128)}) custom-call(bf16[320,1792]{1,0:T(8,128)(2,1)} %copy-done.3, bf16[2,512,3584]{2,1,0:T(8,128)(2,1)} %refs_1_.7, bf16[512,320]{1,0:T(8,128)(2,1)} %get-tuple-element.71.refs_2_, f32[512,3584]{1,0:T(8,128)} %get-tuple-element.77.refs_3_, ...), custom_call_target="tpu_custom_call" | custom-call | flops 100000000 | tf_op jit(solution)/shard_map/pallas_call | solution.py:45
  193.4 17.9 %collective-permute-done.12.refs_0_ = bf16[320,1792]{1,0:T(8,128)(2,1)S(1)} collective-permute-done((bf16[320,1792]{1,0:T(8,128)(2,1)}, bf16[320,1792]{1,0:T(8,128)(2,1)S(1)}, u32[]{:S(2)}, u32[]{:S(2)}) %collective-permute-start.12) | collective-permute-done | bytes 1146912 | tf_op jit(solution)/shard_map/ppermute | solution.py:23
  212.2 6.2 %shard_map.87 = (bf16[2,512,3584]{2,1,0:T(8,128)(2,1)}, bf16[320,512]{1,0:T(8,128)(2,1)}, f32[1,320]{1,0:T(1,128)}, f32[8,128]{1,0:T(8,128)}) custom-call(bf16[320,1792]{1,0:T(8,128)(2,1)} %copy-done.2, bf16[2,512,3584]{2,1,0:T(8,128)(2,1)} %refs_1_.7, bf16[512,320]{1,0:T(8,128)(2,1)} %get-tuple-element.71.refs_2_, ...), custom_call_target="tpu_custom_call", output_to_operand_aliasing={{0}: (6, {})} | custom-call | flops 100000000 | tf_op jit(solution)/shard_map/pallas_call | solution.py:45
  219.6 10.1 %shard_map.88 = (bf16[1280,512]{1,0:T(8,128)(2,1)}, f32[1,1280]{1,0:T(1,128)}, f32[8,128]{1,0:T(8,128)}) custom-call(bf16[1280,3584]{1,0:T(8,128)(2,1)} %bitcast.7.refs_0_.refs_2_, bf16[2,512,3584]{2,1,0:T(8,128)(2,1)} %refs_1_.7, bf16[1280,512]{1,0:T(8,128)(2,1)} %get-tuple-element.64.refs_2_, f32[8,128]{1,0:T(8,128)} %get-tuple-element.83.refs_3_), custom_call_target="tpu_custom_call" | custom-call | flops 100000000 | tf_op jit(solution)/shard_map/pallas_call | solution.py:45
  231.5 9.0 %all-to-all-start.2 = ((f32[128,1,20]{2,1,0:T(1,128)}), f32[128,1,20]{2,1,0:T(1,128)S(1)}, u32[]{:S(2)}, u32[]{:S(2)}) async-start(f32[128,1,20]{2,1,0:T(1,128)} %bitcast.10), calls=%async_computation.2 | async-start | bytes 131072 | tf_op jit(solution)/shard_map/all_to_all | solution.py:523
  240.6 12.5 %shard_map.89 = (bf16[2,512,3584]{2,1,0:T(8,128)(2,1)}, bf16[2,1280,512]{2,1,0:T(8,128)(2,1)}, f32[8,128]{1,0:T(8,128)}) custom-call(s32[3]{0:T(128)} %pad_add_fusion.refs_0_, bf16[512,1280]{1,0:T(8,128)(2,1)} %get-tuple-element.87.refs_1_, bf16[1280,3584]{1,0:T(8,128)(2,1)} %bitcast.7.refs_0_.refs_2_, ...), custom_call_target="tpu_custom_call", output_to_operand_aliasing={{0}: (6, {})} | custom-call | flops 100000000 | tf_op jit(solution)/shard_map/pallas_call | solution.py:45
  (77 shorter events, 27.5 us)
Async XLA Ops:
  0.6 7.2 %collective-permute-start.2 = (bf16[256,3584]{1,0:T(8,128)(2,1)}, bf16[256,3584]{1,0:T(8,128)(2,1)S(1)}, u32[]{:S(2)}, u32[]{:S(2)}) collective-permute-start(bf16[256,3584]{1,0:T(8,128)(2,1)} %refs_3_.1), channel_id=1, source_target_pairs={{0,1},{1,0},{2,3},{3,2},{4,5},{5,4},{6,7},{7,6},{8,9},{9,8},{10,11... | collective-permute-start | bytes 5505032 | tf_op jit(solution)/shard_map/ppermute | solution.py:27
  2.1 44.5 %collective-permute-start.3 = (bf16[256,3584]{1,0:T(8,128)(2,1)}, bf16[256,3584]{1,0:T(8,128)(2,1)}, u32[]{:S(2)}, u32[]{:S(2)}) collective-permute-start(bf16[256,3584]{1,0:T(8,128)(2,1)} %refs_3_.1), channel_id=1, source_target_pairs={{0,32},{32,64},{64,96},{96,0},{1,33},{33,65},{65,97},{97,1},{2,34}... | collective-permute-start | bytes 5505032 | tf_op jit(solution)/shard_map/ppermute | solution.py:23
  3.9 42.7 %collective-permute-start.4 = (bf16[256,3584]{1,0:T(8,128)(2,1)}, bf16[256,3584]{1,0:T(8,128)(2,1)}, u32[]{:S(2)}, u32[]{:S(2)}) collective-permute-start(bf16[256,3584]{1,0:T(8,128)(2,1)} %refs_3_.1), channel_id=1, source_target_pairs={{0,96},{32,0},{64,32},{96,64},{1,97},{33,1},{65,33},{97,65},{2,98}... | collective-permute-start | bytes 5505032 | tf_op jit(solution)/shard_map/ppermute | solution.py:23
  6.0 1.8 collective-permute-start
  6.4 1.4 collective-permute-start.1
  8.4 1.2 copy-start.1
  17.4 75.6 %all-to-all-start = ((bf16[16,40,3584]{2,1,0:T(8,128)(2,1)}), bf16[16,40,3584]{2,1,0:T(8,128)(2,1)}, u32[]{:S(2)}, u32[]{:S(2)}) async-start(bf16[16,40,3584]{2,1,0:T(8,128)(2,1)} %bitcast.28), calls=%async_computation | async-start | bytes 9175040 | tf_op jit(solution)/shard_map/all_to_all | solution.py:478
  49.6 29.1 %collective-permute-start.8 = (bf16[256,1792]{1,0:T(8,128)(2,1)}, bf16[256,1792]{1,0:T(8,128)(2,1)S(1)}, u32[]{:S(2)}, u32[]{:S(2)}) collective-permute-start(bf16[256,1792]{1,0:T(8,128)(2,1)} %get-tuple-element.58), channel_id=1, source_target_pairs={{0,32},{32,64},{64,96},{96,0},{1,33},{33,65},{65,97},{97,1},{2,34}... | collective-permute-start | bytes 2752520 | tf_op jit(solution)/shard_map/ppermute | solution.py:23
  50.1 28.6 %collective-permute-start.9 = (bf16[256,1792]{1,0:T(8,128)(2,1)}, bf16[256,1792]{1,0:T(8,128)(2,1)S(1)}, u32[]{:S(2)}, u32[]{:S(2)}) collective-permute-start(bf16[256,1792]{1,0:T(8,128)(2,1)} %get-tuple-element.59), channel_id=1, source_target_pairs={{0,96},{32,0},{64,32},{96,64},{1,97},{33,1},{65,33},{97,65},{2,98}... | collective-permute-start | bytes 2752520 | tf_op jit(solution)/shard_map/ppermute | solution.py:23
  52.3 20.2 %collective-permute-start.5 = (f32[8,256]{1,0:T(8,128)}, f32[8,256]{1,0:T(8,128)S(1)}, u32[]{:S(2)}, u32[]{:S(2)}) collective-permute-start(f32[8,256]{1,0:T(8,128)} %get-tuple-element.53.refs_1_), channel_id=1, source_target_pairs={{0,32},{32,64},{64,96},{96,0},{1,33},{33,65},{65,97},{97,1},{2,34}... | collective-permute-start | bytes 24584 | tf_op jit(solution)/shard_map/ppermute | solution.py:23
  52.3 21.0 %collective-permute-start.6 = (f32[8,256]{1,0:T(8,128)}, f32[8,256]{1,0:T(8,128)S(1)}, u32[]{:S(2)}, u32[]{:S(2)}) collective-permute-start(f32[8,256]{1,0:T(8,128)} %get-tuple-element.53.refs_1_), channel_id=1, source_target_pairs={{0,64},{32,96},{64,0},{96,32},{1,65},{33,97},{65,1},{97,33},{2,66}... | collective-permute-start | bytes 24584 | tf_op jit(solution)/shard_map/ppermute | solution.py:23
  54.6 18.6 %collective-permute-start.7 = (f32[8,256]{1,0:T(8,128)}, f32[8,256]{1,0:T(8,128)S(1)}, u32[]{:S(2)}, u32[]{:S(2)}) collective-permute-start(f32[8,256]{1,0:T(8,128)} %get-tuple-element.53.refs_1_), channel_id=1, source_target_pairs={{0,96},{32,0},{64,32},{96,64},{1,97},{33,1},{65,33},{97,65},{2,98}... | collective-permute-start | bytes 24584 | tf_op jit(solution)/shard_map/ppermute | solution.py:23
  78.7 1.2 copy-start.5
  98.0 121.6 %all-to-all-start.1 = ((bf16[32,5,8,3584]{3,2,1,0:T(8,128)(2,1)}), bf16[32,5,8,3584]{3,2,1,0:T(8,128)(2,1)}, u32[]{:S(2)}, u32[]{:S(2)}) async-start(bf16[32,5,8,3584]{3,2,1,0:T(8,128)(2,1)} %get-tuple-element.63), calls=%async_computation.1 | async-start | bytes 18350080 | tf_op jit(solution)/shard_map/all_to_all | solution.py:492
  104.5 52.7 %collective-permute-start.10 = (bf16[320,3584]{1,0:T(8,128)(2,1)}, bf16[320,3584]{1,0:T(8,128)(2,1)S(1)}, u32[]{:S(2)}, u32[]{:S(2)}) collective-permute-start(bf16[320,3584]{1,0:T(8,128)(2,1)} %get-tuple-element.69), channel_id=1, source_target_pairs={{0,32},{32,64},{64,96},{96,0},{1,33},{33,65},{65,97},{97,1},{2,34}... | collective-permute-start | bytes 6881288 | tf_op jit(solution)/shard_map/ppermute | solution.py:23
  105.0 52.2 %collective-permute-start.11 = (bf16[320,3584]{1,0:T(8,128)(2,1)}, bf16[320,3584]{1,0:T(8,128)(2,1)}, u32[]{:S(2)}, u32[]{:S(2)}) collective-permute-start(bf16[320,3584]{1,0:T(8,128)(2,1)} %get-tuple-element.69), channel_id=1, source_target_pairs={{0,96},{32,0},{64,32},{96,64},{1,97},{33,1},{65,33},{97,65},{2,98}... | collective-permute-start | bytes 6881288 | tf_op jit(solution)/shard_map/ppermute | solution.py:23
  157.2 1.4 copy-start
  159.2 27.6 %collective-permute-start.13 = (bf16[320,1792]{1,0:T(8,128)(2,1)}, bf16[320,1792]{1,0:T(8,128)(2,1)S(1)}, u32[]{:S(2)}, u32[]{:S(2)}) collective-permute-start(bf16[320,1792]{1,0:T(8,128)(2,1)} %get-tuple-element.73.refs_0_.refs_1_), channel_id=1, source_target_pairs={{0,64},{32,96},{64,0},{96,32},{1,65},{33,97},{65,1},{97,33},{2,66}... | collective-permute-start | bytes 3440648 | tf_op jit(solution)/shard_map/ppermute | solution.py:23
  159.5 51.7 %collective-permute-start.12 = (bf16[320,1792]{1,0:T(8,128)(2,1)}, bf16[320,1792]{1,0:T(8,128)(2,1)S(1)}, u32[]{:S(2)}, u32[]{:S(2)}) collective-permute-start(bf16[320,1792]{1,0:T(8,128)(2,1)} %get-tuple-element.70.refs_1_.refs_2_), channel_id=1, source_target_pairs={{0,64},{32,96},{64,0},{96,32},{1,65},{33,97},{65,1},{97,33},{2,66}... | collective-permute-start | bytes 3440648 | tf_op jit(solution)/shard_map/ppermute | solution.py:23
  186.8 1.0 copy-start.3
  211.2 1.0 copy-start.2
  219.6 20.9 %copy-start.8 = (s32[4,256]{1,0:T(4,128)S(1)}, s32[4,256]{1,0:T(4,128)}, u32[]{:S(2)}) copy-start(s32[4,256]{1,0:T(4,128)} %get-tuple-element.49) | copy-start | bytes 12292
  231.5 21.6 %all-to-all-start.2 = ((f32[128,1,20]{2,1,0:T(1,128)}), f32[128,1,20]{2,1,0:T(1,128)S(1)}, u32[]{:S(2)}, u32[]{:S(2)}) async-start(f32[128,1,20]{2,1,0:T(1,128)} %bitcast.10), calls=%async_computation.2 | async-start | bytes 131072 | tf_op jit(solution)/shard_map/all_to_all | solution.py:523
  240.5 13.3 %copy-start.6 = (bf16[256,4]{0,1:T(4,128)(2,1)S(1)}, bf16[256,4]{0,1:T(4,128)(2,1)}, u32[]{:S(2)}) copy-start(bf16[256,4]{0,1:T(4,128)(2,1)} %param.6) | copy-start | bytes 6148
  (6 other events, 4.0 us)

commit v6 on v5

--- a/solution.py
+++ b/solution.py
@@ -11,6 +11,7 @@
 PLANE = ("y", "x", "core")
 ALL = ("zh", "zl", "y", "x", "core")
 CAP = 10
+LATE = 46
 TOP = 4
 STEPS = (0, 1, 3, 2)
 EXPERTS = 128
@@ -32,7 +33,7 @@
 
 
 def call(body, token, args, in_specs, out_shape, out_specs, grid, micros, scratch=(), aliases=None,
-         scalars=None, after=()):
+         scalars=None, after=(), limit=60):
     lead = 0 if scalars is None else 1
     extra = [*([] if token is None else [token]), *after]
     n_in, n_out = lead + len(args), len(out_shape)
@@ -53,7 +54,7 @@
             scratch_shapes=list(scratch),
         ),
         input_output_aliases=aliases or {},
-        compiler_params=pltpu.CompilerParams(vmem_limit_bytes=60 * 1024 * 1024),
+        compiler_params=pltpu.CompilerParams(vmem_limit_bytes=limit * 1024 * 1024),
         cost_estimate=pl.CostEstimate(
             flops=int(micros * 1e9), bytes_accessed=0, transcendentals=0
         ),
@@ -254,7 +255,7 @@
     return out, token
 
 
-def part_kernel(other, scalars, got, *refs):
+def part_kernel(other, scalars, got, out, *refs):
     picker = refs[-1]
     layer = 1 - scalars[1] if other else scalars[1]
 
@@ -264,34 +265,35 @@
         source = lax.broadcasted_iota(I32, (160, 320), 1)
         picker[...] = (source == row + (row // 20 + layer) * 20).astype(F32).astype(BF)
 
-    def write(out):
-        for half in range(2):
-            rows = dot(picker[...], got[half * 320 : half * 320 + 320, :])
-            out[half * 160 : half * 160 + 160, :] = rows.astype(BF)
-
-    if other:
-        write(refs[-3])
-    else:
-        for side in range(2):
-            pl.when(pl.program_id(0) == side)(functools.partial(write, refs[side]))
-
-
-def part(token, scalars, got, carried=None):
+    for half in range(2):
+        rows = dot(picker[...], got[half * 320 : half * 320 + 320, :])
+        out[half * 160 : half * 160 + 160, :] = rows.astype(BF)
+    if not other:
+        left, right = refs[:2]
+        wide, rest = out.shape[1], right.shape[1]
+
+        @pl.when(pl.program_id(0) == 0)
+        def _():
+            left[:, :wide] = out[...]
+
+        @pl.when(pl.program_id(0) == 1)
+        def _():
+            left[:, wide:] = out[:, : wide - rest]
+            right[...] = out[:, wide - rest :]
+
+
+def part(token, scalars, got, other):
     width = got.shape[1]
     wide = width // 2
-    if carried is None:
-        args, specs, aliases = [got], [], {}
-        shapes = [(320, wide)] * 2
-        out_specs = [pl.BlockSpec((320, wide), lambda j, s: (0, 0))] * 2
-    else:
-        args, specs, aliases = [got, carried], [pl.BlockSpec(memory_space=pl.ANY)], {2: 1}
-        shapes = [(320, width), carried.shape]
-        out_specs = [pl.BlockSpec((320, wide), lambda j, s: (0, j)), *specs]
-    return call(
-        functools.partial(part_kernel, carried is not None), token, args,
-        [pl.BlockSpec((640, wide), lambda j, s: (0, j)), *specs],
-        [jax.ShapeDtypeStruct(sh, BF) for sh in shapes], out_specs,
-        (2,), 0.1, scratch=[pltpu.VMEM((160, 320), BF)], scalars=scalars, aliases=aliases,
+    shapes = [(320, width)] + [(320, width * n // 4) for n in (3, 1)] * (not other)
+    return call(
+        functools.partial(part_kernel, other), token, [got],
+        [pl.BlockSpec((640, wide), lambda j, s: (0, j))],
+        [jax.ShapeDtypeStruct(sh, BF) for sh in shapes],
+        [pl.BlockSpec((320, wide), lambda j, s: (0, j))]
+        + [pl.BlockSpec(sh, lambda j, s: (0, 0)) for sh in shapes[1:]],
+        (2,), 0.1, scratch=[pltpu.VMEM((160, 320), BF)], scalars=scalars,
+        limit=60 if other else LATE,
     )
 
 
@@ -300,22 +302,16 @@
     return call(
         lambda *refs: None, token, carried, anywhere,
         [jax.ShapeDtypeStruct(x.shape, x.dtype) for x in carried], anywhere, (1,), 0.1,
-        aliases={n: n for n in range(len(carried))}, after=after,
+        aliases={n: n for n in range(len(carried))}, after=after, limit=LATE,
     )
 
 
 def lines_of(rows):
-    blocks = [r[...] for r in rows]
-    if len(blocks) > 1:
-        blocks = [jnp.where(pl.program_id(0) == 0, blocks[0], blocks[1]), *blocks[2:]]
-    return jnp.concatenate(blocks, axis=0)
+    return jnp.concatenate([r[...] for r in rows], axis=0)
 
 
 def line_specs(rows, wide):
-    return [
-        pl.BlockSpec((r.shape[0], wide), (lambda j: (0, 0)) if r.shape[1] == wide else (lambda j: (0, j)))
-        for r in rows
-    ]
+    return [pl.BlockSpec((r.shape[0], wide), lambda j: (0, j)) for r in rows]
 
 
 def close(total, saved, hidden, terms):
@@ -348,7 +344,7 @@
         + [pl.BlockSpec((None, shape[1], wide), lambda j: (expert, 0, j)), whole],
         [jax.ShapeDtypeStruct(shape, BF), jax.ShapeDtypeStruct((1, shape[0]), F32)],
         [whole, pl.BlockSpec((1, shape[0]), lambda j: (0, 0))],
-        (2,), 0.1, scratch=[pltpu.VMEM(shape, F32)],
+        (2,), 0.1, limit=LATE, scratch=[pltpu.VMEM(shape, F32)],
     )
 
 
@@ -363,7 +359,7 @@
         functools.partial(down_kernel, len(rows)), token, [saved_t, *rows],
         [pl.BlockSpec(saved_t.shape, lambda j: (0, 0)), *line_specs(rows, wide)],
         [jax.ShapeDtypeStruct((hidden, width), F32)],
-        [pl.BlockSpec((hidden, wide), lambda j: (0, j))], (2,), 0.1,
+        [pl.BlockSpec((hidden, wide), lambda j: (0, j))], (2,), 0.1, limit=LATE,
     )
     return out, token
 
@@ -383,17 +379,16 @@
         rows[...], weight[...], (((1,), (1,)), ((), ())), preferred_element_type=F32
     )
     if last:
-        pl.when(pl.program_id(0) == 1)(functools.partial(close, total, saved, hidden, terms))
+        close(total, saved, hidden, terms)
 
 
 def distant_rows(token, rows, weight, saved, saved_t, before, earlier=None):
-    size, wide = rows.shape
-    hidden = saved.shape[1]
-    block = wide // 2
+    (hidden, width), size = before.shape, rows.shape[0]
+    block = width // 4
     last = earlier is not None
-    side = 2 * last
+    side = 3 * last
     whole = pl.BlockSpec(saved.shape, lambda j: (0, 0))
-    out = jax.ShapeDtypeStruct((2, hidden, 2 * wide), BF)
+    out = jax.ShapeDtypeStruct((2, hidden, width), BF)
     total = jax.ShapeDtypeStruct(saved.shape, F32)
     args = [rows, weight, saved_t, before]
     specs = [
@@ -413,7 +408,7 @@
         out_specs.append(whole)
     return call(
         functools.partial(distant_kernel, last), token, args, specs, shapes, out_specs,
-        (2,), 0.1, scratch=[pltpu.VMEM(saved.shape, F32)] if last else [],
+        (rows.shape[1] // block,), 0.1, limit=LATE, scratch=[pltpu.VMEM(saved.shape, F32)] if last else [],
         aliases={6: 0} if last else {},
     )
 
@@ -488,13 +483,13 @@
     send0, token = line_pick(
         token, scalars, matrices, grad_out, from_down, far, from_up, width // 4
     )
-    (away, send0), token = part(token, scalars, got1, send0)
+    (away,), token = part(token, scalars, got1, True)
     rows0 = lax.all_to_all(send0, PLANE, 0, 0, tiled=True).reshape(1280, width)
     near = [z_shift(away, 1), z_shift(away, -1)]
-    own, token = part(token, scalars, got1)
-    own, token = hold(token, own, near)
-    near = [*own, *near]
-    distant = [z_shift(half, 2) for half in own]
+    (own, *own_parts), token = part(token, scalars, got1, False)
+    own_parts, token = hold(token, own_parts, near)
+    near = [own, *near]
+    distant = [z_shift(x, 2) for x in own_parts]
 
     (hidden_near, terms_near), token = back(token, near, w_down, saved_near, 1)
     before, token = down(token, saved_near_t, near, width)

time: 255 us -> 252 us (0.988)
  local copies, waits for them, and re-layouts: 9.16 us -> 18.1 us
  Pallas kernels: 96.4 us -> 89.5 us
  waiting for transfers between devices: 104 us -> 99.4 us
    unnamed x27 -> x53, local copies, waits for them, and re-layouts: 7.02 us -> 16.7 us
    pallas_call x14, Pallas kernels: 96.4 us -> 89.5 us  [call(): pl.pallas_call(run, out_shape=[*out_shape, jax.ShapeDtypeStruct((8, 128),...]
    ppermute x11, waiting for transfers between devices: 101 us -> 95.9 us  [z_shift(): return lax.ppermute(value, Z, [(i, (i + step) % 4) for i in range(4)])]
where the time goes in v6:
time: 252 us; the launch traced here: 251 us
  waiting for transfers between devices  99.4 us (39%)
  Pallas kernels  89.5 us (36%)
  starting transfers between devices  40.9 us (16%)
  local copies, waits for them, and re-layouts  18.1 us (7%)
  other arithmetic  2.72 us (1%)
    ppermute x11, waiting for transfers between devices, z_shift(): return lax.ppermute(value, Z, [(i, (i + step) % 4) for i in range(4)])  95.9 us
    pallas_call x14, Pallas kernels, call(): pl.pallas_call(run, out_shape=[*out_shape, jax.ShapeDtypeStruct((8, 128),...  89.5 us
    unnamed x53, local copies, waits for them, and re-layouts  16.7 us
    ppermute x11, starting transfers between devices, z_shift(): return lax.ppermute(value, Z, [(i, (i + step) % 4) for i in range(4)])  15.2 us
    all_to_all x1, starting transfers between devices, shards(): returned = lax.all_to_all(terms, PLANE + Z, 0, 0, tiled=True)  10.4 us
    all_to_all x1, starting transfers between devices, shards(): lax.all_to_all(send1.reshape(16, 40, width), ('y', 'x'), 0, 0, tiled=True)  6.8 us
    all_to_all x1, starting transfers between devices, shards(): rows0 = lax.all_to_all(send0, PLANE, 0, 0, tiled=True).reshape(1280, width)  6.47 us
  transfers between devices with their start and end apart: 17, of which 8 were waited for; matrix products, arithmetic and copies ran while one was open for 1% of the time, Pallas kernels for 32%

profile of v6, /device:TPU:1, one launch (start us, length us, event | category | flops | bytes accessed | tf_op | source)
XLA Modules:
  0.0 251.4 jit_solution(16940218920955646210)
XLA Ops:
  9.6 7.8 %shard_map.76 = (bf16[640,3584]{1,0:T(8,128)(2,1)}, s32[4,256]{1,0:T(4,128)}, f32[8,256]{1,0:T(8,128)}, f32[8,128]{1,0:T(8,128)}) custom-call(s32[3]{0:T(128)} %pad_add_fusion.refs_0_, s32[4,256]{1,0:T(4,128)} %bitcast.36, bf16[4,256]{1,0:T(4,128)(2,1)} %bitcast.34, s32[4,256]{1,0:T(4,128)} %copy-done.20, bf16[4,256]{1,0:T(4,128)(2,1)} %copy-done.22, ...), custom_call_target="tpu_custom_call" | custom-call | flops 100000000 | tf_op jit(solution)/shard_map/pallas_call | solution.py:46
  17.4 6.8 %all-to-all-start.1 = ((bf16[16,40,3584]{2,1,0:T(8,128)(2,1)}), bf16[16,40,3584]{2,1,0:T(8,128)(2,1)}, u32[]{:S(2)}, u32[]{:S(2)}) async-start(bf16[16,40,3584]{2,1,0:T(8,128)(2,1)} %bitcast.28), calls=%async_computation.1 | async-start | bytes 9175040 | tf_op jit(solution)/shard_map/all_to_all | solution.py:473
  24.3 22.3 %collective-permute-done.3.refs_0_.refs_4_ = bf16[256,3584]{1,0:T(8,128)(2,1)} collective-permute-done((bf16[256,3584]{1,0:T(8,128)(2,1)}, bf16[256,3584]{1,0:T(8,128)(2,1)}, u32[]{:S(2)}, u32[]{:S(2)}) %collective-permute-start.3) | collective-permute-done | bytes 1835040 | tf_op jit(solution)/shard_map/ppermute | solution.py:24
  46.6 3.0 %shard_map.77 = (bf16[256,1792]{1,0:T(8,128)(2,1)}, bf16[256,1792]{1,0:T(8,128)(2,1)}, f32[8,256]{1,0:T(8,128)}, f32[8,128]{1,0:T(8,128)}) custom-call(bf16[256,3584]{1,0:T(8,128)(2,1)} %collective-permute-done.3.refs_0_.refs_4_, bf16[256,3584]{1,0:T(8,128)(2,1)} %collective-permute-done.4.refs_1_.refs_7_, f32[8,256]{1,0:T(8,128)} %get-tuple-element.50.refs_2_, ...), custom_call_target="tpu_custom_call" | custom-call | flops 999999995904 | tf_op jit(solution)/shard_map/pallas_call | solution.py:46
  50.1 2.2 collective-permute-start.9
  52.3 2.3 collective-permute-start.6
  55.3 7.7 %shard_map.78 = (bf16[1280,512]{1,0:T(8,128)(2,1)}, bf16[512,1280]{1,0:T(8,128)(2,1)}, bf16[960,512]{1,0:T(8,128)(2,1)}, bf16[512,960]{1,0:T(8,128)(2,1)}, bf16[...) custom-call(s32[3]{0:T(128)} %pad_add_fusion.refs_0_, bf16[2,1280,512]{2,1,0:T(8,128)(2,1)} %refs_1_.4, ...), custom_call_target="tpu_custom_call" | custom-call | flops 100000000 | tf_op jit(solution)/shard_map/pallas_call | solution.py:46
  63.0 9.5 %collective-permute-done.5.refs_2_ = f32[8,256]{1,0:T(8,128)S(1)} collective-permute-done((f32[8,256]{1,0:T(8,128)}, f32[8,256]{1,0:T(8,128)S(1)}, u32[]{:S(2)}, u32[]{:S(2)}) %collective-permute-start.5) | collective-permute-done | bytes 8224 | tf_op jit(solution)/shard_map/ppermute | solution.py:24
  73.8 4.8 %shard_map.79 = (bf16[256,1024]{1,0:T(8,128)(2,1)}, bf16[256,1024]{1,0:T(8,128)(2,1)}, f32[8,128]{1,0:T(8,128)}) custom-call(s32[3]{0:T(128)} %pad_add_fusion.refs_0_, f32[8,256]{1,0:T(8,128)} %get-tuple-element.52.refs_1_, f32[8,256]{1,0:T(8,128)} %copy-done.23, f32[8,256]{1,0:T(8,128)} %copy-done.24, f32[8,256]{1,0:T(8,128)} %copy-done.25, ...), custom_call_target="tpu_custom_call" | custom-call | flops 100000000 | tf_op jit(solution)/shard_map/pallas_call | solution.py:46
  79.9 10.4 %shard_map.80 = (bf16[32,5,8,3584]{3,2,1,0:T(8,128)(2,1)}, f32[8,128]{1,0:T(8,128)}) custom-call(s32[3]{0:T(128)} %pad_add_fusion.refs_0_, bf16[256,1024]{1,0:T(8,128)(2,1)} %get-tuple-element.55.refs_1_, bf16[256,1024]{1,0:T(8,128)(2,1)} %get-tuple-element.56.refs_2_, bf16[256,3584]{1,0:T(8,128)(2,1)} %refs_3_.2, ...), custom_call_target="tpu_custom_call" | custom-call | flops 100000000 | tf_op jit(solution)/shard_map/pallas_call | solution.py:46
  90.4 2.7 %all-to-all-done.1 = bf16[16,40,3584]{2,1,0:T(8,128)(2,1)} async-done(((bf16[16,40,3584]{2,1,0:T(8,128)(2,1)}), bf16[16,40,3584]{2,1,0:T(8,128)(2,1)}, u32[]{:S(2)}, u32[]{:S(2)}) %all-to-all-start.1) | async-done | bytes 4587552 | tf_op jit(solution)/shard_map/all_to_all | solution.py:473
  93.1 6.5 %all-to-all-start = ((bf16[32,5,8,3584]{3,2,1,0:T(8,128)(2,1)}), bf16[32,5,8,3584]{3,2,1,0:T(8,128)(2,1)}, u32[]{:S(2)}, u32[]{:S(2)}) async-start(bf16[32,5,8,3584]{3,2,1,0:T(8,128)(2,1)} %get-tuple-element.60), calls=%async_computation | async-start | bytes 18350080 | tf_op jit(solution)/shard_map/all_to_all | solution.py:487
  99.6 5.0 %shard_map.81 = (bf16[320,3584]{1,0:T(8,128)(2,1)}, f32[8,128]{1,0:T(8,128)}) custom-call(s32[3]{0:T(128)} %pad_add_fusion.refs_0_, bf16[640,3584]{1,0:T(8,128)(2,1)} %bitcast.7.refs_1_, f32[8,128]{1,0:T(8,128)} %get-tuple-element.63.refs_2_), custom_call_target="tpu_custom_call" | custom-call | flops 100000000 | tf_op jit(solution)/shard_map/pallas_call | solution.py:46
  107.9 5.5 %shard_map.82 = (bf16[320,3584]{1,0:T(8,128)(2,1)S(1)}, bf16[320,2688]{1,0:T(8,128)(2,1)}, bf16[320,896]{1,0:T(8,128)(2,1)}, f32[8,128]{1,0:T(8,128)S(1)}) custom-call(s32[3]{0:T(128)S(1)} %copy-done.13, bf16[640,3584]{1,0:T(8,128)(2,1)} %bitcast.7.refs_1_, f32[8,128]{1,0:T(8,128)S(1)} %copy-done.15), custom_call_target="tpu_custom_call" | custom-call | flops 100000000 | tf_op jit(solution)/shard_map/pallas_call | solution.py:46
  114.8 42.4 %collective-permute-done.10.refs_3_.refs_1_.refs_2_ = bf16[320,3584]{1,0:T(8,128)(2,1)S(1)} collective-permute-done((bf16[320,3584]{1,0:T(8,128)(2,1)}, bf16[320,3584]{1,0:T(8,128)(2,1)S(1)}, u32[]{:S(2)}, u32[]{:S(2)}) %collective-permute-start.10) | collective-permute-done | bytes 2293792 | tf_op jit(solution)/shard_map/ppermute | solution.py:24
  164.4 6.5 %shard_map.84 = (bf16[960,512]{1,0:T(8,128)(2,1)S(1)}, f32[1,960]{1,0:T(1,128)S(1)}, f32[8,128]{1,0:T(8,128)S(1)}) custom-call(bf16[320,3584]{1,0:T(8,128)(2,1)S(1)} %copy-done.3, bf16[320,3584]{1,0:T(8,128)(2,1)S(1)} %collective-permute-done.10.refs_3_.refs_1_.refs_2_, bf16[320,3584]{1,0:T(8,128)(2,1)} %copy-done, bf16[2,512,3584]{2,1,0:T(8,128)(2,1)} %refs_1_.7, ...), custom_call_target="tpu_custom_call" | custom-call | flops 100000000 | tf_op jit(solution)/shard_map/pallas_call | solution.py:46
  175.9 6.5 %shard_map.85 = (f32[512,3584]{1,0:T(8,128)}, f32[8,128]{1,0:T(8,128)S(1)}) custom-call(bf16[512,960]{1,0:T(8,128)(2,1)S(1)} %copy-done.8, bf16[320,3584]{1,0:T(8,128)(2,1)S(1)} %copy-done.4, bf16[320,3584]{1,0:T(8,128)(2,1)S(1)} %collective-permute-done.10.refs_3_.refs_1_.refs_2_, bf16[320,3584]{1,0:T(8,128)(2,1)S(1)} %copy-done.1, ...), custom_call_target="tpu_custom_call" | custom-call | flops 100000000 | tf_op jit(solution)/shard_map/pallas_call | solution.py:46
  182.4 16.0 %collective-permute-done.13.refs_0_ = bf16[320,2688]{1,0:T(8,128)(2,1)} collective-permute-done((bf16[320,2688]{1,0:T(8,128)(2,1)}, bf16[320,2688]{1,0:T(8,128)(2,1)}, u32[]{:S(2)}, u32[]{:S(2)}) %collective-permute-start.13) | collective-permute-done | bytes 1720352 | tf_op jit(solution)/shard_map/ppermute | solution.py:24
  198.4 7.3 %shard_map.86 = (bf16[2,512,3584]{2,1,0:T(8,128)(2,1)}, f32[320,512]{1,0:T(8,128)S(1)}, f32[8,128]{1,0:T(8,128)S(1)}) custom-call(bf16[320,2688]{1,0:T(8,128)(2,1)} %collective-permute-done.13.refs_0_, bf16[2,512,3584]{2,1,0:T(8,128)(2,1)} %refs_1_.7, bf16[512,320]{1,0:T(8,128)(2,1)S(1)} %copy-done.5, f32[512,3584]{1,0:T(8,128)} %get-tuple-element.76.refs_3_, ...), custom_call_target="tpu_custom_call" | custom-call | flops 100000000 | tf_op jit(solution)/shard_map/pallas_call | solution.py:46
  205.8 4.9 %collective-permute-done.12.refs_0_ = bf16[320,896]{1,0:T(8,128)(2,1)} collective-permute-done((bf16[320,896]{1,0:T(8,128)(2,1)}, bf16[320,896]{1,0:T(8,128)(2,1)}, u32[]{:S(2)}, u32[]{:S(2)}) %collective-permute-start.12) | collective-permute-done | bytes 573472 | tf_op jit(solution)/shard_map/ppermute | solution.py:24
  210.7 3.6 %shard_map.87 = (bf16[2,512,3584]{2,1,0:T(8,128)(2,1)}, bf16[320,512]{1,0:T(8,128)(2,1)S(1)}, f32[1,320]{1,0:T(1,128)S(1)}, f32[8,128]{1,0:T(8,128)S(1)}) custom-call(bf16[320,896]{1,0:T(8,128)(2,1)} %collective-permute-done.12.refs_0_, bf16[2,512,3584]{2,1,0:T(8,128)(2,1)} %refs_1_.7, ...), custom_call_target="tpu_custom_call", output_to_operand_aliasing={{0}: (6, {})} | custom-call | flops 100000000 | tf_op jit(solution)/shard_map/pallas_call | solution.py:46
  215.6 8.7 %shard_map.88 = (bf16[1280,512]{1,0:T(8,128)(2,1)S(1)}, f32[1,1280]{1,0:T(1,128)S(1)}, f32[8,128]{1,0:T(8,128)S(1)}) custom-call(bf16[1280,3584]{1,0:T(8,128)(2,1)} %bitcast.5.refs_0_.refs_2_, bf16[2,512,3584]{2,1,0:T(8,128)(2,1)} %refs_1_.7, bf16[1280,512]{1,0:T(8,128)(2,1)S(1)} %copy-done.6, f32[8,128]{1,0:T(8,128)S(1)} %get-tuple-element.83.refs_3_), custom_call_target="tpu_custom_call" | custom-call | flops 100000000 | tf_op jit(solution)/shard_map/pallas_call | solution.py:46
  227.0 10.4 %all-to-all-start.2 = ((f32[128,1,20]{2,1,0:T(1,128)}), f32[128,1,20]{2,1,0:T(1,128)S(1)}, u32[]{:S(2)}, u32[]{:S(2)}) async-start(f32[128,1,20]{2,1,0:T(1,128)} %bitcast.10), calls=%async_computation.2 | async-start | bytes 131072 | tf_op jit(solution)/shard_map/all_to_all | solution.py:518
  237.5 12.5 %shard_map.89 = (bf16[2,512,3584]{2,1,0:T(8,128)(2,1)}, bf16[2,1280,512]{2,1,0:T(8,128)(2,1)}, f32[8,128]{1,0:T(8,128)}) custom-call(s32[3]{0:T(128)} %pad_add_fusion.refs_0_, bf16[512,1280]{1,0:T(8,128)(2,1)} %get-tuple-element.87.refs_1_, bf16[1280,3584]{1,0:T(8,128)(2,1)} %bitcast.5.refs_0_.refs_2_, ...), custom_call_target="tpu_custom_call", output_to_operand_aliasing={{0}: (6, {})} | custom-call | flops 100000000 | tf_op jit(solution)/shard_map/pallas_call | solution.py:46
  (103 shorter events, 34.9 us)
Async XLA Ops:
  0.6 7.2 %collective-permute-start.2 = (bf16[256,3584]{1,0:T(8,128)(2,1)}, bf16[256,3584]{1,0:T(8,128)(2,1)S(1)}, u32[]{:S(2)}, u32[]{:S(2)}) collective-permute-start(bf16[256,3584]{1,0:T(8,128)(2,1)} %refs_3_.2), channel_id=1, source_target_pairs={{0,1},{1,0},{2,3},{3,2},{4,5},{5,4},{6,7},{7,6},{8,9},{9,8},{10,11... | collective-permute-start | bytes 5505032 | tf_op jit(solution)/shard_map/ppermute | solution.py:28
  2.1 44.5 %collective-permute-start.3 = (bf16[256,3584]{1,0:T(8,128)(2,1)}, bf16[256,3584]{1,0:T(8,128)(2,1)}, u32[]{:S(2)}, u32[]{:S(2)}) collective-permute-start(bf16[256,3584]{1,0:T(8,128)(2,1)} %refs_3_.2), channel_id=1, source_target_pairs={{0,32},{32,64},{64,96},{96,0},{1,33},{33,65},{65,97},{97,1},{2,34}... | collective-permute-start | bytes 5505032 | tf_op jit(solution)/shard_map/ppermute | solution.py:24
  3.9 42.7 %collective-permute-start.4 = (bf16[256,3584]{1,0:T(8,128)(2,1)}, bf16[256,3584]{1,0:T(8,128)(2,1)}, u32[]{:S(2)}, u32[]{:S(2)}) collective-permute-start(bf16[256,3584]{1,0:T(8,128)(2,1)} %refs_3_.2), channel_id=1, source_target_pairs={{0,96},{32,0},{64,32},{96,64},{1,97},{33,1},{65,33},{97,65},{2,98}... | collective-permute-start | bytes 5505032 | tf_op jit(solution)/shard_map/ppermute | solution.py:24
  6.0 1.8 collective-permute-start
  6.4 1.4 collective-permute-start.1
  17.4 75.6 %all-to-all-start.1 = ((bf16[16,40,3584]{2,1,0:T(8,128)(2,1)}), bf16[16,40,3584]{2,1,0:T(8,128)(2,1)}, u32[]{:S(2)}, u32[]{:S(2)}) async-start(bf16[16,40,3584]{2,1,0:T(8,128)(2,1)} %bitcast.28), calls=%async_computation.1 | async-start | bytes 9175040 | tf_op jit(solution)/shard_map/all_to_all | solution.py:473
  49.6 29.0 %collective-permute-start.8 = (bf16[256,1792]{1,0:T(8,128)(2,1)}, bf16[256,1792]{1,0:T(8,128)(2,1)S(1)}, u32[]{:S(2)}, u32[]{:S(2)}) collective-permute-start(bf16[256,1792]{1,0:T(8,128)(2,1)} %get-tuple-element.57), channel_id=1, source_target_pairs={{0,32},{32,64},{64,96},{96,0},{1,33},{33,65},{65,97},{97,1},{2,34}... | collective-permute-start | bytes 2752520 | tf_op jit(solution)/shard_map/ppermute | solution.py:24
  50.1 28.6 %collective-permute-start.9 = (bf16[256,1792]{1,0:T(8,128)(2,1)}, bf16[256,1792]{1,0:T(8,128)(2,1)S(1)}, u32[]{:S(2)}, u32[]{:S(2)}) collective-permute-start(bf16[256,1792]{1,0:T(8,128)(2,1)} %get-tuple-element.58), channel_id=1, source_target_pairs={{0,96},{32,0},{64,32},{96,64},{1,97},{33,1},{65,33},{97,65},{2,98}... | collective-permute-start | bytes 2752520 | tf_op jit(solution)/shard_map/ppermute | solution.py:24
  52.3 20.2 %collective-permute-start.5 = (f32[8,256]{1,0:T(8,128)}, f32[8,256]{1,0:T(8,128)S(1)}, u32[]{:S(2)}, u32[]{:S(2)}) collective-permute-start(f32[8,256]{1,0:T(8,128)} %get-tuple-element.52.refs_1_), channel_id=1, source_target_pairs={{0,32},{32,64},{64,96},{96,0},{1,33},{33,65},{65,97},{97,1},{2,34}... | collective-permute-start | bytes 24584 | tf_op jit(solution)/shard_map/ppermute | solution.py:24
  52.3 21.0 %collective-permute-start.6 = (f32[8,256]{1,0:T(8,128)}, f32[8,256]{1,0:T(8,128)S(1)}, u32[]{:S(2)}, u32[]{:S(2)}) collective-permute-start(f32[8,256]{1,0:T(8,128)} %get-tuple-element.52.refs_1_), channel_id=1, source_target_pairs={{0,64},{32,96},{64,0},{96,32},{1,65},{33,97},{65,1},{97,33},{2,66}... | collective-permute-start | bytes 24584 | tf_op jit(solution)/shard_map/ppermute | solution.py:24
  54.6 18.6 %collective-permute-start.7 = (f32[8,256]{1,0:T(8,128)}, f32[8,256]{1,0:T(8,128)S(1)}, u32[]{:S(2)}, u32[]{:S(2)}) collective-permute-start(f32[8,256]{1,0:T(8,128)} %get-tuple-element.52.refs_1_), channel_id=1, source_target_pairs={{0,96},{32,0},{64,32},{96,64},{1,97},{33,1},{65,33},{97,65},{2,98}... | collective-permute-start | bytes 24584 | tf_op jit(solution)/shard_map/ppermute | solution.py:24
  93.1 122.5 %all-to-all-start = ((bf16[32,5,8,3584]{3,2,1,0:T(8,128)(2,1)}), bf16[32,5,8,3584]{3,2,1,0:T(8,128)(2,1)}, u32[]{:S(2)}, u32[]{:S(2)}) async-start(bf16[32,5,8,3584]{3,2,1,0:T(8,128)(2,1)} %get-tuple-element.60), calls=%async_computation | async-start | bytes 18350080 | tf_op jit(solution)/shard_map/all_to_all | solution.py:487
  99.6 7.7 %copy-start.13 = (s32[3]{0:T(128)S(1)}, s32[3]{0:T(128)}, u32[]{:S(2)}) copy-start(s32[3]{0:T(128)} %pad_add_fusion.refs_0_) | copy-start | bytes 40
  104.5 52.7 %collective-permute-start.10 = (bf16[320,3584]{1,0:T(8,128)(2,1)}, bf16[320,3584]{1,0:T(8,128)(2,1)S(1)}, u32[]{:S(2)}, u32[]{:S(2)}) collective-permute-start(bf16[320,3584]{1,0:T(8,128)(2,1)} %get-tuple-element.68), channel_id=1, source_target_pairs={{0,32},{32,64},{64,96},{96,0},{1,33},{33,65},{65,97},{97,1},{2,34}... | collective-permute-start | bytes 6881288 | tf_op jit(solution)/shard_map/ppermute | solution.py:24
  105.1 52.2 %collective-permute-start.11 = (bf16[320,3584]{1,0:T(8,128)(2,1)}, bf16[320,3584]{1,0:T(8,128)(2,1)S(1)}, u32[]{:S(2)}, u32[]{:S(2)}) collective-permute-start(bf16[320,3584]{1,0:T(8,128)(2,1)} %get-tuple-element.68), channel_id=1, source_target_pairs={{0,96},{32,0},{64,32},{96,64},{1,97},{33,1},{65,33},{97,65},{2,98}... | collective-permute-start | bytes 6881288 | tf_op jit(solution)/shard_map/ppermute | solution.py:24
  158.6 39.8 %collective-permute-start.13 = (bf16[320,2688]{1,0:T(8,128)(2,1)}, bf16[320,2688]{1,0:T(8,128)(2,1)}, u32[]{:S(2)}, u32[]{:S(2)}) collective-permute-start(bf16[320,2688]{1,0:T(8,128)(2,1)} %get-tuple-element.77), channel_id=1, source_target_pairs={{0,64},{32,96},{64,0},{96,32},{1,65},{33,97},{65,1},{97,33},{2,66}... | collective-permute-start | bytes 5160968 | tf_op jit(solution)/shard_map/ppermute | solution.py:24
  159.9 50.8 %collective-permute-start.12 = (bf16[320,896]{1,0:T(8,128)(2,1)}, bf16[320,896]{1,0:T(8,128)(2,1)}, u32[]{:S(2)}, u32[]{:S(2)}) collective-permute-start(bf16[320,896]{1,0:T(8,128)(2,1)} %get-tuple-element.69), channel_id=1, source_target_pairs={{0,64},{32,96},{64,0},{96,32},{1,65},{33,97},{65,1},{97,33},{2,66}... | collective-permute-start | bytes 1720328 | tf_op jit(solution)/shard_map/ppermute | solution.py:24
  164.4 8.1 %copy-start.8 = (bf16[512,960]{1,0:T(8,128)(2,1)S(1)}, bf16[512,960]{1,0:T(8,128)(2,1)}, u32[]{:S(2)}) copy-start(bf16[512,960]{1,0:T(8,128)(2,1)} %get-tuple-element.71.refs_0_) | copy-start | bytes 2949124
  175.9 22.6 %copy-start.5 = (bf16[512,320]{1,0:T(8,128)(2,1)S(1)}, bf16[512,320]{1,0:T(8,128)(2,1)}, u32[]{:S(2)}) copy-start(bf16[512,320]{1,0:T(8,128)(2,1)} %get-tuple-element.70.refs_2_) | copy-start | bytes 983044
  198.4 12.3 %copy-start.11 = (bf16[320,512]{1,0:T(8,128)(2,1)S(1)}, bf16[320,512]{1,0:T(8,128)(2,1)}, u32[]{:S(2)}) copy-start(bf16[320,512]{1,0:T(8,128)(2,1)} %get-tuple-element.80.refs_5_) | copy-start | bytes 983044
  210.7 4.8 %copy-start.6 = (bf16[1280,512]{1,0:T(8,128)(2,1)S(1)}, bf16[1280,512]{1,0:T(8,128)(2,1)}, u32[]{:S(2)}) copy-start(bf16[1280,512]{1,0:T(8,128)(2,1)} %get-tuple-element.61.refs_2_) | copy-start | bytes 3932164
  215.6 21.9 %copy-start.21 = (s32[4,256]{1,0:T(4,128)S(1)}, s32[4,256]{1,0:T(4,128)}, u32[]{:S(2)}) copy-start(s32[4,256]{1,0:T(4,128)} %get-tuple-element.49) | copy-start | bytes 12292
  227.0 23.0 %all-to-all-start.2 = ((f32[128,1,20]{2,1,0:T(1,128)}), f32[128,1,20]{2,1,0:T(1,128)S(1)}, u32[]{:S(2)}, u32[]{:S(2)}) async-start(f32[128,1,20]{2,1,0:T(1,128)} %bitcast.10), calls=%async_computation.2 | async-start | bytes 131072 | tf_op jit(solution)/shard_map/all_to_all | solution.py:518
  237.4 13.3 %copy-start.19 = (bf16[256,4]{0,1:T(4,128)(2,1)S(1)}, bf16[256,4]{0,1:T(4,128)(2,1)}, u32[]{:S(2)}) copy-start(bf16[256,4]{0,1:T(4,128)(2,1)} %param.6) | copy-start | bytes 6148
  (19 other events, 19.5 us)

commit v7 on v6

--- a/solution.py
+++ b/solution.py
@@ -174,7 +174,7 @@
 
 def first_pick(scalars, slots, slots_other, tokens, tokens_other):
     count, width = tokens.shape
-    wide = width // 2
+    wide = width // 4
     small = [*slots, *slots_other]
     shapes = [((640, width), BF), ((TOP, count), I32), ((2 * TOP, count), F32)]
     return call(
@@ -184,7 +184,7 @@
         [jax.ShapeDtypeStruct(*sh) for sh in shapes],
         [pl.BlockSpec((640, wide), lambda j, s: (0, j))]
         + [pl.BlockSpec(sh[0], lambda j, s: (0, 0)) for sh in shapes[1:]],
-        (2,), 0.1, scratch=[pltpu.VMEM((640, 2 * count), BF)], scalars=scalars,
+        (4,), 0.1, scratch=[pltpu.VMEM((640, 2 * count), BF)], scalars=scalars,
     )
 
 
@@ -415,24 +415,22 @@
 
 def finish_kernel(scalars, saved_t, rows, hidden0, near, distant, _, down_out, hidden_out):
     down_out[...] = dot(saved_t[...], rows[...]).astype(BF)
-
-    @pl.when(pl.program_id(0) == 0)
-    def _():
-        row = lax.broadcasted_iota(I32, (160, 1), 0)
-        plane, place = row // CAP, row % CAP
-        source = lax.broadcasted_iota(I32, (160, 640), 1)
-        for z in range(4):
-            line = jnp.where(place < 8, z * 8 + place, 24 + z * 2 + place)
-            hit = (source == plane * 40 + line).astype(F32).astype(BF)
-            for half in range(2):
-                lines = dot(hit, hidden0[half * 640 : half * 640 + 640, :])
-                at = z * 320 + half * 160
-                hidden_out[0, at : at + 160, :] = lines.astype(BF)
-        for at, step in enumerate(STEPS):
-            begin = pl.multiple_of(((scalars[0] + 4 - step) & 3) * 320, 320)
-            hidden_out[1, pl.ds(begin, 320), :] = (
-                near[at * 320 : at * 320 + 320, :] if at < 3 else distant[...]
-            )
+    row = lax.broadcasted_iota(I32, (160, 1), 0)
+    plane, place = row // CAP, row % CAP
+    source = lax.broadcasted_iota(I32, (160, 640), 1)
+    for side in range(2):
+        z = 2 * pl.program_id(0) + side
+        step = (scalars[0] + 4 - z) & 3
+        begin = pl.multiple_of(jnp.where(step == 3, 2, step & 1) * 320, 320)
+        hidden_out[1, side * 320 : side * 320 + 320, :] = jnp.where(
+            step == 2, distant[...], near[pl.ds(begin, 320), :]
+        )
+        line = jnp.where(place < 8, z * 8 + place, 24 + z * 2 + place)
+        hit = (source == plane * 40 + line).astype(F32).astype(BF)
+        for half in range(2):
+            lines = dot(hit, hidden0[half * 640 : half * 640 + 640, :])
+            at = side * 320 + half * 160
+            hidden_out[0, at : at + 160, :] = lines.astype(BF)
 
 
 def finish(token, scalars, saved_t, rows, hidden0, near, distant, result):
@@ -448,7 +446,7 @@
         [jax.ShapeDtypeStruct(result.shape, BF), jax.ShapeDtypeStruct(shape, BF)],
         [
             pl.BlockSpec((None, hidden, wide), lambda j, s: (0, 0, j)),
-            pl.BlockSpec(shape, lambda j, s: (0, 0, 0)),
+            pl.BlockSpec((2, count // 2, hidden), lambda j, s: (0, j, 0)),
         ],
         (2,), 0.1, scalars=scalars, aliases={len(args): 0},
     )

time: 252 us -> 252 us (level)
  no operation moved by 1% of the time
where the time goes in v7:
time: 252 us
  waiting for transfers between devices  99.4 us (39%)
  Pallas kernels  89.6 us (36%)
  starting transfers between devices  40.9 us (16%)
  local copies, waits for them, and re-layouts  18.1 us (7%)
  other arithmetic  2.72 us (1%)
    ppermute x11, waiting for transfers between devices, z_shift(): return lax.ppermute(value, Z, [(i, (i + step) % 4) for i in range(4)])  95.1 us
    pallas_call x14, Pallas kernels, call(): pl.pallas_call(run, out_shape=[*out_shape, jax.ShapeDtypeStruct((8, 128),...  89.6 us
    unnamed x53, local copies, waits for them, and re-layouts  16.7 us
    ppermute x11, starting transfers between devices, z_shift(): return lax.ppermute(value, Z, [(i, (i + step) % 4) for i in range(4)])  15.2 us
    all_to_all x1, starting transfers between devices, shards(): returned = lax.all_to_all(terms, PLANE + Z, 0, 0, tiled=True)  10.4 us
    all_to_all x1, starting transfers between devices, shards(): lax.all_to_all(send1.reshape(16, 40, width), ('y', 'x'), 0, 0, tiled=True)  6.8 us
    all_to_all x1, starting transfers between devices, shards(): rows0 = lax.all_to_all(send0, PLANE, 0, 0, tiled=True).reshape(1280, width)  6.47 us
  transfers between devices with their start and end apart: 17, of which 8 were waited for; matrix products, arithmetic and copies ran while one was open for 1% of the time, Pallas kernels for 32%

profile of v7, /device:TPU:1, one launch (start us, length us, event | category | flops | bytes accessed | tf_op | source)
XLA Modules:
  0.0 251.6 jit_solution(10440325750077703462)
XLA Ops:
  9.6 8.6 %shard_map.76 = (bf16[640,3584]{1,0:T(8,128)(2,1)}, s32[4,256]{1,0:T(4,128)}, f32[8,256]{1,0:T(8,128)}, f32[8,128]{1,0:T(8,128)}) custom-call(s32[3]{0:T(128)} %pad_add_fusion.refs_0_, s32[4,256]{1,0:T(4,128)} %bitcast.36, bf16[4,256]{1,0:T(4,128)(2,1)} %bitcast.34, s32[4,256]{1,0:T(4,128)} %copy-done.20, bf16[4,256]{1,0:T(4,128)(2,1)} %copy-done.22, ...), custom_call_target="tpu_custom_call" | custom-call | flops 100000000 | tf_op jit(solution)/shard_map/pallas_call | solution.py:46
  18.2 6.8 %all-to-all-start.1 = ((bf16[16,40,3584]{2,1,0:T(8,128)(2,1)}), bf16[16,40,3584]{2,1,0:T(8,128)(2,1)}, u32[]{:S(2)}, u32[]{:S(2)}) async-start(bf16[16,40,3584]{2,1,0:T(8,128)(2,1)} %bitcast.28), calls=%async_computation.1 | async-start | bytes 9175040 | tf_op jit(solution)/shard_map/all_to_all | solution.py:471
  25.1 21.5 %collective-permute-done.3.refs_0_.refs_4_ = bf16[256,3584]{1,0:T(8,128)(2,1)} collective-permute-done((bf16[256,3584]{1,0:T(8,128)(2,1)}, bf16[256,3584]{1,0:T(8,128)(2,1)}, u32[]{:S(2)}, u32[]{:S(2)}) %collective-permute-start.3) | collective-permute-done | bytes 1835040 | tf_op jit(solution)/shard_map/ppermute | solution.py:24
  46.6 3.0 %shard_map.77 = (bf16[256,1792]{1,0:T(8,128)(2,1)}, bf16[256,1792]{1,0:T(8,128)(2,1)}, f32[8,256]{1,0:T(8,128)}, f32[8,128]{1,0:T(8,128)}) custom-call(bf16[256,3584]{1,0:T(8,128)(2,1)} %collective-permute-done.3.refs_0_.refs_4_, bf16[256,3584]{1,0:T(8,128)(2,1)} %collective-permute-done.4.refs_1_.refs_7_, f32[8,256]{1,0:T(8,128)} %get-tuple-element.50.refs_2_, ...), custom_call_target="tpu_custom_call" | custom-call | flops 999999995904 | tf_op jit(solution)/shard_map/pallas_call | solution.py:46
  52.3 2.3 collective-permute-start.6
  55.3 7.7 %shard_map.78 = (bf16[1280,512]{1,0:T(8,128)(2,1)}, bf16[512,1280]{1,0:T(8,128)(2,1)}, bf16[960,512]{1,0:T(8,128)(2,1)}, bf16[512,960]{1,0:T(8,128)(2,1)}, bf16[...) custom-call(s32[3]{0:T(128)} %pad_add_fusion.refs_0_, bf16[2,1280,512]{2,1,0:T(8,128)(2,1)} %refs_1_.4, ...), custom_call_target="tpu_custom_call" | custom-call | flops 100000000 | tf_op jit(solution)/shard_map/pallas_call | solution.py:46
  63.0 9.5 %collective-permute-done.5.refs_2_ = f32[8,256]{1,0:T(8,128)S(1)} collective-permute-done((f32[8,256]{1,0:T(8,128)}, f32[8,256]{1,0:T(8,128)S(1)}, u32[]{:S(2)}, u32[]{:S(2)}) %collective-permute-start.5) | collective-permute-done | bytes 8224 | tf_op jit(solution)/shard_map/ppermute | solution.py:24
  73.8 4.8 %shard_map.79 = (bf16[256,1024]{1,0:T(8,128)(2,1)}, bf16[256,1024]{1,0:T(8,128)(2,1)}, f32[8,128]{1,0:T(8,128)}) custom-call(s32[3]{0:T(128)} %pad_add_fusion.refs_0_, f32[8,256]{1,0:T(8,128)} %get-tuple-element.52.refs_1_, f32[8,256]{1,0:T(8,128)} %copy-done.23, f32[8,256]{1,0:T(8,128)} %copy-done.24, f32[8,256]{1,0:T(8,128)} %copy-done.25, ...), custom_call_target="tpu_custom_call" | custom-call | flops 100000000 | tf_op jit(solution)/shard_map/pallas_call | solution.py:46
  79.9 10.4 %shard_map.80 = (bf16[32,5,8,3584]{3,2,1,0:T(8,128)(2,1)}, f32[8,128]{1,0:T(8,128)}) custom-call(s32[3]{0:T(128)} %pad_add_fusion.refs_0_, bf16[256,1024]{1,0:T(8,128)(2,1)} %get-tuple-element.55.refs_1_, bf16[256,1024]{1,0:T(8,128)(2,1)} %get-tuple-element.56.refs_2_, bf16[256,3584]{1,0:T(8,128)(2,1)} %refs_3_.2, ...), custom_call_target="tpu_custom_call" | custom-call | flops 100000000 | tf_op jit(solution)/shard_map/pallas_call | solution.py:46
  90.4 3.5 %all-to-all-done.1 = bf16[16,40,3584]{2,1,0:T(8,128)(2,1)} async-done(((bf16[16,40,3584]{2,1,0:T(8,128)(2,1)}), bf16[16,40,3584]{2,1,0:T(8,128)(2,1)}, u32[]{:S(2)}, u32[]{:S(2)}) %all-to-all-start.1) | async-done | bytes 4587552 | tf_op jit(solution)/shard_map/all_to_all | solution.py:471
  93.9 6.5 %all-to-all-start = ((bf16[32,5,8,3584]{3,2,1,0:T(8,128)(2,1)}), bf16[32,5,8,3584]{3,2,1,0:T(8,128)(2,1)}, u32[]{:S(2)}, u32[]{:S(2)}) async-start(bf16[32,5,8,3584]{3,2,1,0:T(8,128)(2,1)} %get-tuple-element.60), calls=%async_computation | async-start | bytes 18350080 | tf_op jit(solution)/shard_map/all_to_all | solution.py:485
  100.4 5.0 %shard_map.81 = (bf16[320,3584]{1,0:T(8,128)(2,1)}, f32[8,128]{1,0:T(8,128)}) custom-call(s32[3]{0:T(128)} %pad_add_fusion.refs_0_, bf16[640,3584]{1,0:T(8,128)(2,1)} %bitcast.7.refs_1_, f32[8,128]{1,0:T(8,128)} %get-tuple-element.63.refs_2_), custom_call_target="tpu_custom_call" | custom-call | flops 100000000 | tf_op jit(solution)/shard_map/pallas_call | solution.py:46
  105.3 2.7 %collective-permute-start.11 = (bf16[320,3584]{1,0:T(8,128)(2,1)}, bf16[320,3584]{1,0:T(8,128)(2,1)S(1)}, u32[]{:S(2)}, u32[]{:S(2)}) collective-permute-start(bf16[320,3584]{1,0:T(8,128)(2,1)} %get-tuple-element.68), channel_id=1, source_target_pairs={{0,96},{32,0},{64,32},{96,64},{1,97},{33,1},{65,33},{97,65},{2,98}... | collective-permute-start | bytes 6881288 | tf_op jit(solution)/shard_map/ppermute | solution.py:24
  108.7 5.5 %shard_map.82 = (bf16[320,3584]{1,0:T(8,128)(2,1)S(1)}, bf16[320,2688]{1,0:T(8,128)(2,1)}, bf16[320,896]{1,0:T(8,128)(2,1)}, f32[8,128]{1,0:T(8,128)S(1)}) custom-call(s32[3]{0:T(128)S(1)} %copy-done.13, bf16[640,3584]{1,0:T(8,128)(2,1)} %bitcast.7.refs_1_, f32[8,128]{1,0:T(8,128)S(1)} %copy-done.15), custom_call_target="tpu_custom_call" | custom-call | flops 100000000 | tf_op jit(solution)/shard_map/pallas_call | solution.py:46
  115.6 42.4 %collective-permute-done.10.refs_3_.refs_1_.refs_2_ = bf16[320,3584]{1,0:T(8,128)(2,1)S(1)} collective-permute-done((bf16[320,3584]{1,0:T(8,128)(2,1)}, bf16[320,3584]{1,0:T(8,128)(2,1)S(1)}, u32[]{:S(2)}, u32[]{:S(2)}) %collective-permute-start.10) | collective-permute-done | bytes 2293792 | tf_op jit(solution)/shard_map/ppermute | solution.py:24
  165.2 6.5 %shard_map.84 = (bf16[960,512]{1,0:T(8,128)(2,1)S(1)}, f32[1,960]{1,0:T(1,128)S(1)}, f32[8,128]{1,0:T(8,128)S(1)}) custom-call(bf16[320,3584]{1,0:T(8,128)(2,1)S(1)} %copy-done.3, bf16[320,3584]{1,0:T(8,128)(2,1)S(1)} %collective-permute-done.10.refs_3_.refs_1_.refs_2_, bf16[320,3584]{1,0:T(8,128)(2,1)} %copy-done, bf16[2,512,3584]{2,1,0:T(8,128)(2,1)} %refs_1_.7, ...), custom_call_target="tpu_custom_call" | custom-call | flops 100000000 | tf_op jit(solution)/shard_map/pallas_call | solution.py:46
  176.7 6.5 %shard_map.85 = (f32[512,3584]{1,0:T(8,128)}, f32[8,128]{1,0:T(8,128)S(1)}) custom-call(bf16[512,960]{1,0:T(8,128)(2,1)S(1)} %copy-done.8, bf16[320,3584]{1,0:T(8,128)(2,1)S(1)} %copy-done.4, bf16[320,3584]{1,0:T(8,128)(2,1)S(1)} %collective-permute-done.10.refs_3_.refs_1_.refs_2_, bf16[320,3584]{1,0:T(8,128)(2,1)S(1)} %copy-done.1, ...), custom_call_target="tpu_custom_call" | custom-call | flops 100000000 | tf_op jit(solution)/shard_map/pallas_call | solution.py:46
  183.2 16.0 %collective-permute-done.13.refs_0_ = bf16[320,2688]{1,0:T(8,128)(2,1)} collective-permute-done((bf16[320,2688]{1,0:T(8,128)(2,1)}, bf16[320,2688]{1,0:T(8,128)(2,1)}, u32[]{:S(2)}, u32[]{:S(2)}) %collective-permute-start.13) | collective-permute-done | bytes 1720352 | tf_op jit(solution)/shard_map/ppermute | solution.py:24
  199.2 7.3 %shard_map.86 = (bf16[2,512,3584]{2,1,0:T(8,128)(2,1)}, f32[320,512]{1,0:T(8,128)S(1)}, f32[8,128]{1,0:T(8,128)S(1)}) custom-call(bf16[320,2688]{1,0:T(8,128)(2,1)} %collective-permute-done.13.refs_0_, bf16[2,512,3584]{2,1,0:T(8,128)(2,1)} %refs_1_.7, bf16[512,320]{1,0:T(8,128)(2,1)S(1)} %copy-done.5, f32[512,3584]{1,0:T(8,128)} %get-tuple-element.76.refs_3_, ...), custom_call_target="tpu_custom_call" | custom-call | flops 100000000 | tf_op jit(solution)/shard_map/pallas_call | solution.py:46
  206.6 4.9 %collective-permute-done.12.refs_0_ = bf16[320,896]{1,0:T(8,128)(2,1)} collective-permute-done((bf16[320,896]{1,0:T(8,128)(2,1)}, bf16[320,896]{1,0:T(8,128)(2,1)}, u32[]{:S(2)}, u32[]{:S(2)}) %collective-permute-start.12) | collective-permute-done | bytes 573472 | tf_op jit(solution)/shard_map/ppermute | solution.py:24
  211.5 3.6 %shard_map.87 = (bf16[2,512,3584]{2,1,0:T(8,128)(2,1)}, bf16[320,512]{1,0:T(8,128)(2,1)S(1)}, f32[1,320]{1,0:T(1,128)S(1)}, f32[8,128]{1,0:T(8,128)S(1)}) custom-call(bf16[320,896]{1,0:T(8,128)(2,1)} %collective-permute-done.12.refs_0_, bf16[2,512,3584]{2,1,0:T(8,128)(2,1)} %refs_1_.7, ...), custom_call_target="tpu_custom_call", output_to_operand_aliasing={{0}: (6, {})} | custom-call | flops 100000000 | tf_op jit(solution)/shard_map/pallas_call | solution.py:46
  216.4 8.7 %shard_map.88 = (bf16[1280,512]{1,0:T(8,128)(2,1)S(1)}, f32[1,1280]{1,0:T(1,128)S(1)}, f32[8,128]{1,0:T(8,128)S(1)}) custom-call(bf16[1280,3584]{1,0:T(8,128)(2,1)} %bitcast.5.refs_0_.refs_2_, bf16[2,512,3584]{2,1,0:T(8,128)(2,1)} %refs_1_.7, bf16[1280,512]{1,0:T(8,128)(2,1)S(1)} %copy-done.6, f32[8,128]{1,0:T(8,128)S(1)} %get-tuple-element.83.refs_3_), custom_call_target="tpu_custom_call" | custom-call | flops 100000000 | tf_op jit(solution)/shard_map/pallas_call | solution.py:46
  227.8 10.4 %all-to-all-start.2 = ((f32[128,1,20]{2,1,0:T(1,128)}), f32[128,1,20]{2,1,0:T(1,128)S(1)}, u32[]{:S(2)}, u32[]{:S(2)}) async-start(f32[128,1,20]{2,1,0:T(1,128)} %bitcast.10), calls=%async_computation.2 | async-start | bytes 131072 | tf_op jit(solution)/shard_map/all_to_all | solution.py:516
  238.3 11.9 %shard_map.89 = (bf16[2,512,3584]{2,1,0:T(8,128)(2,1)}, bf16[2,1280,512]{2,1,0:T(8,128)(2,1)}, f32[8,128]{1,0:T(8,128)}) custom-call(s32[3]{0:T(128)} %pad_add_fusion.refs_0_, bf16[512,1280]{1,0:T(8,128)(2,1)} %get-tuple-element.87.refs_1_, bf16[1280,3584]{1,0:T(8,128)(2,1)} %bitcast.5.refs_0_.refs_2_, ...), custom_call_target="tpu_custom_call", output_to_operand_aliasing={{0}: (6, {})} | custom-call | flops 100000000 | tf_op jit(solution)/shard_map/pallas_call | solution.py:46
  (103 shorter events, 34.4 us)
Async XLA Ops:
  0.6 7.2 %collective-permute-start.2 = (bf16[256,3584]{1,0:T(8,128)(2,1)}, bf16[256,3584]{1,0:T(8,128)(2,1)S(1)}, u32[]{:S(2)}, u32[]{:S(2)}) collective-permute-start(bf16[256,3584]{1,0:T(8,128)(2,1)} %refs_3_.2), channel_id=1, source_target_pairs={{0,1},{1,0},{2,3},{3,2},{4,5},{5,4},{6,7},{7,6},{8,9},{9,8},{10,11... | collective-permute-start | bytes 5505032 | tf_op jit(solution)/shard_map/ppermute | solution.py:28
  2.1 44.5 %collective-permute-start.3 = (bf16[256,3584]{1,0:T(8,128)(2,1)}, bf16[256,3584]{1,0:T(8,128)(2,1)}, u32[]{:S(2)}, u32[]{:S(2)}) collective-permute-start(bf16[256,3584]{1,0:T(8,128)(2,1)} %refs_3_.2), channel_id=1, source_target_pairs={{0,32},{32,64},{64,96},{96,0},{1,33},{33,65},{65,97},{97,1},{2,34}... | collective-permute-start | bytes 5505032 | tf_op jit(solution)/shard_map/ppermute | solution.py:24
  3.9 42.7 %collective-permute-start.4 = (bf16[256,3584]{1,0:T(8,128)(2,1)}, bf16[256,3584]{1,0:T(8,128)(2,1)}, u32[]{:S(2)}, u32[]{:S(2)}) collective-permute-start(bf16[256,3584]{1,0:T(8,128)(2,1)} %refs_3_.2), channel_id=1, source_target_pairs={{0,96},{32,0},{64,32},{96,64},{1,97},{33,1},{65,33},{97,65},{2,98}... | collective-permute-start | bytes 5505032 | tf_op jit(solution)/shard_map/ppermute | solution.py:24
  6.0 1.8 collective-permute-start
  6.4 1.4 collective-permute-start.1
  18.2 75.6 %all-to-all-start.1 = ((bf16[16,40,3584]{2,1,0:T(8,128)(2,1)}), bf16[16,40,3584]{2,1,0:T(8,128)(2,1)}, u32[]{:S(2)}, u32[]{:S(2)}) async-start(bf16[16,40,3584]{2,1,0:T(8,128)(2,1)} %bitcast.28), calls=%async_computation.1 | async-start | bytes 9175040 | tf_op jit(solution)/shard_map/all_to_all | solution.py:471
  49.6 29.0 %collective-permute-start.8 = (bf16[256,1792]{1,0:T(8,128)(2,1)}, bf16[256,1792]{1,0:T(8,128)(2,1)S(1)}, u32[]{:S(2)}, u32[]{:S(2)}) collective-permute-start(bf16[256,1792]{1,0:T(8,128)(2,1)} %get-tuple-element.57), channel_id=1, source_target_pairs={{0,32},{32,64},{64,96},{96,0},{1,33},{33,65},{65,97},{97,1},{2,34}... | collective-permute-start | bytes 2752520 | tf_op jit(solution)/shard_map/ppermute | solution.py:24
  50.1 28.6 %collective-permute-start.9 = (bf16[256,1792]{1,0:T(8,128)(2,1)}, bf16[256,1792]{1,0:T(8,128)(2,1)S(1)}, u32[]{:S(2)}, u32[]{:S(2)}) collective-permute-start(bf16[256,1792]{1,0:T(8,128)(2,1)} %get-tuple-element.58), channel_id=1, source_target_pairs={{0,96},{32,0},{64,32},{96,64},{1,97},{33,1},{65,33},{97,65},{2,98}... | collective-permute-start | bytes 2752520 | tf_op jit(solution)/shard_map/ppermute | solution.py:24
  52.3 20.2 %collective-permute-start.5 = (f32[8,256]{1,0:T(8,128)}, f32[8,256]{1,0:T(8,128)S(1)}, u32[]{:S(2)}, u32[]{:S(2)}) collective-permute-start(f32[8,256]{1,0:T(8,128)} %get-tuple-element.52.refs_1_), channel_id=1, source_target_pairs={{0,32},{32,64},{64,96},{96,0},{1,33},{33,65},{65,97},{97,1},{2,34}... | collective-permute-start | bytes 24584 | tf_op jit(solution)/shard_map/ppermute | solution.py:24
  52.3 21.0 %collective-permute-start.6 = (f32[8,256]{1,0:T(8,128)}, f32[8,256]{1,0:T(8,128)S(1)}, u32[]{:S(2)}, u32[]{:S(2)}) collective-permute-start(f32[8,256]{1,0:T(8,128)} %get-tuple-element.52.refs_1_), channel_id=1, source_target_pairs={{0,64},{32,96},{64,0},{96,32},{1,65},{33,97},{65,1},{97,33},{2,66}... | collective-permute-start | bytes 24584 | tf_op jit(solution)/shard_map/ppermute | solution.py:24
  54.6 18.6 %collective-permute-start.7 = (f32[8,256]{1,0:T(8,128)}, f32[8,256]{1,0:T(8,128)S(1)}, u32[]{:S(2)}, u32[]{:S(2)}) collective-permute-start(f32[8,256]{1,0:T(8,128)} %get-tuple-element.52.refs_1_), channel_id=1, source_target_pairs={{0,96},{32,0},{64,32},{96,64},{1,97},{33,1},{65,33},{97,65},{2,98}... | collective-permute-start | bytes 24584 | tf_op jit(solution)/shard_map/ppermute | solution.py:24
  93.9 122.5 %all-to-all-start = ((bf16[32,5,8,3584]{3,2,1,0:T(8,128)(2,1)}), bf16[32,5,8,3584]{3,2,1,0:T(8,128)(2,1)}, u32[]{:S(2)}, u32[]{:S(2)}) async-start(bf16[32,5,8,3584]{3,2,1,0:T(8,128)(2,1)} %get-tuple-element.60), calls=%async_computation | async-start | bytes 18350080 | tf_op jit(solution)/shard_map/all_to_all | solution.py:485
  100.4 7.7 %copy-start.13 = (s32[3]{0:T(128)S(1)}, s32[3]{0:T(128)}, u32[]{:S(2)}) copy-start(s32[3]{0:T(128)} %pad_add_fusion.refs_0_) | copy-start | bytes 40
  105.3 52.7 %collective-permute-start.10 = (bf16[320,3584]{1,0:T(8,128)(2,1)}, bf16[320,3584]{1,0:T(8,128)(2,1)S(1)}, u32[]{:S(2)}, u32[]{:S(2)}) collective-permute-start(bf16[320,3584]{1,0:T(8,128)(2,1)} %get-tuple-element.68), channel_id=1, source_target_pairs={{0,32},{32,64},{64,96},{96,0},{1,33},{33,65},{65,97},{97,1},{2,34}... | collective-permute-start | bytes 6881288 | tf_op jit(solution)/shard_map/ppermute | solution.py:24
  105.3 52.7 %collective-permute-start.11 = (bf16[320,3584]{1,0:T(8,128)(2,1)}, bf16[320,3584]{1,0:T(8,128)(2,1)S(1)}, u32[]{:S(2)}, u32[]{:S(2)}) collective-permute-start(bf16[320,3584]{1,0:T(8,128)(2,1)} %get-tuple-element.68), channel_id=1, source_target_pairs={{0,96},{32,0},{64,32},{96,64},{1,97},{33,1},{65,33},{97,65},{2,98}... | collective-permute-start | bytes 6881288 | tf_op jit(solution)/shard_map/ppermute | solution.py:24
  159.4 39.8 %collective-permute-start.13 = (bf16[320,2688]{1,0:T(8,128)(2,1)}, bf16[320,2688]{1,0:T(8,128)(2,1)}, u32[]{:S(2)}, u32[]{:S(2)}) collective-permute-start(bf16[320,2688]{1,0:T(8,128)(2,1)} %get-tuple-element.77), channel_id=1, source_target_pairs={{0,64},{32,96},{64,0},{96,32},{1,65},{33,97},{65,1},{97,33},{2,66}... | collective-permute-start | bytes 5160968 | tf_op jit(solution)/shard_map/ppermute | solution.py:24
  160.7 50.8 %collective-permute-start.12 = (bf16[320,896]{1,0:T(8,128)(2,1)}, bf16[320,896]{1,0:T(8,128)(2,1)}, u32[]{:S(2)}, u32[]{:S(2)}) collective-permute-start(bf16[320,896]{1,0:T(8,128)(2,1)} %get-tuple-element.69), channel_id=1, source_target_pairs={{0,64},{32,96},{64,0},{96,32},{1,65},{33,97},{65,1},{97,33},{2,66}... | collective-permute-start | bytes 1720328 | tf_op jit(solution)/shard_map/ppermute | solution.py:24
  165.2 8.1 %copy-start.8 = (bf16[512,960]{1,0:T(8,128)(2,1)S(1)}, bf16[512,960]{1,0:T(8,128)(2,1)}, u32[]{:S(2)}) copy-start(bf16[512,960]{1,0:T(8,128)(2,1)} %get-tuple-element.71.refs_0_) | copy-start | bytes 2949124
  176.7 22.6 %copy-start.5 = (bf16[512,320]{1,0:T(8,128)(2,1)S(1)}, bf16[512,320]{1,0:T(8,128)(2,1)}, u32[]{:S(2)}) copy-start(bf16[512,320]{1,0:T(8,128)(2,1)} %get-tuple-element.70.refs_2_) | copy-start | bytes 983044
  199.2 12.3 %copy-start.11 = (bf16[320,512]{1,0:T(8,128)(2,1)S(1)}, bf16[320,512]{1,0:T(8,128)(2,1)}, u32[]{:S(2)}) copy-start(bf16[320,512]{1,0:T(8,128)(2,1)} %get-tuple-element.80.refs_5_) | copy-start | bytes 983044
  211.5 4.8 %copy-start.6 = (bf16[1280,512]{1,0:T(8,128)(2,1)S(1)}, bf16[1280,512]{1,0:T(8,128)(2,1)}, u32[]{:S(2)}) copy-start(bf16[1280,512]{1,0:T(8,128)(2,1)} %get-tuple-element.61.refs_2_) | copy-start | bytes 3932164
  216.3 21.9 %copy-start.21 = (s32[4,256]{1,0:T(4,128)S(1)}, s32[4,256]{1,0:T(4,128)}, u32[]{:S(2)}) copy-start(s32[4,256]{1,0:T(4,128)} %get-tuple-element.49) | copy-start | bytes 12292
  227.8 22.4 %all-to-all-start.2 = ((f32[128,1,20]{2,1,0:T(1,128)}), f32[128,1,20]{2,1,0:T(1,128)S(1)}, u32[]{:S(2)}, u32[]{:S(2)}) async-start(f32[128,1,20]{2,1,0:T(1,128)} %bitcast.10), calls=%async_computation.2 | async-start | bytes 131072 | tf_op jit(solution)/shard_map/all_to_all | solution.py:516
  238.2 12.7 %copy-start.19 = (bf16[256,4]{0,1:T(4,128)(2,1)S(1)}, bf16[256,4]{0,1:T(4,128)(2,1)}, u32[]{:S(2)}) copy-start(bf16[256,4]{0,1:T(4,128)(2,1)} %param.6) | copy-start | bytes 6148
  (19 other events, 19.5 us)

commit v8 on v7

--- a/solution.py
+++ b/solution.py
@@ -174,7 +174,7 @@
 
 def first_pick(scalars, slots, slots_other, tokens, tokens_other):
     count, width = tokens.shape
-    wide = width // 4
+    wide = width // 2
     small = [*slots, *slots_other]
     shapes = [((640, width), BF), ((TOP, count), I32), ((2 * TOP, count), F32)]
     return call(
@@ -184,7 +184,7 @@
         [jax.ShapeDtypeStruct(*sh) for sh in shapes],
         [pl.BlockSpec((640, wide), lambda j, s: (0, j))]
         + [pl.BlockSpec(sh[0], lambda j, s: (0, 0)) for sh in shapes[1:]],
-        (4,), 0.1, scratch=[pltpu.VMEM((640, 2 * count), BF)], scalars=scalars,
+        (2,), 0.1, scratch=[pltpu.VMEM((640, 2 * count), BF)], scalars=scalars,
     )
 
 

time: 252 us -> 252 us (level)
  no operation moved by 1% of the time
where the time goes in v8:
time: 252 us; the launch traced here: 251 us
  waiting for transfers between devices  99.4 us (39%)
  Pallas kernels  88.9 us (35%)
  starting transfers between devices  40.9 us (16%)
  local copies, waits for them, and re-layouts  18.1 us (7%)
  other arithmetic  2.72 us (1%)
    ppermute x11, waiting for transfers between devices, z_shift(): return lax.ppermute(value, Z, [(i, (i + step) % 4) for i in range(4)])  95.9 us
    pallas_call x14, Pallas kernels, call(): pl.pallas_call(run, out_shape=[*out_shape, jax.ShapeDtypeStruct((8, 128),...  88.9 us
    unnamed x53, local copies, waits for them, and re-layouts  16.7 us
    ppermute x11, starting transfers between devices, z_shift(): return lax.ppermute(value, Z, [(i, (i + step) % 4) for i in range(4)])  15.2 us
    all_to_all x1, starting transfers between devices, shards(): returned = lax.all_to_all(terms, PLANE + Z, 0, 0, tiled=True)  10.4 us
    all_to_all x1, starting transfers between devices, shards(): lax.all_to_all(send1.reshape(16, 40, width), ('y', 'x'), 0, 0, tiled=True)  6.8 us
    all_to_all x1, starting transfers between devices, shards(): rows0 = lax.all_to_all(send0, PLANE, 0, 0, tiled=True).reshape(1280, width)  6.47 us
  transfers between devices with their start and end apart: 17, of which 8 were waited for; matrix products, arithmetic and copies ran while one was open for 1% of the time, Pallas kernels for 32%

profile of v8, /device:TPU:1, one launch (start us, length us, event | category | flops | bytes accessed | tf_op | source)
XLA Modules:
  0.0 250.8 jit_solution(9506897103086791697)
XLA Ops:
  9.6 7.8 %shard_map.76 = (bf16[640,3584]{1,0:T(8,128)(2,1)}, s32[4,256]{1,0:T(4,128)}, f32[8,256]{1,0:T(8,128)}, f32[8,128]{1,0:T(8,128)}) custom-call(s32[3]{0:T(128)} %pad_add_fusion.refs_0_, s32[4,256]{1,0:T(4,128)} %bitcast.36, bf16[4,256]{1,0:T(4,128)(2,1)} %bitcast.34, s32[4,256]{1,0:T(4,128)} %copy-done.20, bf16[4,256]{1,0:T(4,128)(2,1)} %copy-done.22, ...), custom_call_target="tpu_custom_call" | custom-call | flops 100000000 | tf_op jit(solution)/shard_map/pallas_call | solution.py:46
  17.4 6.8 %all-to-all-start.1 = ((bf16[16,40,3584]{2,1,0:T(8,128)(2,1)}), bf16[16,40,3584]{2,1,0:T(8,128)(2,1)}, u32[]{:S(2)}, u32[]{:S(2)}) async-start(bf16[16,40,3584]{2,1,0:T(8,128)(2,1)} %bitcast.28), calls=%async_computation.1 | async-start | bytes 9175040 | tf_op jit(solution)/shard_map/all_to_all | solution.py:471
  24.3 22.3 %collective-permute-done.3.refs_0_.refs_4_ = bf16[256,3584]{1,0:T(8,128)(2,1)} collective-permute-done((bf16[256,3584]{1,0:T(8,128)(2,1)}, bf16[256,3584]{1,0:T(8,128)(2,1)}, u32[]{:S(2)}, u32[]{:S(2)}) %collective-permute-start.3) | collective-permute-done | bytes 1835040 | tf_op jit(solution)/shard_map/ppermute | solution.py:24
  46.6 3.0 %shard_map.77 = (bf16[256,1792]{1,0:T(8,128)(2,1)}, bf16[256,1792]{1,0:T(8,128)(2,1)}, f32[8,256]{1,0:T(8,128)}, f32[8,128]{1,0:T(8,128)}) custom-call(bf16[256,3584]{1,0:T(8,128)(2,1)} %collective-permute-done.3.refs_0_.refs_4_, bf16[256,3584]{1,0:T(8,128)(2,1)} %collective-permute-done.4.refs_1_.refs_7_, f32[8,256]{1,0:T(8,128)} %get-tuple-element.50.refs_2_, ...), custom_call_target="tpu_custom_call" | custom-call | flops 999999995904 | tf_op jit(solution)/shard_map/pallas_call | solution.py:46
  50.1 2.2 collective-permute-start.9
  52.3 2.3 collective-permute-start.6
  55.3 7.7 %shard_map.78 = (bf16[1280,512]{1,0:T(8,128)(2,1)}, bf16[512,1280]{1,0:T(8,128)(2,1)}, bf16[960,512]{1,0:T(8,128)(2,1)}, bf16[512,960]{1,0:T(8,128)(2,1)}, bf16[...) custom-call(s32[3]{0:T(128)} %pad_add_fusion.refs_0_, bf16[2,1280,512]{2,1,0:T(8,128)(2,1)} %refs_1_.4, ...), custom_call_target="tpu_custom_call" | custom-call | flops 100000000 | tf_op jit(solution)/shard_map/pallas_call | solution.py:46
  63.0 9.5 %collective-permute-done.5.refs_2_ = f32[8,256]{1,0:T(8,128)S(1)} collective-permute-done((f32[8,256]{1,0:T(8,128)}, f32[8,256]{1,0:T(8,128)S(1)}, u32[]{:S(2)}, u32[]{:S(2)}) %collective-permute-start.5) | collective-permute-done | bytes 8224 | tf_op jit(solution)/shard_map/ppermute | solution.py:24
  73.8 4.8 %shard_map.79 = (bf16[256,1024]{1,0:T(8,128)(2,1)}, bf16[256,1024]{1,0:T(8,128)(2,1)}, f32[8,128]{1,0:T(8,128)}) custom-call(s32[3]{0:T(128)} %pad_add_fusion.refs_0_, f32[8,256]{1,0:T(8,128)} %get-tuple-element.52.refs_1_, f32[8,256]{1,0:T(8,128)} %copy-done.23, f32[8,256]{1,0:T(8,128)} %copy-done.24, f32[8,256]{1,0:T(8,128)} %copy-done.25, ...), custom_call_target="tpu_custom_call" | custom-call | flops 100000000 | tf_op jit(solution)/shard_map/pallas_call | solution.py:46
  79.9 10.4 %shard_map.80 = (bf16[32,5,8,3584]{3,2,1,0:T(8,128)(2,1)}, f32[8,128]{1,0:T(8,128)}) custom-call(s32[3]{0:T(128)} %pad_add_fusion.refs_0_, bf16[256,1024]{1,0:T(8,128)(2,1)} %get-tuple-element.55.refs_1_, bf16[256,1024]{1,0:T(8,128)(2,1)} %get-tuple-element.56.refs_2_, bf16[256,3584]{1,0:T(8,128)(2,1)} %refs_3_.2, ...), custom_call_target="tpu_custom_call" | custom-call | flops 100000000 | tf_op jit(solution)/shard_map/pallas_call | solution.py:46
  90.4 2.7 %all-to-all-done.1 = bf16[16,40,3584]{2,1,0:T(8,128)(2,1)} async-done(((bf16[16,40,3584]{2,1,0:T(8,128)(2,1)}), bf16[16,40,3584]{2,1,0:T(8,128)(2,1)}, u32[]{:S(2)}, u32[]{:S(2)}) %all-to-all-start.1) | async-done | bytes 4587552 | tf_op jit(solution)/shard_map/all_to_all | solution.py:471
  93.1 6.5 %all-to-all-start = ((bf16[32,5,8,3584]{3,2,1,0:T(8,128)(2,1)}), bf16[32,5,8,3584]{3,2,1,0:T(8,128)(2,1)}, u32[]{:S(2)}, u32[]{:S(2)}) async-start(bf16[32,5,8,3584]{3,2,1,0:T(8,128)(2,1)} %get-tuple-element.60), calls=%async_computation | async-start | bytes 18350080 | tf_op jit(solution)/shard_map/all_to_all | solution.py:485
  99.6 5.0 %shard_map.81 = (bf16[320,3584]{1,0:T(8,128)(2,1)}, f32[8,128]{1,0:T(8,128)}) custom-call(s32[3]{0:T(128)} %pad_add_fusion.refs_0_, bf16[640,3584]{1,0:T(8,128)(2,1)} %bitcast.7.refs_1_, f32[8,128]{1,0:T(8,128)} %get-tuple-element.63.refs_2_), custom_call_target="tpu_custom_call" | custom-call | flops 100000000 | tf_op jit(solution)/shard_map/pallas_call | solution.py:46
  107.9 5.5 %shard_map.82 = (bf16[320,3584]{1,0:T(8,128)(2,1)S(1)}, bf16[320,2688]{1,0:T(8,128)(2,1)}, bf16[320,896]{1,0:T(8,128)(2,1)}, f32[8,128]{1,0:T(8,128)S(1)}) custom-call(s32[3]{0:T(128)S(1)} %copy-done.13, bf16[640,3584]{1,0:T(8,128)(2,1)} %bitcast.7.refs_1_, f32[8,128]{1,0:T(8,128)S(1)} %copy-done.15), custom_call_target="tpu_custom_call" | custom-call | flops 100000000 | tf_op jit(solution)/shard_map/pallas_call | solution.py:46
  114.8 42.4 %collective-permute-done.10.refs_3_.refs_1_.refs_2_ = bf16[320,3584]{1,0:T(8,128)(2,1)S(1)} collective-permute-done((bf16[320,3584]{1,0:T(8,128)(2,1)}, bf16[320,3584]{1,0:T(8,128)(2,1)S(1)}, u32[]{:S(2)}, u32[]{:S(2)}) %collective-permute-start.10) | collective-permute-done | bytes 2293792 | tf_op jit(solution)/shard_map/ppermute | solution.py:24
  164.4 6.5 %shard_map.84 = (bf16[960,512]{1,0:T(8,128)(2,1)S(1)}, f32[1,960]{1,0:T(1,128)S(1)}, f32[8,128]{1,0:T(8,128)S(1)}) custom-call(bf16[320,3584]{1,0:T(8,128)(2,1)S(1)} %copy-done.3, bf16[320,3584]{1,0:T(8,128)(2,1)S(1)} %collective-permute-done.10.refs_3_.refs_1_.refs_2_, bf16[320,3584]{1,0:T(8,128)(2,1)} %copy-done, bf16[2,512,3584]{2,1,0:T(8,128)(2,1)} %refs_1_.7, ...), custom_call_target="tpu_custom_call" | custom-call | flops 100000000 | tf_op jit(solution)/shard_map/pallas_call | solution.py:46
  175.9 6.5 %shard_map.85 = (f32[512,3584]{1,0:T(8,128)}, f32[8,128]{1,0:T(8,128)S(1)}) custom-call(bf16[512,960]{1,0:T(8,128)(2,1)S(1)} %copy-done.8, bf16[320,3584]{1,0:T(8,128)(2,1)S(1)} %copy-done.4, bf16[320,3584]{1,0:T(8,128)(2,1)S(1)} %collective-permute-done.10.refs_3_.refs_1_.refs_2_, bf16[320,3584]{1,0:T(8,128)(2,1)S(1)} %copy-done.1, ...), custom_call_target="tpu_custom_call" | custom-call | flops 100000000 | tf_op jit(solution)/shard_map/pallas_call | solution.py:46
  182.4 16.0 %collective-permute-done.13.refs_0_ = bf16[320,2688]{1,0:T(8,128)(2,1)} collective-permute-done((bf16[320,2688]{1,0:T(8,128)(2,1)}, bf16[320,2688]{1,0:T(8,128)(2,1)}, u32[]{:S(2)}, u32[]{:S(2)}) %collective-permute-start.13) | collective-permute-done | bytes 1720352 | tf_op jit(solution)/shard_map/ppermute | solution.py:24
  198.4 7.3 %shard_map.86 = (bf16[2,512,3584]{2,1,0:T(8,128)(2,1)}, f32[320,512]{1,0:T(8,128)S(1)}, f32[8,128]{1,0:T(8,128)S(1)}) custom-call(bf16[320,2688]{1,0:T(8,128)(2,1)} %collective-permute-done.13.refs_0_, bf16[2,512,3584]{2,1,0:T(8,128)(2,1)} %refs_1_.7, bf16[512,320]{1,0:T(8,128)(2,1)S(1)} %copy-done.5, f32[512,3584]{1,0:T(8,128)} %get-tuple-element.76.refs_3_, ...), custom_call_target="tpu_custom_call" | custom-call | flops 100000000 | tf_op jit(solution)/shard_map/pallas_call | solution.py:46
  205.8 4.9 %collective-permute-done.12.refs_0_ = bf16[320,896]{1,0:T(8,128)(2,1)} collective-permute-done((bf16[320,896]{1,0:T(8,128)(2,1)}, bf16[320,896]{1,0:T(8,128)(2,1)}, u32[]{:S(2)}, u32[]{:S(2)}) %collective-permute-start.12) | collective-permute-done | bytes 573472 | tf_op jit(solution)/shard_map/ppermute | solution.py:24
  210.7 3.6 %shard_map.87 = (bf16[2,512,3584]{2,1,0:T(8,128)(2,1)}, bf16[320,512]{1,0:T(8,128)(2,1)S(1)}, f32[1,320]{1,0:T(1,128)S(1)}, f32[8,128]{1,0:T(8,128)S(1)}) custom-call(bf16[320,896]{1,0:T(8,128)(2,1)} %collective-permute-done.12.refs_0_, bf16[2,512,3584]{2,1,0:T(8,128)(2,1)} %refs_1_.7, ...), custom_call_target="tpu_custom_call", output_to_operand_aliasing={{0}: (6, {})} | custom-call | flops 100000000 | tf_op jit(solution)/shard_map/pallas_call | solution.py:46
  215.6 8.7 %shard_map.88 = (bf16[1280,512]{1,0:T(8,128)(2,1)S(1)}, f32[1,1280]{1,0:T(1,128)S(1)}, f32[8,128]{1,0:T(8,128)S(1)}) custom-call(bf16[1280,3584]{1,0:T(8,128)(2,1)} %bitcast.5.refs_0_.refs_2_, bf16[2,512,3584]{2,1,0:T(8,128)(2,1)} %refs_1_.7, bf16[1280,512]{1,0:T(8,128)(2,1)S(1)} %copy-done.6, f32[8,128]{1,0:T(8,128)S(1)} %get-tuple-element.83.refs_3_), custom_call_target="tpu_custom_call" | custom-call | flops 100000000 | tf_op jit(solution)/shard_map/pallas_call | solution.py:46
  227.0 10.4 %all-to-all-start.2 = ((f32[128,1,20]{2,1,0:T(1,128)}), f32[128,1,20]{2,1,0:T(1,128)S(1)}, u32[]{:S(2)}, u32[]{:S(2)}) async-start(f32[128,1,20]{2,1,0:T(1,128)} %bitcast.10), calls=%async_computation.2 | async-start | bytes 131072 | tf_op jit(solution)/shard_map/all_to_all | solution.py:516
  237.5 11.9 %shard_map.89 = (bf16[2,512,3584]{2,1,0:T(8,128)(2,1)}, bf16[2,1280,512]{2,1,0:T(8,128)(2,1)}, f32[8,128]{1,0:T(8,128)}) custom-call(s32[3]{0:T(128)} %pad_add_fusion.refs_0_, bf16[512,1280]{1,0:T(8,128)(2,1)} %get-tuple-element.87.refs_1_, bf16[1280,3584]{1,0:T(8,128)(2,1)} %bitcast.5.refs_0_.refs_2_, ...), custom_call_target="tpu_custom_call", output_to_operand_aliasing={{0}: (6, {})} | custom-call | flops 100000000 | tf_op jit(solution)/shard_map/pallas_call | solution.py:46
  (103 shorter events, 34.9 us)
Async XLA Ops:
  0.6 7.2 %collective-permute-start.2 = (bf16[256,3584]{1,0:T(8,128)(2,1)}, bf16[256,3584]{1,0:T(8,128)(2,1)S(1)}, u32[]{:S(2)}, u32[]{:S(2)}) collective-permute-start(bf16[256,3584]{1,0:T(8,128)(2,1)} %refs_3_.2), channel_id=1, source_target_pairs={{0,1},{1,0},{2,3},{3,2},{4,5},{5,4},{6,7},{7,6},{8,9},{9,8},{10,11... | collective-permute-start | bytes 5505032 | tf_op jit(solution)/shard_map/ppermute | solution.py:28
  2.1 44.5 %collective-permute-start.3 = (bf16[256,3584]{1,0:T(8,128)(2,1)}, bf16[256,3584]{1,0:T(8,128)(2,1)}, u32[]{:S(2)}, u32[]{:S(2)}) collective-permute-start(bf16[256,3584]{1,0:T(8,128)(2,1)} %refs_3_.2), channel_id=1, source_target_pairs={{0,32},{32,64},{64,96},{96,0},{1,33},{33,65},{65,97},{97,1},{2,34}... | collective-permute-start | bytes 5505032 | tf_op jit(solution)/shard_map/ppermute | solution.py:24
  3.9 42.7 %collective-permute-start.4 = (bf16[256,3584]{1,0:T(8,128)(2,1)}, bf16[256,3584]{1,0:T(8,128)(2,1)}, u32[]{:S(2)}, u32[]{:S(2)}) collective-permute-start(bf16[256,3584]{1,0:T(8,128)(2,1)} %refs_3_.2), channel_id=1, source_target_pairs={{0,96},{32,0},{64,32},{96,64},{1,97},{33,1},{65,33},{97,65},{2,98}... | collective-permute-start | bytes 5505032 | tf_op jit(solution)/shard_map/ppermute | solution.py:24
  6.0 1.8 collective-permute-start
  6.4 1.4 collective-permute-start.1
  17.4 75.6 %all-to-all-start.1 = ((bf16[16,40,3584]{2,1,0:T(8,128)(2,1)}), bf16[16,40,3584]{2,1,0:T(8,128)(2,1)}, u32[]{:S(2)}, u32[]{:S(2)}) async-start(bf16[16,40,3584]{2,1,0:T(8,128)(2,1)} %bitcast.28), calls=%async_computation.1 | async-start | bytes 9175040 | tf_op jit(solution)/shard_map/all_to_all | solution.py:471
  49.6 29.0 %collective-permute-start.8 = (bf16[256,1792]{1,0:T(8,128)(2,1)}, bf16[256,1792]{1,0:T(8,128)(2,1)S(1)}, u32[]{:S(2)}, u32[]{:S(2)}) collective-permute-start(bf16[256,1792]{1,0:T(8,128)(2,1)} %get-tuple-element.57), channel_id=1, source_target_pairs={{0,32},{32,64},{64,96},{96,0},{1,33},{33,65},{65,97},{97,1},{2,34}... | collective-permute-start | bytes 2752520 | tf_op jit(solution)/shard_map/ppermute | solution.py:24
  50.1 28.6 %collective-permute-start.9 = (bf16[256,1792]{1,0:T(8,128)(2,1)}, bf16[256,1792]{1,0:T(8,128)(2,1)S(1)}, u32[]{:S(2)}, u32[]{:S(2)}) collective-permute-start(bf16[256,1792]{1,0:T(8,128)(2,1)} %get-tuple-element.58), channel_id=1, source_target_pairs={{0,96},{32,0},{64,32},{96,64},{1,97},{33,1},{65,33},{97,65},{2,98}... | collective-permute-start | bytes 2752520 | tf_op jit(solution)/shard_map/ppermute | solution.py:24
  52.3 20.2 %collective-permute-start.5 = (f32[8,256]{1,0:T(8,128)}, f32[8,256]{1,0:T(8,128)S(1)}, u32[]{:S(2)}, u32[]{:S(2)}) collective-permute-start(f32[8,256]{1,0:T(8,128)} %get-tuple-element.52.refs_1_), channel_id=1, source_target_pairs={{0,32},{32,64},{64,96},{96,0},{1,33},{33,65},{65,97},{97,1},{2,34}... | collective-permute-start | bytes 24584 | tf_op jit(solution)/shard_map/ppermute | solution.py:24
  52.3 21.0 %collective-permute-start.6 = (f32[8,256]{1,0:T(8,128)}, f32[8,256]{1,0:T(8,128)S(1)}, u32[]{:S(2)}, u32[]{:S(2)}) collective-permute-start(f32[8,256]{1,0:T(8,128)} %get-tuple-element.52.refs_1_), channel_id=1, source_target_pairs={{0,64},{32,96},{64,0},{96,32},{1,65},{33,97},{65,1},{97,33},{2,66}... | collective-permute-start | bytes 24584 | tf_op jit(solution)/shard_map/ppermute | solution.py:24
  54.6 18.6 %collective-permute-start.7 = (f32[8,256]{1,0:T(8,128)}, f32[8,256]{1,0:T(8,128)S(1)}, u32[]{:S(2)}, u32[]{:S(2)}) collective-permute-start(f32[8,256]{1,0:T(8,128)} %get-tuple-element.52.refs_1_), channel_id=1, source_target_pairs={{0,96},{32,0},{64,32},{96,64},{1,97},{33,1},{65,33},{97,65},{2,98}... | collective-permute-start | bytes 24584 | tf_op jit(solution)/shard_map/ppermute | solution.py:24
  93.1 122.5 %all-to-all-start = ((bf16[32,5,8,3584]{3,2,1,0:T(8,128)(2,1)}), bf16[32,5,8,3584]{3,2,1,0:T(8,128)(2,1)}, u32[]{:S(2)}, u32[]{:S(2)}) async-start(bf16[32,5,8,3584]{3,2,1,0:T(8,128)(2,1)} %get-tuple-element.60), calls=%async_computation | async-start | bytes 18350080 | tf_op jit(solution)/shard_map/all_to_all | solution.py:485
  99.6 7.7 %copy-start.13 = (s32[3]{0:T(128)S(1)}, s32[3]{0:T(128)}, u32[]{:S(2)}) copy-start(s32[3]{0:T(128)} %pad_add_fusion.refs_0_) | copy-start | bytes 40
  104.5 52.7 %collective-permute-start.10 = (bf16[320,3584]{1,0:T(8,128)(2,1)}, bf16[320,3584]{1,0:T(8,128)(2,1)S(1)}, u32[]{:S(2)}, u32[]{:S(2)}) collective-permute-start(bf16[320,3584]{1,0:T(8,128)(2,1)} %get-tuple-element.68), channel_id=1, source_target_pairs={{0,32},{32,64},{64,96},{96,0},{1,33},{33,65},{65,97},{97,1},{2,34}... | collective-permute-start | bytes 6881288 | tf_op jit(solution)/shard_map/ppermute | solution.py:24
  105.1 52.2 %collective-permute-start.11 = (bf16[320,3584]{1,0:T(8,128)(2,1)}, bf16[320,3584]{1,0:T(8,128)(2,1)S(1)}, u32[]{:S(2)}, u32[]{:S(2)}) collective-permute-start(bf16[320,3584]{1,0:T(8,128)(2,1)} %get-tuple-element.68), channel_id=1, source_target_pairs={{0,96},{32,0},{64,32},{96,64},{1,97},{33,1},{65,33},{97,65},{2,98}... | collective-permute-start | bytes 6881288 | tf_op jit(solution)/shard_map/ppermute | solution.py:24
  158.6 39.8 %collective-permute-start.13 = (bf16[320,2688]{1,0:T(8,128)(2,1)}, bf16[320,2688]{1,0:T(8,128)(2,1)}, u32[]{:S(2)}, u32[]{:S(2)}) collective-permute-start(bf16[320,2688]{1,0:T(8,128)(2,1)} %get-tuple-element.77), channel_id=1, source_target_pairs={{0,64},{32,96},{64,0},{96,32},{1,65},{33,97},{65,1},{97,33},{2,66}... | collective-permute-start | bytes 5160968 | tf_op jit(solution)/shard_map/ppermute | solution.py:24
  159.9 50.8 %collective-permute-start.12 = (bf16[320,896]{1,0:T(8,128)(2,1)}, bf16[320,896]{1,0:T(8,128)(2,1)}, u32[]{:S(2)}, u32[]{:S(2)}) collective-permute-start(bf16[320,896]{1,0:T(8,128)(2,1)} %get-tuple-element.69), channel_id=1, source_target_pairs={{0,64},{32,96},{64,0},{96,32},{1,65},{33,97},{65,1},{97,33},{2,66}... | collective-permute-start | bytes 1720328 | tf_op jit(solution)/shard_map/ppermute | solution.py:24
  164.4 8.1 %copy-start.8 = (bf16[512,960]{1,0:T(8,128)(2,1)S(1)}, bf16[512,960]{1,0:T(8,128)(2,1)}, u32[]{:S(2)}) copy-start(bf16[512,960]{1,0:T(8,128)(2,1)} %get-tuple-element.71.refs_0_) | copy-start | bytes 2949124
  175.9 22.6 %copy-start.5 = (bf16[512,320]{1,0:T(8,128)(2,1)S(1)}, bf16[512,320]{1,0:T(8,128)(2,1)}, u32[]{:S(2)}) copy-start(bf16[512,320]{1,0:T(8,128)(2,1)} %get-tuple-element.70.refs_2_) | copy-start | bytes 983044
  198.4 12.3 %copy-start.11 = (bf16[320,512]{1,0:T(8,128)(2,1)S(1)}, bf16[320,512]{1,0:T(8,128)(2,1)}, u32[]{:S(2)}) copy-start(bf16[320,512]{1,0:T(8,128)(2,1)} %get-tuple-element.80.refs_5_) | copy-start | bytes 983044
  210.7 4.8 %copy-start.6 = (bf16[1280,512]{1,0:T(8,128)(2,1)S(1)}, bf16[1280,512]{1,0:T(8,128)(2,1)}, u32[]{:S(2)}) copy-start(bf16[1280,512]{1,0:T(8,128)(2,1)} %get-tuple-element.61.refs_2_) | copy-start | bytes 3932164
  215.6 21.9 %copy-start.21 = (s32[4,256]{1,0:T(4,128)S(1)}, s32[4,256]{1,0:T(4,128)}, u32[]{:S(2)}) copy-start(s32[4,256]{1,0:T(4,128)} %get-tuple-element.49) | copy-start | bytes 12292
  227.0 22.4 %all-to-all-start.2 = ((f32[128,1,20]{2,1,0:T(1,128)}), f32[128,1,20]{2,1,0:T(1,128)S(1)}, u32[]{:S(2)}, u32[]{:S(2)}) async-start(f32[128,1,20]{2,1,0:T(1,128)} %bitcast.10), calls=%async_computation.2 | async-start | bytes 131072 | tf_op jit(solution)/shard_map/all_to_all | solution.py:516
  237.4 12.7 %copy-start.19 = (bf16[256,4]{0,1:T(4,128)(2,1)S(1)}, bf16[256,4]{0,1:T(4,128)(2,1)}, u32[]{:S(2)}) copy-start(bf16[256,4]{0,1:T(4,128)(2,1)} %param.6) | copy-start | bytes 6148
  (19 other events, 19.5 us)
